TPU v7x, 32 devices: a whole 2x2x4 slice. The times are simulated.
32 devices in a mesh: tiles: 8 (over y, x, core), cols: 4 (over z).
Axes of the slice: x: 2, y: 2, z: 4, core: 2. Of those that a mesh axis runs over, the one named last changes fastest.
Arguments:
- front_diag: float32 [4096, 4096], P('tiles', 'cols'), as said below
- front_below: float32 [4096, 4096], P('tiles', 'cols'), may hold values from -2 to 2
- ancestor: float32 [4096, 4096], P('tiles', 'cols'), may hold values from -6 to 6
- owner_cols: int32 [4], replicated, may hold values from 0 to 3, each once
- rel: int32 [4096], replicated, may hold values from 0 to 4095, as said below
Outputs:
- factor_diag: float32 [4096, 4096], P('tiles', 'cols')
- factor_below: float32 [4096, 4096], P('tiles', 'cols')
- ancestor_out: float32 [4096, 4096], P('tiles', 'cols')
Inputs may be any that keep to these rules, and one draw needn't show every extreme that they name: Within each aligned block of 512 entries, rel is a permutation of that block's own indices. `owner_cols`: each column tile appears exactly once. `front_diag`: the symmetric block defined by the lower triangle is positive definite.
All inputs are finite; a program needn't handle non-finite values.
Results may differ from a plain program's by a relative error of at most 0.000073.
Values sent between devices are 32-bit elements; how exact they have to be, the bound alone decides.
No kernel may reach another device: no remote copies, remote signals or barrier semaphores. Data moves between devices by JAX's collectives and lax.ppermute only.
A program may use at most 128 MiB of HBM per device.

v0:
```python
import jax
import jax.numpy as jnp
from jax import lax
from jax.sharding import PartitionSpec as P

PANELS = 2


def broadcast(block, axis, holder):
    block = jnp.where(lax.axis_index(axis) == holder, block, jnp.zeros_like(block))
    return lax.psum(block, axis)


def product_nt(left_side, right_side):
    return lax.dot_general(
        left_side,
        right_side,
        (((1,), (1,)), ((), ())),
        precision=lax.Precision.HIGHEST,
        preferred_element_type=jnp.float32,
    )


def product_nn(left_side, right_side):
    return jnp.dot(
        left_side, right_side, precision=lax.Precision.HIGHEST, preferred_element_type=jnp.float32
    )


def factor_tile(diag_block):
    symmetric = jnp.tril(diag_block) + jnp.tril(diag_block, -1).T
    factor = jnp.linalg.cholesky(symmetric)
    identity = jnp.eye(factor.shape[0], dtype=jnp.float32)
    inverse_factor = jax.scipy.linalg.solve_triangular(factor, identity, lower=True)
    return (factor, inverse_factor)


def solve_rows(inverse_factor, piece_rows):
    return product_nt(piece_rows, inverse_factor)


def masked_rows(factor, inverse_factor, piece_rows, tile_index, step_index, offset):
    own_rows = lax.dynamic_slice_in_dim(factor, offset, piece_rows.shape[0], 0)
    solved = solve_rows(inverse_factor, piece_rows)
    later = jnp.where(tile_index > step_index, solved, jnp.zeros_like(solved))
    return jnp.where(tile_index == step_index, own_rows, later)


def shards(front_diag, front_below, ancestor, owner_cols, rel):
    row_count, tile_width = front_diag.shape
    tile_pos = lax.axis_index("tiles")
    col_pos = lax.axis_index("cols")
    row_tile = tile_pos // 2
    half_offset = tile_pos % 2 * row_count
    target_tile = lax.dynamic_slice_in_dim(owner_cols, col_pos, 1)[0]
    identity = jnp.eye(tile_width, dtype=jnp.float32)

    def one_step(step_index, carry):
        upper_part, lower_part, schur_sum = carry
        halves = [
            broadcast(upper_part, "tiles", 2 * step_index + half_number) for half_number in range(2)
        ]
        diag_block = jnp.where(col_pos == step_index, jnp.concatenate(halves, 0), identity)
        factor, inverse_factor = factor_tile(diag_block)
        own_diag = masked_rows(
            factor, inverse_factor, upper_part, row_tile, step_index, half_offset
        )
        own_below = solve_rows(inverse_factor, lower_part)
        column = broadcast(jnp.stack((own_diag, own_below)), "cols", step_index)
        diag_factor = column[0]
        below_factor = column[1]
        match_rows = jnp.concatenate(
            [
                broadcast(diag_factor, "tiles", 2 * col_pos + half_number)
                for half_number in range(2)
            ],
            0,
        )
        target_rows = jnp.concatenate(
            [
                broadcast(below_factor, "tiles", 2 * target_tile + half_number)
                for half_number in range(2)
            ],
            0,
        )
        here = col_pos == step_index
        later = col_pos > step_index
        new_upper = jnp.where(
            here,
            diag_factor,
            jnp.where(later, upper_part - product_nt(diag_factor, match_rows), upper_part),
        )
        new_lower = jnp.where(
            here,
            below_factor,
            jnp.where(later, lower_part - product_nt(below_factor, match_rows), lower_part),
        )
        new_schur = schur_sum + product_nt(below_factor, target_rows)
        return (new_upper, new_lower, new_schur)

    start = (front_diag, front_below, jnp.zeros((row_count, tile_width), jnp.float32))
    upper_done, factor_below, schur_sum = lax.fori_loop(0, PANELS, one_step, start)
    global_rows = tile_pos * row_count + jnp.arange(row_count, dtype=jnp.int32)
    global_cols = col_pos * tile_width + jnp.arange(tile_width, dtype=jnp.int32)
    lower_mask = global_rows[:, None] >= global_cols[None, :]
    factor_diag = jnp.where(lower_mask, upper_done, jnp.zeros_like(upper_done))
    row_places = (
        lax.dynamic_slice_in_dim(rel, tile_pos * row_count, row_count) - tile_pos * row_count
    )
    column_places = (
        lax.dynamic_slice_in_dim(rel, target_tile * tile_width, tile_width)
        - target_tile * tile_width
    )
    row_move = (row_places[None, :] == jnp.arange(row_count, dtype=jnp.int32)[:, None]).astype(
        jnp.float32
    )
    column_move = (
        column_places[None, :] == jnp.arange(tile_width, dtype=jnp.int32)[:, None]
    ).astype(jnp.float32)
    placed = product_nt(product_nn(row_move, schur_sum), column_move)
    return (factor_diag, factor_below, ancestor - placed)


def solution(mesh):
    placed = (P("tiles", "cols"), P("tiles", "cols"), P("tiles", "cols"), P(), P())
    return jax.shard_map(
        shards,
        mesh=mesh,
        in_specs=placed,
        out_specs=(P("tiles", "cols"), P("tiles", "cols"), P("tiles", "cols")),
        check_vma=False,
    )
```

profile of v0, /device:TPU:31, one launch (start us, length us, event | category | flops | bytes accessed | tf_op | source)
XLA Modules:
  0.0 1605.7 jit_solution(8462156365010440306)
XLA Ops:
  11.5 1571.8 %while.24 = (s32[]{:T(128)}, f32[512,1024]{1,0:T(8,128)S(1)}, f32[512,1024]{1,0:T(8,128)}, f32[512,1024]{1,0:T(8,128)}, s32[]{:T(128)}, /*index=5*/s32[]{:T(128)...) while((s32[]{:T(128)}, f32[512,1024]{1,0:T(8,128)S(1)}, ...), condition=%wide.region_24.25_spmd.clone, body=%wide.region_0.24_spmd.clone.sunk | while | flops 42322001920 | bytes 459031616 | solution.py:102
  18.2 79.6 %all-reduce.11.cloned.1.call-done = (f32[512,1024]{1,0:T(8,128)}, f32[512,1024]{1,0:T(8,128)}) async-done(((f32[512,1024]{1,0:T(8,128)}, f32[512,1024]{1,0:T(8,128)}), (f32[512,1024]{1,0:T(8,128)}, f32[512,1024]{1,0:T(8,128)})) %all-reduce.11.cloned.1.call-update) | async-done | bytes 4194320 | tf_op jit(solution)/shard_map/while/body/eval_jaxpr/psum | solution.py:11
  126.6 11.7 cholesky.1057
  140.8 9.8 custom-call.192
  154.6 11.9 cholesky.1060
  167.1 9.8 custom-call.193
  180.3 11.7 cholesky.1062
  193.4 9.8 custom-call.194
  206.7 11.9 cholesky.1064
  220.0 9.8 custom-call.195
  233.2 11.7 cholesky.1066
  246.3 10.2 custom-call.196
  259.8 11.7 cholesky.1068
  272.8 9.8 custom-call.197
  285.6 11.9 cholesky.1070
  298.7 9.8 custom-call.198
  311.2 11.7 cholesky.1071
  336.6 24.1 %while.25 = (s32[]{:T(128)}, f32[1024,1024]{1,0:T(8,128)}, s32[8,2]{0,1:T(2,128)S(1)}, f32[8,128,128]{2,1,0:T(8,128)S(1)}, s32[]{:T(128)}) while((s32[]{:T(128)}, f32[1024,1024]{1,0:T(8,128)}, s32[8,2]{0,1:T(2,128)S(1)}, f32[8,128,128]{2,1,0:T(8,128)S(1)}, s32[]{:T(128)}) %tuple.146), condition=%wide.while_cond, body=%wide.while_body.sunk | while | flops 2 | bytes 131181 | solution.py:34
  360.7 78.8 %custom-call.200 = f32[8,128,128]{1,2,0:T(8,128)S(1)} custom-call(f32[8,128,128]{2,1,0:T(8,128)S(1)} %get-tuple-element.589), custom_call_target="InvertDiagBlocksLowerTriangular" | custom-call | tf_op jit(solution)/shard_map/while/body/eval_jaxpr/jit(_solve_triangular)/triangular_solve | solution.py:34
  479.4 154.1 %all-reduce.13.cloned.1.call-done = f32[2,512,1024]{2,1,0:T(8,128)} async-done(((f32[2,512,1024]{2,1,0:T(8,128)}), f32[2,512,1024]{2,1,0:T(8,128)}) %all-reduce.13.cloned.1.call-update) | async-done | bytes 4194320 | tf_op jit(solution)/shard_map/while/body/eval_jaxpr/psum | solution.py:11
  639.9 127.2 %all-reduce.15.cloned.1.call-done = (f32[512,1024]{1,0:T(8,128)}, f32[512,1024]{1,0:T(8,128)}, f32[512,1024]{1,0:T(8,128)}, f32[512,1024]{1,0:T(8,128)}) async-done(((f32[512,1024]{1,0:T(8,128)}, f32[512,1024]{1,0:T(8,128)}, f32[512,1024]{1,0:T(8,128)}, f32[512,1024]{1,0:T(8,128)}), (f32[512,1024]{1,0:T(8,128)}, f32[512,1024]{1,0:T(8,128)}, f32[512,1024]{1,0:T(8,128)}, ...) | async-done | bytes 8388624 | tf_op jit(solution)/shard_map/while/body/eval_jaxpr/psum | solution.py:11
  771.2 7.5 fusion.242
  778.7 7.7 fusion.241
  786.5 7.7 select_add_fusion.2
  802.5 79.8 %all-reduce.11.cloned.1.call-done = (f32[512,1024]{1,0:T(8,128)}, f32[512,1024]{1,0:T(8,128)}) async-done(((f32[512,1024]{1,0:T(8,128)}, f32[512,1024]{1,0:T(8,128)}), (f32[512,1024]{1,0:T(8,128)}, f32[512,1024]{1,0:T(8,128)})) %all-reduce.11.cloned.1.call-update) | async-done | bytes 4194320 | tf_op jit(solution)/shard_map/while/body/eval_jaxpr/psum | solution.py:11
  910.6 11.7 cholesky.1057
  924.9 9.8 custom-call.192
  938.6 11.9 cholesky.1060
  951.2 9.8 custom-call.193
  964.4 11.7 cholesky.1062
  977.4 9.8 custom-call.194
  990.8 12.1 cholesky.1064
  1004.2 9.8 custom-call.195
  1017.5 11.7 cholesky.1066
  1030.5 9.9 custom-call.196
  1043.8 11.7 cholesky.1068
  1056.8 9.8 custom-call.197
  1069.6 11.9 cholesky.1070
  1082.8 9.8 custom-call.198
  1095.2 11.7 cholesky.1071
  1120.7 24.1 %while.25 = (s32[]{:T(128)}, f32[1024,1024]{1,0:T(8,128)}, s32[8,2]{0,1:T(2,128)S(1)}, f32[8,128,128]{2,1,0:T(8,128)S(1)}, s32[]{:T(128)}) while((s32[]{:T(128)}, f32[1024,1024]{1,0:T(8,128)}, s32[8,2]{0,1:T(2,128)S(1)}, f32[8,128,128]{2,1,0:T(8,128)S(1)}, s32[]{:T(128)}) %tuple.146), condition=%wide.while_cond, body=%wide.while_body.sunk | while | flops 2 | bytes 131181 | solution.py:34
  1144.8 79.0 %custom-call.200 = f32[8,128,128]{1,2,0:T(8,128)S(1)} custom-call(f32[8,128,128]{2,1,0:T(8,128)S(1)} %get-tuple-element.589), custom_call_target="InvertDiagBlocksLowerTriangular" | custom-call | tf_op jit(solution)/shard_map/while/body/eval_jaxpr/jit(_solve_triangular)/triangular_solve | solution.py:34
  1253.7 7.3 fusion.239
  1263.6 154.1 %all-reduce.13.cloned.1.call-done = f32[2,512,1024]{2,1,0:T(8,128)} async-done(((f32[2,512,1024]{2,1,0:T(8,128)}), f32[2,512,1024]{2,1,0:T(8,128)}) %all-reduce.13.cloned.1.call-update) | async-done | bytes 4194320 | tf_op jit(solution)/shard_map/while/body/eval_jaxpr/psum | solution.py:11
  1424.1 127.2 %all-reduce.15.cloned.1.call-done = (f32[512,1024]{1,0:T(8,128)}, f32[512,1024]{1,0:T(8,128)}, f32[512,1024]{1,0:T(8,128)}, f32[512,1024]{1,0:T(8,128)}) async-done(((f32[512,1024]{1,0:T(8,128)}, f32[512,1024]{1,0:T(8,128)}, f32[512,1024]{1,0:T(8,128)}, f32[512,1024]{1,0:T(8,128)}), (f32[512,1024]{1,0:T(8,128)}, f32[512,1024]{1,0:T(8,128)}, f32[512,1024]{1,0:T(8,128)}, ...) | async-done | bytes 8388624 | tf_op jit(solution)/shard_map/while/body/eval_jaxpr/psum | solution.py:11
  1555.4 7.5 fusion.242
  1562.9 7.7 fusion.241
  1570.7 7.7 select_add_fusion.2
  (264 shorter events, 314.7 us)
Async XLA Ops:
  7.2 4.3 copy-start.1
  7.2 1.7 copy-start.13
  7.2 3.1 copy-start.14
  11.7 86.1 %all-reduce.11.cloned.1.call-start = ((), (), s32[]{:S(2)}) async-start(), calls=%async_computation | async-start | bytes 8388608 | tf_op jit(solution)/shard_map/while/body/eval_jaxpr/psum | solution.py:11
  14.4 619.1 %all-reduce.13.cloned.1.call-start = ((), (), s32[]{:S(2)}) async-start(), calls=%async_computation.1 | async-start | bytes 8388608 | tf_op jit(solution)/shard_map/while/body/eval_jaxpr/psum | solution.py:11
  124.6 2.0 copy-start.3
  439.5 3.9 copy-start.2
  457.8 5.1 copy-start.4
  462.8 6.9 copy-start.7
  479.4 287.8 %all-reduce.15.cloned.1.call-start = ((), (), s32[]{:S(2)}) async-start(), calls=%async_computation.2 | async-start | bytes 16777216 | tf_op jit(solution)/shard_map/while/body/eval_jaxpr/psum | solution.py:11
  767.1 2.2 copy-start.10
  767.1 3.5 copy-start
  767.1 4.1 copy-start.5
  778.7 7.8 copy-start.6
  778.7 7.8 copy-start.8
  778.7 7.8 copy-start.11
  778.7 7.8 copy-start.12
  794.3 1.3 copy-start.9
  796.0 86.3 %all-reduce.11.cloned.1.call-start = ((), (), s32[]{:S(2)}) async-start(), calls=%async_computation | async-start | bytes 8388608 | tf_op jit(solution)/shard_map/while/body/eval_jaxpr/psum | solution.py:11
  798.6 619.1 %all-reduce.13.cloned.1.call-start = ((), (), s32[]{:S(2)}) async-start(), calls=%async_computation.1 | async-start | bytes 8388608 | tf_op jit(solution)/shard_map/while/body/eval_jaxpr/psum | solution.py:11
  908.7 2.0 copy-start.3
  1223.8 3.9 copy-start.2
  1242.0 4.8 copy-start.4
  1246.8 6.9 copy-start.7
  1263.5 287.8 %all-reduce.15.cloned.1.call-start = ((), (), s32[]{:S(2)}) async-start(), calls=%async_computation.2 | async-start | bytes 16777216 | tf_op jit(solution)/shard_map/while/body/eval_jaxpr/psum | solution.py:11
  1551.3 2.2 copy-start.10
  1551.3 3.5 copy-start
  1551.3 4.1 copy-start.5
  1562.9 7.8 copy-start.6
  1562.9 7.8 copy-start.8
  1562.9 7.7 copy-start.11
  1562.9 7.7 copy-start.12
  1578.4 1.3 copy-start.9
Sparse Core Ops, SparseCore 0:
  16.5 81.3 all-reduce.10
  479.5 154.0 all-reduce.12
  640.0 127.0 all-reduce.14
  800.4 81.8 all-reduce.10
  1263.7 154.0 all-reduce.12
  1424.2 127.0 all-reduce.14
where the time goes:
time: 1610 us
  waiting for transfers between devices  722 us (45%)
  other arithmetic  580 us (36%)
  matrix products  178 us (11%)
  local copies, waits for them, and re-layouts  93.4 us (6%)
    psum x6, waiting for transfers between devices, broadcast(): return lax.psum(block, axis)  722 us
    another operation x60, other arithmetic, factor_tile(): factor = jnp.linalg.cholesky(symmetric)  345 us
    another operation x6, other arithmetic, factor_tile(): jax.scipy.linalg.solve_triangular(factor, identity, lower=True)  171 us
    dot_general x11, matrix products, product_nt(): lax.dot_general(left_side, right_side, (((1,), (1,)), ((), ())), precisio...  81 us
    another operation x48, local copies, waits for them, and re-layouts  47.9 us
    another operation x28, matrix products, factor_tile(): factor = jnp.linalg.cholesky(symmetric)  46.1 us
    another operation x30, matrix products, factor_tile(): jax.scipy.linalg.solve_triangular(factor, identity, lower=True)  45.9 us
  transfers between devices with their start and end apart: 6, of which 6 were waited for; matrix products, arithmetic and copies ran while one was open for 0% of the time, Pallas kernels for 0%

commit v1 on v0

v1 whole, which is shorter than its diff:
```python
import functools

import jax
import jax.numpy as jnp
from jax import lax
from jax.experimental import pallas as pl
from jax.experimental.pallas import tpu as pltpu
from jax.sharding import PartitionSpec as P

PANELS = 2
BLOCK = 128
GROUP = 8


def factor_block(block):
    group_count = BLOCK // GROUP
    lane = lax.broadcasted_iota(jnp.int32, (GROUP, BLOCK), 1)
    sub = lax.broadcasted_iota(jnp.int32, (GROUP, BLOCK), 0)
    rows = [block[GROUP * m : GROUP * (m + 1), :] for m in range(group_count)]
    factor = [jnp.zeros((GROUP, BLOCK), jnp.float32) for _ in range(group_count)]
    inverse = []
    for s in range(group_count):
        first = GROUP * s
        columns = {
            m: [
                jnp.broadcast_to(rows[m][:, first + j : first + j + 1], (GROUP, BLOCK))
                for j in range(GROUP)
            ]
            for m in range(s, group_count)
        }
        entry = {
            (k, j): jnp.broadcast_to(columns[s][j][k : k + 1, :], (GROUP, BLOCK))
            for j in range(GROUP)
            for k in range(j, GROUP)
        }
        here = (lane >= first) & (lane < first + GROUP)
        own = jnp.where(here, (lane - first == sub).astype(jnp.float32), rows[s])
        spread = [jnp.broadcast_to(own[k : k + 1, :], (GROUP, BLOCK)) for k in range(GROUP)]
        reciprocal, ratio = [], {}
        for j in range(GROUP):
            reciprocal.append(1.0 / entry[j, j])
            for k in range(j + 1, GROUP):
                ratio[k, j] = entry[k, j] * reciprocal[j]
            for k in range(j + 1, GROUP):
                for i in range(k, GROUP):
                    entry[i, k] = entry[i, k] - entry[i, j] * ratio[k, j]
                spread[k] = spread[k] - ratio[k, j] * spread[j]
        scale = [lax.rsqrt(entry[j, j]) for j in range(GROUP)]
        for m in range(s, group_count):
            piece = columns[m]
            for k in range(GROUP):
                for j in range(k):
                    piece[k] = piece[k] - ratio[k, j] * piece[j]
                factor[m] = jnp.where(lane == first + k, piece[k] * scale[k], factor[m])
            if m > s:
                parts = [piece[k] * reciprocal[k] * spread[k] for k in range(GROUP)]
                while len(parts) > 1:
                    parts = [parts[i] + parts[i + 1] for i in range(0, len(parts), 2)]
                rows[m] = jnp.where(here, 0.0, rows[m]) - parts[0]
        done = jnp.zeros((GROUP, BLOCK), jnp.float32)
        for k in range(GROUP):
            done = jnp.where(sub == k, spread[k] * scale[k], done)
        inverse.append(jnp.where(lane <= first + sub, done, 0.0))
        factor[s] = jnp.where(lane <= first + sub, factor[s], 0.0)
    return jnp.concatenate(factor, 0), jnp.concatenate(inverse, 0)


def exact_dot(left, right, dims):
    return lax.dot_general(
        left, right, (dims, ((), ())),
        precision=lax.Precision.HIGHEST, preferred_element_type=jnp.float32,
    )


def factor_kernel(a_ref, l_ref, w_ref, s_ref):
    order = a_ref.shape[0]
    count = order // BLOCK
    row = lax.broadcasted_iota(jnp.int32, (BLOCK, BLOCK), 0)
    col = lax.broadcasted_iota(jnp.int32, (BLOCK, BLOCK), 1)
    for i in range(count):
        for j in range(i + 1):
            tile = a_ref[i * BLOCK : (i + 1) * BLOCK, j * BLOCK : (j + 1) * BLOCK]
            flipped = tile.T
            if i == j:
                tile = jnp.where(row >= col, tile, flipped)
            else:
                s_ref[j * BLOCK : (j + 1) * BLOCK, i * BLOCK : (i + 1) * BLOCK] = flipped
            s_ref[i * BLOCK : (i + 1) * BLOCK, j * BLOCK : (j + 1) * BLOCK] = tile
    l_ref[...] = jnp.zeros_like(l_ref)
    lane = lax.broadcasted_iota(jnp.int32, (BLOCK, order), 1)

    def step(b, carry):
        start = pl.multiple_of(b * BLOCK, BLOCK)
        own = pl.ds(start, BLOCK)
        lower, inverse = factor_block(s_ref[own, own])
        l_ref[own, own] = lower
        s_ref[own, own] = (row == col).astype(jnp.float32)
        strip = exact_dot(inverse, s_ref[own, :], ((1,), (0,)))
        w_ref[own, :] = jnp.where(lane < start + BLOCK, strip, 0.0)

        def below(m, carry):
            these = pl.ds(pl.multiple_of(m * BLOCK, BLOCK), BLOCK)
            solved = exact_dot(s_ref[these, own], inverse, ((1,), (1,)))
            l_ref[these, own] = solved
            s_ref[these, own] = jnp.zeros((BLOCK, BLOCK), jnp.float32)
            s_ref[these, :] = s_ref[these, :] - exact_dot(solved, strip, ((1,), (0,)))
            return carry

        return lax.fori_loop(b + 1, count, below, carry)

    lax.fori_loop(0, count, step, 0)


def factor_tile(tile):
    order = tile.shape[0]
    flat = jax.ShapeDtypeStruct((order, order), jnp.float32)
    return pl.pallas_call(
        factor_kernel,
        out_shape=[flat, flat],
        in_specs=[pl.BlockSpec(memory_space=pltpu.VMEM)],
        out_specs=[pl.BlockSpec(memory_space=pltpu.VMEM)] * 2,
        scratch_shapes=[pltpu.VMEM((order, order), jnp.float32)],
        compiler_params=pltpu.CompilerParams(vmem_limit_bytes=32 * 2**20),
        cost_estimate=pl.CostEstimate(
            flops=order * 60_000_000, transcendentals=0, bytes_accessed=12 * order * order
        ),
    )(tile)


def dot_nt(left, right):
    return lax.dot_general(
        left, right, (((1,), (1,)), ((), ())),
        precision=lax.Precision.HIGH, preferred_element_type=jnp.float32,
    )


def dot_nn(left, right):
    return lax.dot_general(
        left, right, (((1,), (0,)), ((), ())),
        precision=lax.Precision.HIGH, preferred_element_type=jnp.float32,
    )


def exchange(block, bit, tile_count):
    return lax.ppermute(block, "tiles", [(i, i ^ bit) for i in range(tile_count)])


def tile_bits(tile_count):
    bits, bit = [], 2
    while bit < tile_count:
        bits.append(bit)
        bit *= 2
    return bits + [1]


def along_cols(block, source, col_pos, col_count):
    out = block
    for step in (1, -1):
        held, at = block, source
        while 0 <= at + step < col_count:
            held = lax.ppermute(held, "cols", [(at, at + step)])
            at += step
            out = jnp.where(col_pos == at, held, out)
    return out


def gather_rows(piece, tile_pos, tile_count):
    held = piece[None]
    bits = tile_bits(tile_count)
    for bit in bits:
        held = jnp.concatenate((held, exchange(held, bit, tile_count)), 0)
    weights = []
    for m in range(tile_count):
        weights.append(sum(bit for p, bit in enumerate(bits) if m >> p & 1))
    place = {w: m for m, w in enumerate(weights)}
    sorted_pieces = []
    table = jnp.array([place[w] for w in range(tile_count)], jnp.int32)
    for i in range(tile_count):
        m = table[i ^ tile_pos]
        sorted_pieces.append(lax.dynamic_index_in_dim(held, m, 0, keepdims=False))
    return jnp.concatenate(sorted_pieces, 1)


def fetch_target(block, tile_pos, tile_count, target):
    for bit in tile_bits(tile_count)[:-1]:
        other = exchange(block, bit, tile_count)
        mine = (tile_pos & bit) == ((2 * target) & bit)
        block = jnp.where(mine, block, other)
    other = exchange(block, 1, tile_count)
    even = tile_pos % 2 == 0
    return jnp.concatenate((jnp.where(even, block, other), jnp.where(even, other, block)), 0)


def shards(tile_count, col_count, front_diag, front_below, ancestor, owner_cols, rel):
    rows, width = front_diag.shape
    lead = PANELS * width
    steps = lead // rows
    tile_pos = lax.axis_index("tiles")
    col_pos = lax.axis_index("cols")
    target = lax.dynamic_slice_in_dim(owner_cols, col_pos, 1)[0]
    later_col = jnp.maximum(col_pos, PANELS)

    pieces = lax.all_to_all(
        front_diag.reshape(tile_count, rows // tile_count, width), "tiles", 0, 0, tiled=True
    )

    def spread_pieces(first, count, columns):
        parts = []
        for panel in range(PANELS):
            take = min(width, columns - panel * width)
            if take > 0:
                parts.append(
                    along_cols(
                        pieces[first : first + count, :, :take], panel, col_pos, col_count
                    )
                )
        return jnp.concatenate(parts, 2)

    lead_rows = []
    for i in range(steps):
        piece = spread_pieces(i, 1, (i + 1) * rows)
        lead_rows.append(gather_rows(piece, tile_pos, tile_count)[0])
    own_below = jnp.concatenate(
        [along_cols(front_below, panel, col_pos, col_count) for panel in range(PANELS)], 1
    )
    side = gather_rows(
        spread_pieces(steps, tile_count - steps, lead), tile_pos, tile_count
    )
    target_below = fetch_target(own_below, tile_pos, tile_count, target)
    match_side = lax.dynamic_slice_in_dim(side, 2 * later_col - steps, 2, 0).reshape(width, lead)
    own_side = lax.dynamic_index_in_dim(
        side, jnp.maximum(tile_pos - steps, 0), 0, keepdims=False
    )

    factor_rows, inverse_rows = [], []
    for i in range(steps):
        diag = lead_rows[i][:, i * rows :]
        if i:
            front = lead_rows[i][:, : i * rows]
            solved = jnp.concatenate(
                [
                    dot_nt(front[:, : (j + 1) * rows], inverse_rows[j][:, : (j + 1) * rows])
                    for j in range(i)
                ],
                1,
            )
            diag = diag - dot_nt(solved, solved)
        factor, inverse = factor_tile(diag)
        if i:
            done = jnp.concatenate(inverse_rows, 0)[:, : i * rows]
            cross = -dot_nn(inverse, dot_nn(solved, done))
            factor_row = jnp.concatenate((solved, factor), 1)
            inverse_row = jnp.concatenate((cross, inverse), 1)
        else:
            factor_row, inverse_row = factor, inverse
        fill = ((0, 0), (0, lead - (i + 1) * rows))
        factor_rows.append(jnp.pad(factor_row, fill))
        inverse_rows.append(jnp.pad(inverse_row, fill))
    both = jnp.concatenate((own_below, own_side), 0)
    solved = jnp.concatenate(
        [
            dot_nt(both[:, : (j + 1) * rows], inverse_rows[j][:, : (j + 1) * rows])
            for j in range(steps)
        ],
        1,
    )
    full_inverse = jnp.concatenate(inverse_rows, 0)
    again = jnp.concatenate(
        [
            dot_nn(
                solved[:, j * rows :], full_inverse[j * rows :, j * rows : (j + 1) * rows]
            )
            for j in range(steps)
        ],
        1,
    )
    change = dot_nt(again, match_side)
    panel_col = jnp.minimum(col_pos, PANELS - 1) * width
    own_solved = lax.dynamic_slice_in_dim(solved, panel_col, width, 1)
    in_lead = col_pos < PANELS
    factor_below = jnp.where(in_lead, own_solved[:rows], front_below - change[:rows])
    lead_factor = lax.dynamic_slice(
        jnp.concatenate(factor_rows, 0),
        (jnp.minimum(tile_pos, steps - 1) * rows, panel_col),
        (rows, width),
    )
    lead_part = jnp.where(tile_pos < steps, lead_factor, own_solved[rows:])
    global_rows = tile_pos * rows + jnp.arange(rows, dtype=jnp.int32)
    global_cols = col_pos * width + jnp.arange(width, dtype=jnp.int32)
    lower_mask = global_rows[:, None] >= global_cols[None, :]
    factor_diag = jnp.where(
        lower_mask, jnp.where(in_lead, lead_part, front_diag - change[rows:]), 0.0
    )
    update = dot_nt(again[:rows], target_below)
    row_places = lax.dynamic_slice_in_dim(rel, tile_pos * rows, rows) - tile_pos * rows
    row_move = (row_places[None, :] == jnp.arange(rows, dtype=jnp.int32)[:, None]).astype(
        jnp.float32
    )
    moved = dot_nn(row_move, update)
    parts = []
    for half in range(width // rows):
        start = target * width + half * rows
        places = lax.dynamic_slice_in_dim(rel, start, rows) - start
        move = (places[None, :] == jnp.arange(rows, dtype=jnp.int32)[:, None]).astype(
            jnp.float32
        )
        parts.append(dot_nt(moved[:, half * rows : (half + 1) * rows], move))
    return (factor_diag, factor_below, ancestor - jnp.concatenate(parts, 1))


def solution(mesh):
    placed = (P("tiles", "cols"), P("tiles", "cols"), P("tiles", "cols"), P(), P())
    return jax.shard_map(
        functools.partial(shards, mesh.shape["tiles"], mesh.shape["cols"]),
        mesh=mesh,
        in_specs=placed,
        out_specs=(P("tiles", "cols"), P("tiles", "cols"), P("tiles", "cols")),
        check_vma=False,
    )
```

time: 1610 us -> 832 us (0.52)
  other arithmetic: 580 us -> 77.7 us
  waiting for transfers between devices: 722 us -> 283 us
  Pallas kernels: 0 us -> 97.9 us
  starting transfers between devices: 0.25 us -> 88.4 us
  blocking collectives: 0 us -> 28.4 us
  local copies, waits for them, and re-layouts: 93.4 us -> 68 us
  matrix products: 178 us -> 157 us
    psum x6 -> x0, waiting for transfers between devices: 722 us -> none  [broadcast(): return lax.psum(block, axis)]
    another operation x66 -> x0, other arithmetic: 516 us -> none  [the longest x60 345 us: factor_tile(): factor = jnp.linalg.cholesky(symmetric)]
    ppermute x0 -> x48, waiting for transfers between devices: none -> 283 us  [the longest x30 154 us: along_cols(): held = lax.ppermute(held, 'cols', [(at, at + step)])]
    pallas_call x0 -> x4, Pallas kernels: none -> 97.9 us  [factor_tile(): pl.pallas_call(factor_kernel, out_shape=[flat, flat], in_specs=[pl.BlockS...]
    another operation x58 -> x0, matrix products: 92.1 us -> none  [the longest x28 46.1 us: factor_tile(): factor = jnp.linalg.cholesky(symmetric)]
    ppermute x0 -> x48, starting transfers between devices: none -> 88.4 us  [the longest x18 52 us: exchange(): lax.ppermute(block, 'tiles', [(i, i ^ bit) for i in range(tile_count)])]
    dot_general x12 -> x28, matrix products: 85.9 us -> 157 us  [the longest x17 97.8 us: dot_nt(): lax.dot_general(left, right, (((1,), (1,)), ((), ())), precision=lax.Prec...]
    another operation x66 -> x0, local copies, waits for them, and re-layouts: 53 us -> none
  transfers between devices with their start and end apart: 6 -> 48, of which waited for: 6 -> 16; matrix products, arithmetic and copies ran while one was open for 0% -> 15% of each run, Pallas kernels for 0% -> 12%
where the time goes in v1:
time: 832 us; the launch traced here: 820 us
  waiting for transfers between devices  283 us (34%)
  matrix products  157 us (19%)
  Pallas kernels  97.9 us (12%)
  starting transfers between devices  88.4 us (11%)
  other arithmetic  77.7 us (9%)
  local copies, waits for them, and re-layouts  68 us (8%)
  blocking collectives  28.4 us (3%)
  between operations  19.1 us (2%)
    ppermute x30, waiting for transfers between devices, along_cols(): held = lax.ppermute(held, 'cols', [(at, at + step)])  154 us
    ppermute x18, waiting for transfers between devices, exchange(): lax.ppermute(block, 'tiles', [(i, i ^ bit) for i in range(tile_count)])  129 us
    pallas_call x4, Pallas kernels, factor_tile(): pl.pallas_call(factor_kernel, out_shape=[flat, flat], in_specs=[pl.BlockS...  97.9 us
    dot_general x17, matrix products, dot_nt(): lax.dot_general(left, right, (((1,), (1,)), ((), ())), precision=lax.Prec...  97.8 us
    dot_general x11, matrix products, dot_nn(): lax.dot_general(left, right, (((1,), (0,)), ((), ())), precision=lax.Prec...  59.6 us
    ppermute x18, starting transfers between devices, exchange(): lax.ppermute(block, 'tiles', [(i, i ^ bit) for i in range(tile_count)])  52 us
    ppermute x30, starting transfers between devices, along_cols(): held = lax.ppermute(held, 'cols', [(at, at + step)])  36.4 us
    all_to_all x1, blocking collectives, shards(): lax.all_to_all(front_diag.reshape(tile_count, rows // tile_count, width),...  28.4 us
  transfers between devices with their start and end apart: 48, of which 16 were waited for; matrix products, arithmetic and copies ran while one was open for 15% of the time, Pallas kernels for 12%

profile of v1, /device:TPU:31, one launch (start us, length us, event | category | flops | bytes accessed | tf_op | source)
XLA Modules:
  0.0 820.4 jit_solution(14352902614265797899)
XLA Ops:
  0.6 28.4 %all_to_all.5 = f32[8,64,1024]{2,1,0:T(8,128)S(1)} all-to-all(f32[8,64,1024]{2,1,0:T(8,128)} %bitcast.133), channel_id=1, replica_groups=mesh['tiles'=8,'cols'=4] {'tiles'}, dimensions={0} | all-to-all | bytes 4194304 | tf_op jit(solution)/shard_map/all_to_all | solution.py:203
  32.4 6.6 collective-permute-done.17
  50.8 9.1 %collective-permute-done.2 = f32[1,64,512]{2,1,0:T(8,128)} collective-permute-done((f32[1,64,512]{2,1,0:T(8,128)}, f32[1,64,512]{2,1,0:T(8,128)}, u32[]{:S(2)}, u32[]{:S(2)}) %collective-permute-start.2) | collective-permute-done | bytes 131104 | tf_op jit(solution)/shard_map/ppermute | solution.py:161
  62.6 3.3 collective-permute-done.26
  65.9 5.6 collective-permute-done.23
  111.1 3.6 collective-permute-start.5
  114.7 36.4 %collective-permute-done.14 = f32[1,64,1024]{2,1,0:T(8,128)S(1)} collective-permute-done((f32[1,64,1024]{2,1,0:T(8,128)}, f32[1,64,1024]{2,1,0:T(8,128)S(1)}, u32[]{:S(2)}, u32[]{:S(2)}) %collective-permute-start.14) | collective-permute-done | bytes 262176 | tf_op jit(solution)/shard_map/ppermute | solution.py:161
  151.9 4.8 collective-permute-done.8
  163.9 9.6 %collective-permute-done.18 = f32[1,1,64,1536]{3,2,1,0:T(8,128)S(1)} collective-permute-done((f32[1,1,64,1536]{3,2,1,0:T(8,128)S(1)}, f32[1,1,64,1536]{3,2,1,0:T(8,128)S(1)}, u32[]{:S(2)}, u32[]{:S(2)}) %collective-permute-start.18) | collective-permute-done | bytes 393248 | tf_op jit(solution)/shard_map/ppermute | solution.py:145
  179.7 11.7 %collective-permute-done.10 = f32[2,1,64,1024]{3,2,1,0:T(8,128)S(1)} collective-permute-done((f32[2,1,64,1024]{3,2,1,0:T(8,128)S(1)}, f32[2,1,64,1024]{3,2,1,0:T(8,128)S(1)}, u32[]{:S(2)}, u32[]{:S(2)}) %collective-permute-start.10) | collective-permute-done | bytes 524320 | tf_op jit(solution)/shard_map/ppermute | solution.py:145
  193.8 24.3 %shard_map.121 = (f32[512,512]{1,0:T(8,128)S(1)}, f32[512,512]{1,0:T(8,128)S(1)}) custom-call(f32[512,512]{1,0:T(8,128)S(1)} %bitcast.127), custom_call_target="tpu_custom_call" | custom-call | flops 30720000000 | bytes 3145728 | tf_op jit(solution)/shard_map/pallas_call | solution.py:117
  220.9 9.3 %collective-permute-start.11 = (f32[4,1,64,1024]{3,2,1,0:T(8,128)S(1)}, f32[4,1,64,1024]{3,2,1,0:T(8,128)S(1)}, u32[]{:S(2)}, u32[]{:S(2)}) collective-permute-start(f32[4,1,64,1024]{3,2,1,0:T(8,128)S(1)} %pad_maximum_fusion.38), channel_id=1, source_target_pairs={{0,4},{4,0},{8,12},{12,8},{16,20},{20,16},{24,28},{28,24},{1,5},{5... | collective-permute-start | bytes 3145736 | tf_op jit(solution)/shard_map/ppermute | solution.py:145
  235.0 39.0 %collective-permute-done.41 = f32[4,64,1024]{2,1,0:T(8,128)S(1)} collective-permute-done((f32[4,64,1024]{2,1,0:T(8,128)S(1)}, f32[4,64,1024]{2,1,0:T(8,128)S(1)}, u32[]{:S(2)}, u32[]{:S(2)}) %collective-permute-start.41) | collective-permute-done | bytes 1048608 | tf_op jit(solution)/shard_map/ppermute | solution.py:161
  275.3 18.8 %collective-permute-start.29 = (f32[4,1,64,2048]{3,2,1,0:T(8,128)}, f32[4,1,64,2048]{3,2,1,0:T(8,128)}, u32[]{:S(2)}, u32[]{:S(2)}) collective-permute-start(f32[4,1,64,2048]{3,2,1,0:T(8,128)} %pad_maximum_fusion.33), channel_id=1, source_target_pairs={{0,4},{4,0},{8,12},{12,8},{16,20},{20,16},{24,28},{28,24},{1,5},{5... | collective-permute-start | bytes 6291464 | tf_op jit(solution)/shard_map/ppermute | solution.py:145
  300.5 9.5 %collective-permute-start.20 = (f32[4,1,64,1536]{3,2,1,0:T(8,128)}, f32[4,1,64,1536]{3,2,1,0:T(8,128)}, u32[]{:S(2)}, u32[]{:S(2)}) collective-permute-start(f32[4,1,64,1536]{3,2,1,0:T(8,128)} %pad_maximum_fusion.36), channel_id=1, source_target_pairs={{0,4},{4,0},{8,12},{12,8},{16,20},{20,16},{24,28},{28,24},{1,5},{5... | collective-permute-start | bytes 4718600 | tf_op jit(solution)/shard_map/ppermute | solution.py:145
  312.5 24.7 %shard_map.122 = (f32[512,512]{1,0:T(8,128)S(1)}, f32[512,512]{1,0:T(8,128)S(1)}) custom-call(f32[512,512]{1,0:T(8,128)S(1)} %convolution_subtract_fusion.a_ref), custom_call_target="tpu_custom_call" | custom-call | flops 30720000000 | bytes 3145728 | tf_op jit(solution)/shard_map/pallas_call | solution.py:117
  351.2 44.9 %collective-permute-done.32 = f32[512,1024]{1,0:T(8,128)} collective-permute-done((f32[512,1024]{1,0:T(8,128)}, f32[512,1024]{1,0:T(8,128)}, u32[]{:S(2)}, u32[]{:S(2)}) %collective-permute-start.32) | collective-permute-done | bytes 2097184 | tf_op jit(solution)/shard_map/ppermute | solution.py:161
  396.2 4.6 select_select_fusion.1
  409.2 24.4 %shard_map.123 = (f32[512,512]{1,0:T(8,128)S(1)}, f32[512,512]{1,0:T(8,128)S(1)}) custom-call(f32[512,512]{1,0:T(8,128)S(1)} %slice_subtract_fusion.3.a_ref), custom_call_target="tpu_custom_call" | custom-call | flops 30720000000 | bytes 3145728 | tf_op jit(solution)/shard_map/pallas_call | solution.py:117
  433.7 3.7 fusion.36
  439.3 55.9 %collective-permute-done.45 = f32[512,2048]{1,0:T(8,128)S(1)} collective-permute-done((f32[512,2048]{1,0:T(8,128)}, f32[512,2048]{1,0:T(8,128)S(1)}, u32[]{:S(2)}, u32[]{:S(2)}) %collective-permute-start.45) | collective-permute-done | bytes 4194336 | tf_op jit(solution)/shard_map/ppermute | solution.py:145
  504.9 4.7 pad.26
  509.7 3.9 select_maximum_fusion
  516.4 5.5 pad_maximum_fusion.5
  526.2 3.7 fusion.50
  532.4 3.7 fusion.71
  543.2 47.6 %collective-permute-done.46 = f32[512,2048]{1,0:T(8,128)} collective-permute-done((f32[512,2048]{1,0:T(8,128)}, f32[512,2048]{1,0:T(8,128)}, u32[]{:S(2)}, u32[]{:S(2)}) %collective-permute-start.46) | collective-permute-done | bytes 4194336 | tf_op jit(solution)/shard_map/ppermute | solution.py:145
  595.2 4.0 slice_subtract_fusion.2.a_ref
  599.2 12.8 %fusion = f32[512,1536]{1,0:T(8,128)} fusion(f32[512,2048]{1,0:T(8,128)} %pad.26, f32[512,2048]{1,0:T(8,128)} %pad.25, f32[512,2048]{1,0:T(8,128)S(1)} %copy-done.28, f32[512,512]{0,1:T(8,128)S(1)} %copy-done.45, f32[512,512]{0,1:T(8,128)S(1)} %fusion.71, f32[512,512]{0,1:T(8,128)S(1)} %copy-done.46), kind=kOutput, calls=%fused_computation.9 | convolution fusion | flops 7254048768 | bytes 18874368 | tf_op jit(solution)/shard_map/dot_general | solution.py:138
  612.0 24.5 %shard_map.124 = (f32[512,512]{1,0:T(8,128)S(1)}, f32[512,512]{1,0:T(8,128)S(1)}) custom-call(f32[512,512]{1,0:T(8,128)S(1)} %slice_subtract_fusion.2.a_ref), custom_call_target="tpu_custom_call" | custom-call | flops 30720000000 | bytes 3145728 | tf_op jit(solution)/shard_map/pallas_call | solution.py:117
  636.5 4.6 convolution_negate_fusion
  641.1 6.8 broadcast_select_fusion.3
  647.9 5.6 pad_maximum_fusion
  665.0 4.8 dynamic-slice_bitcast_fusion
  669.8 6.4 pad_maximum_fusion.6
  676.3 9.2 %fusion.14 = f32[1024,512]{0,1:T(8,128)} fusion(f32[1024,2048]{1,0:T(8,128)} %pad_maximum_fusion.6, f32[512,512]{1,0:T(8,128)S(1)} %copy-done.1, f32[512,1024]{1,0:T(8,128)} %copy-done.20), kind=kOutput, calls=%fused_computation.27 | convolution fusion | flops 4832624640 | bytes 11534336 | tf_op jit(solution)/shard_map/dot_general | solution.py:131
  685.5 4.9 fusion.34
  690.4 6.9 fusion.38
  698.7 3.6 fusion.103
  705.2 7.6 fusion.42
  715.7 10.1 %fusion.16 = f32[1024,512]{0,1:T(8,128)} fusion(f32[1024,512]{0,1:T(8,128)} %copy-done.26, f32[1024,512]{0,1:T(8,128)} %fusion.14, f32[1024,512]{0,1:T(8,128)} %fusion.34, f32[512,512]{1,0:T(8,128)S(1)} %get-tuple-element.18, f32[512,1536]{1,0:T(8,128)} %convolution_negate_fusion, f32[512,2048]{1,0:T(8,128)} %pad.26, f32[512,2048]{1,0:T(8,128)} %pad.25), kind=kOutput, calls=%fused_computation.29 | convolution fusion | flops 4837343232 | bytes 20971520 | tf_op jit(solution)/shard_map/dot_general | solution.py:138
  728.9 4.9 fusion.65
  733.8 11.9 %fusion.30 = f32[1024,512]{0,1:T(8,128)} fusion(f32[512,512]{1,0:T(8,128)S(1)} %get-tuple-element.18, f32[512,1536]{1,0:T(8,128)} %convolution_negate_fusion, f32[512,2048]{1,0:T(8,128)} %pad.26, f32[512,2048]{1,0:T(8,128)} %pad.25, f32[512,2048]{1,0:T(8,128)S(1)} %copy-done.29, f32[1024,512]{1,0:T(8,128)S(1)} %copy-done.39, f32[1024,512]{1,0:T(8,128)} %copy.22, ...), kind=kOutput, calls=%fused_computation.44 | convolution fusion | flops 6452936704 | bytes 27262976 | tf_op jit(solution)/shard_map/dot_general | solution.py:138
  745.7 5.3 pad_maximum_fusion.7
  751.0 4.4 constant_dynamic-slice_fusion
  755.4 31.3 %fusion.2 = f32[1024,1024]{1,0:T(8,128)} fusion(f32[1024,2048]{1,0:T(8,128)S(1)} %bitcast.132, f32[1024,512]{0,1:T(8,128)} %fusion.103, f32[1024,512]{0,1:T(8,128)} %fusion.42, f32[1024,512]{0,1:T(8,128)} %fusion.16, f32[1024,512]{0,1:T(8,128)} %fusion.30), kind=kOutput, calls=%fused_computation.15 | convolution fusion | flops 12891193344 | bytes 20971520 | tf_op jit(solution)/shard_map/dot_general | solution.py:131
  786.7 17.7 %fusion.10 = f32[512,1024]{1,0:T(8,128)S(1)} fusion(f32[512,2048]{1,0:T(8,128)} %get-tuple-element.25, f32[512,2048]{1,0:T(8,128)} %get-tuple-element.24, f32[1024,512]{0,1:T(8,128)} %fusion.103, f32[1024,512]{0,1:T(8,128)} %fusion.42, f32[1024,512]{0,1:T(8,128)} %fusion.16, f32[1024,512]{0,1:T(8,128)} %fusion.30), kind=kOutput, calls=%fused_computation.23 | convolution fusion | flops 6447693824 | bytes 18874368 | tf_op jit(solution)/shard_map/dot_general | solution.py:131
  812.3 7.7 fusion.63
  (321 shorter events, 159.0 us)
Async XLA Ops:
  29.0 1.4 collective-permute-start.16
  29.7 2.7 collective-permute-start.15
  30.4 8.6 %collective-permute-start.17 = (f32[1,64,512]{2,1,0:T(8,128)S(1)}, f32[1,64,512]{2,1,0:T(8,128)S(1)}, u32[]{:S(2)}, u32[]{:S(2)}) collective-permute-start(f32[1,64,512]{2,1,0:T(8,128)S(1)} %collective-permute-done.16), channel_id=1, source_target_pairs={{2,3},{6,7},{10,11},{14,15},{18,19},{22,23},{26,27},{30,31}} | collective-permute-start | bytes 393224 | tf_op jit(solution)/shard_map/ppermute | solution.py:161
  31.8 9.4 %collective-permute-start.21 = (f32[1,64,1024]{2,1,0:T(8,128)S(1)}, f32[1,64,1024]{2,1,0:T(8,128)S(1)}, u32[]{:S(2)}, u32[]{:S(2)}) collective-permute-start(f32[1,64,1024]{2,1,0:T(8,128)S(1)} %slice.151), channel_id=1, source_target_pairs={{0,1},{4,5},{8,9},{12,13},{16,17},{20,21},{24,25},{28,29}} | collective-permute-start | bytes 786440 | tf_op jit(solution)/shard_map/ppermute | solution.py:161
  39.8 2.0 collective-permute-start
  40.4 4.7 collective-permute-start.25
  41.1 5.3 collective-permute-start.22
  41.8 1.3 collective-permute-start.1
  43.1 16.8 %collective-permute-start.2 = (f32[1,64,512]{2,1,0:T(8,128)}, f32[1,64,512]{2,1,0:T(8,128)}, u32[]{:S(2)}, u32[]{:S(2)}) collective-permute-start(f32[1,64,512]{2,1,0:T(8,128)} %collective-permute-done.1), channel_id=1, source_target_pairs={{2,3},{6,7},{10,11},{14,15},{18,19},{22,23},{26,27},{30,31}} | collective-permute-start | bytes 393224 | tf_op jit(solution)/shard_map/ppermute | solution.py:161
  44.4 18.1 %collective-permute-start.24 = (f32[1,64,1024]{2,1,0:T(8,128)S(1)}, f32[1,64,1024]{2,1,0:T(8,128)S(1)}, u32[]{:S(2)}, u32[]{:S(2)}) collective-permute-start(f32[1,64,1024]{2,1,0:T(8,128)S(1)} %slice.151), channel_id=1, source_target_pairs={{1,0},{5,4},{9,8},{13,12},{17,16},{21,20},{25,24},{29,28}} | collective-permute-start | bytes 786440 | tf_op jit(solution)/shard_map/ppermute | solution.py:161
  45.1 20.8 %collective-permute-start.26 = (f32[1,64,1024]{2,1,0:T(8,128)S(1)}, f32[1,64,1024]{2,1,0:T(8,128)}, u32[]{:S(2)}, u32[]{:S(2)}) collective-permute-start(f32[1,64,1024]{2,1,0:T(8,128)S(1)} %collective-permute-done.25), channel_id=1, source_target_pairs={{2,3},{6,7},{10,11},{14,15},{18,19},{22,23},{26,27},{30,31}} | collective-permute-start | bytes 786440 | tf_op jit(solution)/shard_map/ppermute | solution.py:161
  46.4 25.1 %collective-permute-start.23 = (f32[1,64,1024]{2,1,0:T(8,128)S(1)}, f32[1,64,1024]{2,1,0:T(8,128)}, u32[]{:S(2)}, u32[]{:S(2)}) collective-permute-start(f32[1,64,1024]{2,1,0:T(8,128)S(1)} %collective-permute-done.22), channel_id=1, source_target_pairs={{2,3},{6,7},{10,11},{14,15},{18,19},{22,23},{26,27},{30,31}} | collective-permute-start | bytes 786440 | tf_op jit(solution)/shard_map/ppermute | solution.py:161
  47.7 112.0 %collective-permute-start.30 = (f32[512,1024]{1,0:T(8,128)}, f32[512,1024]{1,0:T(8,128)}, u32[]{:S(2)}, u32[]{:S(2)}) collective-permute-start(f32[512,1024]{1,0:T(8,128)} %param.11), channel_id=1, source_target_pairs={{0,1},{4,5},{8,9},{12,13},{16,17},{20,21},{24,25},{28,29}} | collective-permute-start | bytes 6291464 | tf_op jit(solution)/shard_map/ppermute | solution.py:161
  59.9 49.0 %collective-permute-start.36 = (f32[4,64,1024]{2,1,0:T(8,128)}, f32[4,64,1024]{2,1,0:T(8,128)}, u32[]{:S(2)}, u32[]{:S(2)}) collective-permute-start(f32[4,64,1024]{2,1,0:T(8,128)} %slice.156), channel_id=1, source_target_pairs={{0,1},{4,5},{8,9},{12,13},{16,17},{20,21},{24,25},{28,29}} | collective-permute-start | bytes 3145736 | tf_op jit(solution)/shard_map/ppermute | solution.py:161
  62.5 13.0 %collective-permute-start.3 = (f32[1,1,64,512]{3,2,1,0:T(8,128)S(1)}, f32[1,1,64,512]{3,2,1,0:T(8,128)S(1)}, u32[]{:S(2)}, u32[]{:S(2)}) collective-permute-start(f32[1,1,64,512]{3,2,1,0:T(8,128)S(1)} %select_bitcast_fusion.1), channel_id=1, source_target_pairs={{0,8},{4,12},{8,0},{12,4},{16,24},{20,28},{24,16},{28,20},{1,9},{5... | collective-permute-start | bytes 393224 | tf_op jit(solution)/shard_map/ppermute | solution.py:145
  72.8 4.7 collective-permute-start.12
  74.2 3.4 collective-permute-start.6
  75.6 5.7 collective-permute-start.4
  77.4 33.6 %collective-permute-start.27 = (f32[1,1,64,2048]{3,2,1,0:T(8,128)S(1)}, f32[1,1,64,2048]{3,2,1,0:T(8,128)S(1)}, u32[]{:S(2)}, u32[]{:S(2)}) collective-permute-start(f32[1,1,64,2048]{3,2,1,0:T(8,128)S(1)} %maximum_bitcast_fusion.1), channel_id=1, source_target_pairs={{0,8},{4,12},{8,0},{12,4},{16,24},{20,28},{24,16},{28,20},{1,9},{5... | collective-permute-start | bytes 1572872 | tf_op jit(solution)/shard_map/ppermute | solution.py:145
  77.5 27.8 %collective-permute-start.13 = (f32[1,64,1024]{2,1,0:T(8,128)}, f32[1,64,1024]{2,1,0:T(8,128)}, u32[]{:S(2)}, u32[]{:S(2)}) collective-permute-start(f32[1,64,1024]{2,1,0:T(8,128)} %collective-permute-done.12), channel_id=1, source_target_pairs={{1,2},{5,6},{9,10},{13,14},{17,18},{21,22},{25,26},{29,30}} | collective-permute-start | bytes 786440 | tf_op jit(solution)/shard_map/ppermute | solution.py:161
  81.3 25.3 %collective-permute-start.7 = (f32[1,64,1024]{2,1,0:T(8,128)}, f32[1,64,1024]{2,1,0:T(8,128)}, u32[]{:S(2)}, u32[]{:S(2)}) collective-permute-start(f32[1,64,1024]{2,1,0:T(8,128)} %collective-permute-done.6), channel_id=1, source_target_pairs={{1,2},{5,6},{9,10},{13,14},{17,18},{21,22},{25,26},{29,30}} | collective-permute-start | bytes 786440 | tf_op jit(solution)/shard_map/ppermute | solution.py:161
  105.3 45.9 %collective-permute-start.14 = (f32[1,64,1024]{2,1,0:T(8,128)}, f32[1,64,1024]{2,1,0:T(8,128)S(1)}, u32[]{:S(2)}, u32[]{:S(2)}) collective-permute-start(f32[1,64,1024]{2,1,0:T(8,128)} %collective-permute-done.13), channel_id=1, source_target_pairs={{2,3},{6,7},{10,11},{14,15},{18,19},{22,23},{26,27},{30,31}} | collective-permute-start | bytes 786440 | tf_op jit(solution)/shard_map/ppermute | solution.py:161
  106.6 50.0 %collective-permute-start.8 = (f32[1,64,1024]{2,1,0:T(8,128)}, f32[1,64,1024]{2,1,0:T(8,128)S(1)}, u32[]{:S(2)}, u32[]{:S(2)}) collective-permute-start(f32[1,64,1024]{2,1,0:T(8,128)} %collective-permute-done.7), channel_id=1, source_target_pairs={{2,3},{6,7},{10,11},{14,15},{18,19},{22,23},{26,27},{30,31}} | collective-permute-start | bytes 786440 | tf_op jit(solution)/shard_map/ppermute | solution.py:161
  108.9 66.7 %collective-permute-start.34 = (f32[512,1024]{1,0:T(8,128)}, f32[512,1024]{1,0:T(8,128)}, u32[]{:S(2)}, u32[]{:S(2)}) collective-permute-start(f32[512,1024]{1,0:T(8,128)} %param.11), channel_id=1, source_target_pairs={{1,2},{5,6},{9,10},{13,14},{17,18},{21,22},{25,26},{29,30}} | collective-permute-start | bytes 6291464 | tf_op jit(solution)/shard_map/ppermute | solution.py:161
  111.1 47.4 %collective-permute-start.5 = (f32[4,1,64,512]{3,2,1,0:T(8,128)S(1)}, f32[4,1,64,512]{3,2,1,0:T(8,128)S(1)}, u32[]{:S(2)}, u32[]{:S(2)}) collective-permute-start(f32[4,1,64,512]{3,2,1,0:T(8,128)S(1)} %pad_maximum_fusion.45), channel_id=1, source_target_pairs={{0,4},{4,0},{8,12},{12,8},{16,20},{20,16},{24,28},{28,24},{1,5},{5... | collective-permute-start | bytes 1572872 | tf_op jit(solution)/shard_map/ppermute | solution.py:145
  151.2 25.3 %collective-permute-start.40 = (f32[4,64,1024]{2,1,0:T(8,128)}, f32[4,64,1024]{2,1,0:T(8,128)S(1)}, u32[]{:S(2)}, u32[]{:S(2)}) collective-permute-start(f32[4,64,1024]{2,1,0:T(8,128)} %slice.156), channel_id=1, source_target_pairs={{1,2},{5,6},{9,10},{13,14},{17,18},{21,22},{25,26},{29,30}} | collective-permute-start | bytes 3145736 | tf_op jit(solution)/shard_map/ppermute | solution.py:161
  156.6 21.8 %collective-permute-start.37 = (f32[4,64,1024]{2,1,0:T(8,128)}, f32[4,64,1024]{2,1,0:T(8,128)S(1)}, u32[]{:S(2)}, u32[]{:S(2)}) collective-permute-start(f32[4,64,1024]{2,1,0:T(8,128)} %collective-permute-done.36), channel_id=1, source_target_pairs={{1,2},{5,6},{9,10},{13,14},{17,18},{21,22},{25,26},{29,30}} | collective-permute-start | bytes 3145736 | tf_op jit(solution)/shard_map/ppermute | solution.py:161
  158.5 5.3 collective-permute-start.9
  159.7 32.8 %collective-permute-start.28 = (f32[2,1,64,2048]{3,2,1,0:T(8,128)S(1)}, f32[2,1,64,2048]{3,2,1,0:T(8,128)S(1)}, u32[]{:S(2)}, u32[]{:S(2)}) collective-permute-start(f32[2,1,64,2048]{3,2,1,0:T(8,128)S(1)} %pad_maximum_fusion.39), channel_id=1, source_target_pairs={{0,16},{4,20},{8,24},{12,28},{16,0},{20,4},{24,8},{28,12},{1,17},{... | collective-permute-start | bytes 3145736 | tf_op jit(solution)/shard_map/ppermute | solution.py:145
  163.8 9.7 %collective-permute-start.18 = (f32[1,1,64,1536]{3,2,1,0:T(8,128)S(1)}, f32[1,1,64,1536]{3,2,1,0:T(8,128)S(1)}, u32[]{:S(2)}, u32[]{:S(2)}) collective-permute-start(f32[1,1,64,1536]{3,2,1,0:T(8,128)S(1)} %maximum_bitcast_fusion.2), channel_id=1, source_target_pairs={{0,8},{4,12},{8,0},{12,4},{16,24},{20,28},{24,16},{28,20},{1,9},{5... | collective-permute-start | bytes 1179656 | tf_op jit(solution)/shard_map/ppermute | solution.py:145
  173.5 17.9 %collective-permute-start.10 = (f32[2,1,64,1024]{3,2,1,0:T(8,128)S(1)}, f32[2,1,64,1024]{3,2,1,0:T(8,128)S(1)}, u32[]{:S(2)}, u32[]{:S(2)}) collective-permute-start(f32[2,1,64,1024]{3,2,1,0:T(8,128)S(1)} %pad_maximum_fusion.46), channel_id=1, source_target_pairs={{0,16},{4,20},{8,24},{12,28},{16,0},{20,4},{24,8},{28,12},{1,17},{... | collective-permute-start | bytes 1572872 | tf_op jit(solution)/shard_map/ppermute | solution.py:145
  175.7 57.4 %collective-permute-start.39 = (f32[4,64,1024]{2,1,0:T(8,128)}, f32[4,64,1024]{2,1,0:T(8,128)S(1)}, u32[]{:S(2)}, u32[]{:S(2)}) collective-permute-start(f32[4,64,1024]{2,1,0:T(8,128)} %slice.156), channel_id=1, source_target_pairs={{1,0},{5,4},{9,8},{13,12},{17,16},{21,20},{25,24},{29,28}} | collective-permute-start | bytes 3145736 | tf_op jit(solution)/shard_map/ppermute | solution.py:161
  176.4 98.9 %collective-permute-start.31 = (f32[512,1024]{1,0:T(8,128)}, f32[512,1024]{1,0:T(8,128)}, u32[]{:S(2)}, u32[]{:S(2)}) collective-permute-start(f32[512,1024]{1,0:T(8,128)} %collective-permute-done.30), channel_id=1, source_target_pairs={{1,2},{5,6},{9,10},{13,14},{17,18},{21,22},{25,26},{29,30}} | collective-permute-start | bytes 6291464 | tf_op jit(solution)/shard_map/ppermute | solution.py:161
  178.4 95.6 %collective-permute-start.41 = (f32[4,64,1024]{2,1,0:T(8,128)S(1)}, f32[4,64,1024]{2,1,0:T(8,128)S(1)}, u32[]{:S(2)}, u32[]{:S(2)}) collective-permute-start(f32[4,64,1024]{2,1,0:T(8,128)S(1)} %collective-permute-done.40), channel_id=1, source_target_pairs={{2,3},{6,7},{10,11},{14,15},{18,19},{22,23},{26,27},{30,31}} | collective-permute-start | bytes 3145736 | tf_op jit(solution)/shard_map/ppermute | solution.py:161
  191.4 29.5 %collective-permute-start.19 = (f32[2,1,64,1536]{3,2,1,0:T(8,128)S(1)}, f32[2,1,64,1536]{3,2,1,0:T(8,128)S(1)}, u32[]{:S(2)}, u32[]{:S(2)}) collective-permute-start(f32[2,1,64,1536]{3,2,1,0:T(8,128)S(1)} %pad_maximum_fusion.42), channel_id=1, source_target_pairs={{0,16},{4,20},{8,24},{12,28},{16,0},{20,4},{24,8},{28,12},{1,17},{... | collective-permute-start | bytes 2359304 | tf_op jit(solution)/shard_map/ppermute | solution.py:145
  192.5 103.9 %collective-permute-start.38 = (f32[4,64,1024]{2,1,0:T(8,128)S(1)}, f32[4,64,1024]{2,1,0:T(8,128)S(1)}, u32[]{:S(2)}, u32[]{:S(2)}) collective-permute-start(f32[4,64,1024]{2,1,0:T(8,128)S(1)} %collective-permute-done.37), channel_id=1, source_target_pairs={{2,3},{6,7},{10,11},{14,15},{18,19},{22,23},{26,27},{30,31}} | collective-permute-start | bytes 3145736 | tf_op jit(solution)/shard_map/ppermute | solution.py:161
  220.9 79.6 %collective-permute-start.11 = (f32[4,1,64,1024]{3,2,1,0:T(8,128)S(1)}, f32[4,1,64,1024]{3,2,1,0:T(8,128)S(1)}, u32[]{:S(2)}, u32[]{:S(2)}) collective-permute-start(f32[4,1,64,1024]{3,2,1,0:T(8,128)S(1)} %pad_maximum_fusion.38), channel_id=1, source_target_pairs={{0,4},{4,0},{8,12},{12,8},{16,20},{20,16},{24,28},{28,24},{1,5},{5... | collective-permute-start | bytes 3145736 | tf_op jit(solution)/shard_map/ppermute | solution.py:145
  233.0 116.2 %collective-permute-start.33 = (f32[512,1024]{1,0:T(8,128)}, f32[512,1024]{1,0:T(8,128)}, u32[]{:S(2)}, u32[]{:S(2)}) collective-permute-start(f32[512,1024]{1,0:T(8,128)} %param.11), channel_id=1, source_target_pairs={{1,0},{5,4},{9,8},{13,12},{17,16},{21,20},{25,24},{29,28}} | collective-permute-start | bytes 6291464 | tf_op jit(solution)/shard_map/ppermute | solution.py:161
  274.0 77.2 %collective-permute-start.35 = (f32[512,1024]{1,0:T(8,128)}, f32[512,1024]{1,0:T(8,128)}, u32[]{:S(2)}, u32[]{:S(2)}) collective-permute-start(f32[512,1024]{1,0:T(8,128)} %collective-permute-done.34), channel_id=1, source_target_pairs={{2,3},{6,7},{10,11},{14,15},{18,19},{22,23},{26,27},{30,31}} | collective-permute-start | bytes 6291464 | tf_op jit(solution)/shard_map/ppermute | solution.py:161
  275.3 238.3 %collective-permute-start.29 = (f32[4,1,64,2048]{3,2,1,0:T(8,128)}, f32[4,1,64,2048]{3,2,1,0:T(8,128)}, u32[]{:S(2)}, u32[]{:S(2)}) collective-permute-start(f32[4,1,64,2048]{3,2,1,0:T(8,128)} %pad_maximum_fusion.33), channel_id=1, source_target_pairs={{0,4},{4,0},{8,12},{12,8},{16,20},{20,16},{24,28},{28,24},{1,5},{5... | collective-permute-start | bytes 6291464 | tf_op jit(solution)/shard_map/ppermute | solution.py:145
  296.5 99.7 %collective-permute-start.32 = (f32[512,1024]{1,0:T(8,128)}, f32[512,1024]{1,0:T(8,128)}, u32[]{:S(2)}, u32[]{:S(2)}) collective-permute-start(f32[512,1024]{1,0:T(8,128)} %collective-permute-done.31), channel_id=1, source_target_pairs={{2,3},{6,7},{10,11},{14,15},{18,19},{22,23},{26,27},{30,31}} | collective-permute-start | bytes 6291464 | tf_op jit(solution)/shard_map/ppermute | solution.py:161
  300.5 44.0 %collective-permute-start.20 = (f32[4,1,64,1536]{3,2,1,0:T(8,128)}, f32[4,1,64,1536]{3,2,1,0:T(8,128)}, u32[]{:S(2)}, u32[]{:S(2)}) collective-permute-start(f32[4,1,64,1536]{3,2,1,0:T(8,128)} %pad_maximum_fusion.36), channel_id=1, source_target_pairs={{0,4},{4,0},{8,12},{12,8},{16,20},{20,16},{24,28},{28,24},{1,5},{5... | collective-permute-start | bytes 4718600 | tf_op jit(solution)/shard_map/ppermute | solution.py:145
  344.4 61.9 %collective-permute-start.42 = (f32[1,4,64,2048]{3,2,1,0:T(8,128)S(1)}, f32[1,4,64,2048]{3,2,1,0:T(8,128)S(1)}, u32[]{:S(2)}, u32[]{:S(2)}) collective-permute-start(f32[1,4,64,2048]{3,2,1,0:T(8,128)S(1)} %copy-done.15), channel_id=1, source_target_pairs={{0,8},{4,12},{8,0},{12,4},{16,24},{20,28},{24,16},{28,20},{1,9},{5... | collective-permute-start | bytes 6291464 | tf_op jit(solution)/shard_map/ppermute | solution.py:145
  403.3 91.8 %collective-permute-start.45 = (f32[512,2048]{1,0:T(8,128)}, f32[512,2048]{1,0:T(8,128)S(1)}, u32[]{:S(2)}, u32[]{:S(2)}) collective-permute-start(f32[512,2048]{1,0:T(8,128)} %pad_maximum_fusion.16), channel_id=1, source_target_pairs={{0,8},{4,12},{8,0},{12,4},{16,24},{20,28},{24,16},{28,20},{1,9},{5... | collective-permute-start | bytes 12582920 | tf_op jit(solution)/shard_map/ppermute | solution.py:145
  409.0 106.8 %collective-permute-start.43 = (f32[2,4,64,2048]{3,2,1,0:T(8,128)}, f32[2,4,64,2048]{3,2,1,0:T(8,128)}, u32[]{:S(2)}, u32[]{:S(2)}) collective-permute-start(f32[2,4,64,2048]{3,2,1,0:T(8,128)} %pad_maximum_fusion.17), channel_id=1, source_target_pairs={{0,16},{4,20},{8,24},{12,28},{16,0},{20,4},{24,8},{28,12},{1,17},{... | collective-permute-start | bytes 12582920 | tf_op jit(solution)/shard_map/ppermute | solution.py:145
  497.9 92.9 %collective-permute-start.46 = (f32[512,2048]{1,0:T(8,128)}, f32[512,2048]{1,0:T(8,128)}, u32[]{:S(2)}, u32[]{:S(2)}) collective-permute-start(f32[512,2048]{1,0:T(8,128)} %broadcast_select_fusion), channel_id=1, source_target_pairs={{0,16},{4,20},{8,24},{12,28},{16,0},{20,4},{24,8},{28,12},{1,17},{... | collective-permute-start | bytes 12582920 | tf_op jit(solution)/shard_map/ppermute | solution.py:145
  521.9 126.0 %collective-permute-start.44 = (f32[4,4,64,2048]{3,2,1,0:T(8,128)}, f32[4,4,64,2048]{3,2,1,0:T(8,128)}, u32[]{:S(2)}, u32[]{:S(2)}) collective-permute-start(f32[4,4,64,2048]{3,2,1,0:T(8,128)} %pad_maximum_fusion.5), channel_id=1, source_target_pairs={{0,4},{4,0},{8,12},{12,8},{16,20},{20,16},{24,28},{28,24},{1,5},{5... | collective-permute-start | bytes 25165832 | tf_op jit(solution)/shard_map/ppermute | solution.py:145
  593.8 47.3 %collective-permute-start.47 = (f32[512,2048]{1,0:T(8,128)S(1)}, f32[512,2048]{1,0:T(8,128)}, u32[]{:S(2)}, u32[]{:S(2)}) collective-permute-start(f32[512,2048]{1,0:T(8,128)S(1)} %broadcast_select_fusion.1), channel_id=1, source_target_pairs={{0,4},{4,0},{8,12},{12,8},{16,20},{20,16},{24,28},{28,24},{1,5},{5... | collective-permute-start | bytes 12582920 | tf_op jit(solution)/shard_map/ppermute | solution.py:145
  (71 other events, 1340.1 us)

commit v2 on v1

v2 whole, which is shorter than its diff:
```python
import functools

import jax
import jax.numpy as jnp
from jax import lax
from jax.experimental import pallas as pl
from jax.experimental.pallas import tpu as pltpu
from jax.sharding import PartitionSpec as P

PANELS = 2
BLOCK = 128
GROUP = 8


def factor_block(block):
    group_count = BLOCK // GROUP
    lane = lax.broadcasted_iota(jnp.int32, (GROUP, BLOCK), 1)
    sub = lax.broadcasted_iota(jnp.int32, (GROUP, BLOCK), 0)
    rows = [block[GROUP * m : GROUP * (m + 1), :] for m in range(group_count)]
    factor = [jnp.zeros((GROUP, BLOCK), jnp.float32) for _ in range(group_count)]
    inverse = []
    for s in range(group_count):
        first = GROUP * s
        columns = {
            m: [
                jnp.broadcast_to(rows[m][:, first + j : first + j + 1], (GROUP, BLOCK))
                for j in range(GROUP)
            ]
            for m in range(s, group_count)
        }
        entry = {
            (k, j): jnp.broadcast_to(columns[s][j][k : k + 1, :], (GROUP, BLOCK))
            for j in range(GROUP)
            for k in range(j, GROUP)
        }
        here = (lane >= first) & (lane < first + GROUP)
        own = jnp.where(here, (lane - first == sub).astype(jnp.float32), rows[s])
        spread = [jnp.broadcast_to(own[k : k + 1, :], (GROUP, BLOCK)) for k in range(GROUP)]
        reciprocal, ratio = [], {}
        for j in range(GROUP):
            reciprocal.append(1.0 / entry[j, j])
            for k in range(j + 1, GROUP):
                ratio[k, j] = entry[k, j] * reciprocal[j]
            for k in range(j + 1, GROUP):
                for i in range(k, GROUP):
                    entry[i, k] = entry[i, k] - entry[i, j] * ratio[k, j]
                spread[k] = spread[k] - ratio[k, j] * spread[j]
        scale = [lax.rsqrt(entry[j, j]) for j in range(GROUP)]
        for m in range(s, group_count):
            piece = columns[m]
            for k in range(GROUP):
                for j in range(k):
                    piece[k] = piece[k] - ratio[k, j] * piece[j]
                factor[m] = jnp.where(lane == first + k, piece[k] * scale[k], factor[m])
            if m > s:
                parts = [piece[k] * reciprocal[k] * spread[k] for k in range(GROUP)]
                while len(parts) > 1:
                    parts = [parts[i] + parts[i + 1] for i in range(0, len(parts), 2)]
                rows[m] = jnp.where(here, 0.0, rows[m]) - parts[0]
        done = jnp.zeros((GROUP, BLOCK), jnp.float32)
        for k in range(GROUP):
            done = jnp.where(sub == k, spread[k] * scale[k], done)
        inverse.append(jnp.where(lane <= first + sub, done, 0.0))
        factor[s] = jnp.where(lane <= first + sub, factor[s], 0.0)
    return jnp.concatenate(factor, 0), jnp.concatenate(inverse, 0)


def exact_dot(left, right, dims):
    return lax.dot_general(
        left, right, (dims, ((), ())),
        precision=lax.Precision.HIGHEST, preferred_element_type=jnp.float32,
    )


def split(value):
    high = value.astype(jnp.bfloat16)
    return high, (value - high.astype(jnp.float32)).astype(jnp.bfloat16)


NT = ((1,), (1,))
NN = ((1,), (0,))


def dot3(left, right, dims):
    def one(a, b):
        return lax.dot_general(a, b, (dims, ((), ())), preferred_element_type=jnp.float32)

    return one(left[0], right[0]) + (one(left[0], right[1]) + one(left[1], right[0]))


def columns_of(pair, start, stop):
    return pair[0][:, start:stop], pair[1][:, start:stop]


def collect(held_ref, chosen, out_ref, tile_pos, order, sems):
    count, rows = held_ref.shape[0], held_ref.shape[2]
    copies = []
    for i in range(count):
        place = 0
        if count > 1:
            apart = i ^ tile_pos
            for p, bit in enumerate(order):
                place = place + ((apart // bit) % 2) * 2**p
        copies.append(
            pltpu.make_async_copy(
                held_ref.at[place, chosen], out_ref.at[pl.ds(i * rows, rows), :], sems.at[i]
            )
        )
    return copies


def tile_kernel(index, first, last, order, waits, *refs):
    refs = list(refs)
    begin = first == 0
    if begin:
        info_ref, held_ref = refs.pop(0), refs.pop(0)
    else:
        state = [refs.pop(0) for _ in range(3)]
    done_refs = [(refs.pop(0), refs.pop(0)) for _ in range(index)]
    del refs[:waits]
    l_ref, w_ref, s_ref, high_ref, low_ref, token_ref = refs[:6]
    token_ref[0, 0] = 0.0
    rows = s_ref.shape[0]
    count = rows // BLOCK
    lead = index * rows
    row = lax.broadcasted_iota(jnp.int32, (BLOCK, BLOCK), 0)
    col = lax.broadcasted_iota(jnp.int32, (BLOCK, BLOCK), 1)
    if begin:
        t_ref, sems = refs[6:]
        copies = collect(held_ref, 0, t_ref, info_ref[0], order, sems)
        for copy in copies:
            copy.start()
        l_ref[:, lead:] = jnp.zeros((rows, rows), jnp.float32)
        w_ref[...] = jnp.zeros_like(w_ref)
        for copy in copies:
            copy.wait()
        diag = t_ref[:, lead:]
        if index:
            given = split(t_ref[:, :lead])
            for j in range(index):
                end = (j + 1) * rows
                pair = done_refs[j][0][...], done_refs[j][1][...]
                l_ref[:, j * rows : end] = dot3(columns_of(given, 0, end), pair, NT)
            solved = split(l_ref[:, :lead])
            diag = diag - dot3(solved, solved, NT)
        for i in range(count):
            for j in range(i + 1):
                tile = diag[i * BLOCK : (i + 1) * BLOCK, j * BLOCK : (j + 1) * BLOCK]
                flipped = tile.T
                if i == j:
                    tile = jnp.where(row >= col, tile, flipped)
                else:
                    s_ref[j * BLOCK : (j + 1) * BLOCK, i * BLOCK : (i + 1) * BLOCK] = flipped
                s_ref[i * BLOCK : (i + 1) * BLOCK, j * BLOCK : (j + 1) * BLOCK] = tile
    else:
        for source, target in zip(state, (l_ref, w_ref, s_ref)):
            target[...] = source[...]
    lane = lax.broadcasted_iota(jnp.int32, (BLOCK, rows), 1)

    def step(b, carry):
        start = pl.multiple_of(b * BLOCK, BLOCK)
        own = pl.ds(start, BLOCK)
        own_l = pl.ds(pl.multiple_of(lead + b * BLOCK, BLOCK), BLOCK)
        lower, inverse = factor_block(s_ref[own, own])
        l_ref[own, own_l] = lower
        s_ref[own, own] = (row == col).astype(jnp.float32)
        strip = exact_dot(inverse, s_ref[own, :], NN)
        w_ref[own, :] = jnp.where(lane < start + BLOCK, strip, 0.0)

        def below(m, carry):
            these = pl.ds(pl.multiple_of(m * BLOCK, BLOCK), BLOCK)
            solved = exact_dot(s_ref[these, own], inverse, NT)
            l_ref[these, own_l] = solved
            s_ref[these, own] = jnp.zeros((BLOCK, BLOCK), jnp.float32)
            s_ref[these, :] = s_ref[these, :] - exact_dot(solved, strip, NN)
            return carry

        return lax.fori_loop(b + 1, count, below, carry)

    lax.fori_loop(first, last, step, 0)
    if last == count:
        inverse = split(w_ref[...])
        high_ref[:, lead:], low_ref[:, lead:] = inverse
        if index:
            solved = split(l_ref[:, :lead])
            for k in range(index):
                total = None
                for j in range(k, index):
                    pair = columns_of(done_refs[j], k * rows, (k + 1) * rows)
                    term = dot3(columns_of(solved, j * rows, (j + 1) * rows), pair, NN)
                    total = term if total is None else total + term
                cross = split(-dot3(inverse, split(total), NN))
                here = slice(k * rows, (k + 1) * rows)
                high_ref[:, here], low_ref[:, here] = cross


VMEM = pl.BlockSpec(memory_space=pltpu.VMEM)
SMEM = pl.BlockSpec(memory_space=pltpu.SMEM)
ANY = pl.BlockSpec(memory_space=pl.ANY)


def limit(size=60):
    return pltpu.CompilerParams(vmem_limit_bytes=size * 2**20)


def cost(flops):
    return pl.CostEstimate(flops=flops, transcendentals=0, bytes_accessed=2**20)


TOKEN = jax.ShapeDtypeStruct((1, 1), jnp.float32)


def tile_part(index, first, last, rows, order, info, held, state, done, waits):
    flat = jax.ShapeDtypeStruct((rows, rows), jnp.float32)
    wide = jax.ShapeDtypeStruct((rows, (index + 1) * rows), jnp.float32)
    half = jax.ShapeDtypeStruct((rows, (index + 1) * rows), jnp.bfloat16)
    begin = first == 0
    given = [info, held] if begin else list(state)
    pairs = [part for pair in done for part in pair]
    return pl.pallas_call(
        functools.partial(tile_kernel, index, first, last, order, len(waits)),
        out_shape=[wide, flat, flat, half, half, TOKEN],
        in_specs=([SMEM, ANY] if begin else [VMEM] * 3) + [VMEM] * len(pairs) + [ANY] * len(waits),
        out_specs=[VMEM] * 5 + [SMEM],
        scratch_shapes=[
            pltpu.VMEM((rows, (index + 1) * rows), jnp.float32),
            pltpu.SemaphoreType.DMA((held.shape[0],)),
        ] if begin else [],
        compiler_params=limit(),
        cost_estimate=cost((last - first) * 8_000_000_000),
    )(*given, *pairs, *waits)


def both_solves(source, width, panel, inverse, solved_ref, scratch_ref, high_ref, low_ref):
    rows = source[0].shape[0]
    steps = len(inverse)
    step = inverse[0][0].shape[0]
    for j in range(steps):
        pair = inverse[j][0][...], inverse[j][1][...]
        scratch_ref[:, j * step : (j + 1) * step] = dot3(
            columns_of(source, 0, (j + 1) * step), pair, NT
        )
    solved_ref[...] = jnp.where(panel == 0, scratch_ref[:, :width], scratch_ref[:, width:])
    solved = split(scratch_ref[...])
    for k in range(steps):
        total = None
        for j in range(k, steps):
            pair = columns_of(inverse[j], k * step, (k + 1) * step)
            term = dot3(columns_of(solved, j * step, (j + 1) * step), pair, NN)
            total = term if total is None else total + term
        here = slice(k * step, (k + 1) * step)
        high_ref[:, here], low_ref[:, here] = split(total)


def below_kernel(steps, info_ref, *refs):
    refs = list(refs)
    held = [(refs.pop(0), refs.pop(0)) for _ in range(CHUNKS)]
    inverse = [(refs.pop(0), refs.pop(0)) for _ in range(steps)]
    solved_ref, high_ref, low_ref, token_ref, scratch_ref = refs
    token_ref[0, 0] = 0.0
    width = solved_ref.shape[1]
    chunk = width // CHUNKS
    even = info_ref[1] % 2 == 0
    for k, (own, other) in enumerate(held):
        for panel in range(PANELS):
            start = panel * width + k * chunk
            pick = even if panel == 0 else jnp.logical_not(even)
            scratch_ref[:, start : start + chunk] = jnp.where(pick, own[...], other[...])
    both_solves(
        split(scratch_ref[...]), width, info_ref[1], inverse, solved_ref, scratch_ref, high_ref, low_ref
    )


def side_kernel(orders, steps, sizes, info_ref, *refs):
    refs = list(refs)
    held = [refs.pop(0) for _ in sizes]
    inverse = [(refs.pop(0), refs.pop(0)) for _ in range(steps)]
    solved_ref, high_ref, low_ref, token_ref, scratch_ref, sems = refs
    token_ref[0, 0] = 0.0
    tile_pos = info_ref[0]
    own = jnp.maximum(tile_pos - steps, 0)
    start = 0
    for ref, size, order in zip(held, sizes, orders):
        @pl.when((own >= start) & (own < start + size))
        def _(ref=ref, start=start, order=order):
            copies = collect(ref, own - start, scratch_ref, tile_pos, order, sems)
            for copy in copies:
                copy.start()
            for copy in copies:
                copy.wait()
        start += size
    both_solves(
        split(scratch_ref[...]), solved_ref.shape[1], info_ref[1], inverse, solved_ref, scratch_ref, high_ref, low_ref
    )


def change_kernel(orders, steps, sizes, info_ref, *refs):
    refs = list(refs)
    held = [refs.pop(0) for _ in sizes]
    factor = [refs.pop(0) for _ in range(steps)]
    below, side = refs[:3], refs[3:6]
    front_below_ref, front_diag_ref, below_ref, diag_ref, token_ref, match_ref, sems = refs[6:]
    token_ref[0, 0] = 0.0
    tile_pos, col_pos = info_ref[0], info_ref[1]
    rows, width = below_ref.shape

    @pl.when(col_pos < PANELS)
    def _():
        below_ref[...] = below[0][...]

    @pl.when(col_pos >= PANELS)
    def _():
        start = 0
        for ref, size, order in zip(held, sizes, orders):
            for n in range(size):
                @pl.when((start + n + steps) // 2 == col_pos)
                def _(ref=ref, n=n, at=start + n, order=order):
                    half = match_ref.at[pl.ds((at % 2) * rows, rows), :]
                    copies = collect(ref, n, half, tile_pos, order, sems)
                    for copy in copies:
                        copy.start()
                    for copy in copies:
                        copy.wait()
            start += size
        for part in range(width // rows):
            here = slice(part * rows, (part + 1) * rows)
            match = split(match_ref[here, :])
            pair = below[1][...], below[2][...]
            below_ref[:, here] = front_below_ref[:, here] - dot3(pair, match, NT)

            @pl.when(tile_pos // 2 >= col_pos)
            def _():
                pair = side[1][...], side[2][...]
                diag_ref[:, here] = front_diag_ref[:, here] - dot3(pair, match, NT)

    @pl.when((col_pos < PANELS) & (tile_pos >= steps))
    def _():
        diag_ref[...] = side[0][...]

    for i in range(steps):
        size = (i + 1) * rows
        for panel in range(PANELS):
            @pl.when((tile_pos == i) & (col_pos == panel))
            def _(i=i, panel=panel, size=size):
                for part in range(width // rows):
                    at = panel * width + part * rows
                    here = slice(part * rows, (part + 1) * rows)
                    if at < size:
                        diag_ref[:, here] = factor[i][:, at : at + rows]

    row = lax.broadcasted_iota(jnp.int32, (rows, width), 0) + tile_pos * rows
    col = lax.broadcasted_iota(jnp.int32, (rows, width), 1) + col_pos * width
    diag_ref[...] = jnp.where(row >= col, diag_ref[...], 0.0)


def update_kernel(info_ref, row_ref, col_ref, high_ref, low_ref, *refs):
    held = [(refs[2 * k], refs[2 * k + 1]) for k in range(CHUNKS)]
    ancestor_ref, out_ref, acc_ref = refs[2 * CHUNKS :]
    rows, width = out_ref.shape
    chunk = width // CHUNKS
    even = info_ref[0] % 2 == 0
    for k, (block, other) in enumerate(held):
        for part in range(2):
            pick = even if part == 0 else jnp.logical_not(even)
            here = slice(part * rows, (part + 1) * rows)
            target = split(jnp.where(pick, block[...], other[...]))
            total = None
            for panel in range(PANELS):
                start = panel * width + k * chunk
                term = dot3(
                    (high_ref[:, start : start + chunk], low_ref[:, start : start + chunk]),
                    columns_of(target, panel * chunk, (panel + 1) * chunk),
                    NT,
                )
                total = term if total is None else total + term
            acc_ref[:, here] = total if k == 0 else acc_ref[:, here] + total
    place = lax.broadcasted_iota(jnp.int32, (rows, rows), 0)

    def move(pair, where, left):
        def one(value):
            sides = (where, value) if left else (value, where)
            dims = NN if left else NT
            return lax.dot_general(*sides, (dims, ((), ())), preferred_element_type=jnp.float32)

        return one(pair[0]) + one(pair[1])

    row_move = (row_ref[...] == place).astype(jnp.float32).astype(jnp.bfloat16)
    acc_ref[...] = move(split(acc_ref[...]), row_move, True)
    for part in range(2):
        here = slice(part * rows, (part + 1) * rows)
        col_move = (col_ref[part : part + 1, :] == place).astype(jnp.float32).astype(jnp.bfloat16)
        out_ref[:, here] = ancestor_ref[:, here] - move(split(acc_ref[:, here]), col_move, False)


def exchange(block, bit, tile_count):
    return lax.ppermute(block, "tiles", [(i, i ^ bit) for i in range(tile_count)])


def tile_bits(tile_count):
    bits, bit = [], 2
    while bit < tile_count:
        bits.append(bit)
        bit *= 2
    return bits + [1]


def climb(block, col_pos, col_count, tie, keep=None):
    held = block
    reach = 2
    while reach < col_count:
        pairs = [(at, at + reach) for at in range(reach) if at + reach < col_count]
        held = tie(held)
        other = lax.ppermute(held, "cols", pairs)
        yield [other]
        held = jnp.where(col_pos >= reach, other, held)
        reach *= 2
    held = tie(held)
    other = lax.ppermute(held, "cols", [(at, at ^ 1) for at in range(col_count)])
    if keep is not None:
        keep.extend((held, other))
    yield [other]
    return held, other


def by_panel(pair, col_pos):
    even = col_pos % 2 == 0
    return jnp.where(even, pair[0], pair[1]), jnp.where(even, pair[1], pair[0])


def gather_rows(piece, order, tile_pos, tile_count, tie):
    held = piece[None]
    for bit in order:
        held = tie(held)
        other = exchange(held, bit, tile_count)
        yield [other]
        held = jnp.concatenate((held, other), 0)
    if piece.shape[1] % 8 == 0:
        return held
    place = {}
    for m in range(tile_count):
        place[sum(bit for p, bit in enumerate(order) if m >> p & 1)] = m
    table = jnp.array([place[w] for w in range(tile_count)], jnp.int32)
    return jnp.concatenate(
        [
            lax.dynamic_index_in_dim(held, table[i ^ tile_pos], 0, keepdims=False)
            for i in range(tile_count)
        ],
        1,
    )[None]


def fetch_target(block, order, tile_pos, tile_count, target, tie):
    for bit in order[:-1]:
        block = tie(block)
        other = exchange(block, bit, tile_count)
        yield [other]
        mine = (tile_pos & bit) == ((2 * target) & bit)
        block = jnp.where(mine, block, other)
    block = tie(block)
    other = exchange(block, 1, tile_count)
    yield [other]
    return block, other


class Plan:
    def __init__(self):
        self.streams = []
        self.results = {}
        self.token = None

    def tie(self, value):
        return value if self.token is None else value + self.token[0, 0]

    def add(self, name, stream, windows):
        self.streams.append([name, stream, list(windows)])

    def run(self, window):
        flying = []
        for entry in self.streams:
            name, stream, windows = entry
            while windows and windows[0] <= window:
                windows.pop(0)
                try:
                    flying += next(stream)
                except StopIteration as stop:
                    self.results[name] = stop.value
                    windows.clear()
        return flying

    def advance(self, name, kept, key):
        for entry in self.streams:
            if entry[0] == name:
                while not kept.get(key):
                    next(entry[1])

    def finish(self, name):
        for entry in self.streams:
            if entry[0] == name:
                while name not in self.results:
                    try:
                        next(entry[1])
                    except StopIteration as stop:
                        self.results[name] = stop.value
                entry[2] = []
        return self.results[name]


CHUNKS = 4
PARTS = 2
LEAD_WINDOWS = ([1, 2, 3, 4, 5], [2, 3, 5, 6, 7], [4, 5, 6, 7, 9], [5, 6, 7, 8, 10])
SIDE_WINDOWS = ([6, 7, 8, 9, 11], [7, 8, 10, 11, 13])
BELOW_WINDOWS = ([8, 9, 10, 11, 12], [9, 10, 11, 12, 14], [10, 11, 12, 13, 15], [11, 12, 14, 15, 16])


def shards(tile_count, col_count, front_diag, front_below, ancestor, owner_cols, rel):
    rows, width = front_diag.shape
    lead = PANELS * width
    steps = lead // rows
    tile_pos = lax.axis_index("tiles")
    col_pos = lax.axis_index("cols")
    target = lax.dynamic_slice_in_dim(owner_cols, col_pos, 1)[0]
    info = jnp.stack((tile_pos, col_pos)).astype(jnp.int32)
    bits = tile_bits(tile_count)
    turned = bits[-2::-1] + [1]
    plan = Plan()
    chunk = width // CHUNKS
    own_parts = {}

    def below_stream(k, order):
        block = front_below[:, k * chunk : (k + 1) * chunk]
        own_parts[k] = []
        pair = yield from climb(block, col_pos, col_count, plan.tie, own_parts[k])
        both = jnp.concatenate(by_panel(pair, col_pos), 1)
        return (yield from fetch_target(both, order, tile_pos, tile_count, target, plan.tie))

    for k, windows in enumerate(BELOW_WINDOWS):
        plan.add(("below", k), below_stream(k, turned if k % 2 else bits), windows)
    plan.run(0)
    pieces = lax.all_to_all(
        front_diag.reshape(tile_count, rows // tile_count, width), "tiles", 0, 0, tiled=True
    )

    def lead_stream(i):
        size = (i + 1) * rows
        take = pieces[i : i + 1, :, : min(size, width)]
        pair = yield from climb(take, col_pos, col_count, plan.tie)
        panels = by_panel(pair, col_pos)
        piece = panels[0] if size <= width else jnp.concatenate(panels, 2)[:, :, :size]
        return (yield from gather_rows(piece, bits, tile_pos, tile_count, plan.tie))

    def side_stream(start, stop, order):
        pair = yield from climb(pieces[start:stop], col_pos, col_count, plan.tie)
        piece = jnp.concatenate(by_panel(pair, col_pos), 2)
        return (yield from gather_rows(piece, order, tile_pos, tile_count, plan.tie))

    for i, windows in enumerate(LEAD_WINDOWS):
        plan.add(("lead", i), lead_stream(i), windows)
    middle = steps + (tile_count - steps) // 2
    plan.add(("side", 0), side_stream(steps, middle, bits), SIDE_WINDOWS[0])
    plan.add(("side", 1), side_stream(middle, tile_count, turned), SIDE_WINDOWS[1])
    flying = []
    for window in range(1, 4):
        flying += plan.run(window)
    started = plan.run(4)

    factor_rows, inverse_rows = [], []
    window = 5
    blocks = rows // BLOCK
    cuts = sorted({blocks * p // PARTS for p in range(PARTS + 1)})
    for i in range(steps):
        held = plan.finish(("lead", i))
        state = None
        for first, last in zip(cuts[:-1], cuts[1:]):
            begun = plan.run(window)
            state = tile_part(
                i, first, last, rows, bits, info, held, state and state[:3], inverse_rows, flying
            )
            flying, started = started + begun, []
            plan.token = state[5]
            window += 1
        window = 5 + PARTS * (i + 1)
        factor_rows.append(state[0])
        inverse_rows.append(tuple(state[3:5]))
    for k in range(CHUNKS):
        plan.advance(("below", k), own_parts, k)
    begun = plan.run(window)
    pairs = [part for pair in inverse_rows for part in pair]
    solves = [
        jax.ShapeDtypeStruct((rows, width), jnp.float32),
        jax.ShapeDtypeStruct((rows, lead), jnp.bfloat16),
        jax.ShapeDtypeStruct((rows, lead), jnp.bfloat16),
        TOKEN,
    ]
    wide = pltpu.VMEM((rows, lead), jnp.float32)
    below = pl.pallas_call(
        functools.partial(below_kernel, steps),
        out_shape=solves,
        in_specs=[SMEM] + [VMEM] * (2 * CHUNKS + len(pairs)),
        out_specs=[VMEM] * 3 + [SMEM],
        scratch_shapes=[wide],
        compiler_params=limit(),
        cost_estimate=cost(20_000_000_000),
    )(info, *[part for k in range(CHUNKS) for part in own_parts[k]], *pairs)
    plan.token = below[3]
    plan.run(window + 1)
    sides = [plan.finish(("side", n)) for n in range(2)]
    sems = pltpu.SemaphoreType.DMA((sides[0].shape[0],))
    sizes = (middle - steps, tile_count - middle)
    orders = (bits, turned)
    side = pl.pallas_call(
        functools.partial(side_kernel, orders, steps, sizes),
        out_shape=solves,
        in_specs=[SMEM, ANY, ANY] + [VMEM] * len(pairs),
        out_specs=[VMEM] * 3 + [SMEM],
        scratch_shapes=[wide, sems],
        compiler_params=limit(),
        cost_estimate=cost(20_000_000_000),
    )(info, *sides, *pairs)
    plan.token = side[3]
    plan.run(window + 2)
    flat = jax.ShapeDtypeStruct((rows, width), jnp.float32)
    factor_below, factor_diag, token = pl.pallas_call(
        functools.partial(change_kernel, orders, steps, sizes),
        out_shape=[flat, flat, TOKEN],
        in_specs=[SMEM, ANY, ANY] + [VMEM] * (steps + 8),
        out_specs=[VMEM] * 2 + [SMEM],
        scratch_shapes=[pltpu.VMEM((width, lead), jnp.float32), sems],
        compiler_params=limit(),
        cost_estimate=cost(20_000_000_000),
    )(info, *sides, *factor_rows, *below[:3], *side[:3], front_below, front_diag)
    plan.token = token
    plan.run(window + 3)
    target_parts = [part for k in range(CHUNKS) for part in plan.finish(("below", k))]
    row_places = lax.dynamic_slice_in_dim(rel, tile_pos * rows, rows) - tile_pos * rows
    col_places = lax.dynamic_slice_in_dim(rel, target * width, width).reshape(2, rows)
    col_places = col_places - target * width - jnp.array([[0], [rows]], jnp.int32)
    ancestor_out = pl.pallas_call(
        update_kernel,
        out_shape=flat,
        in_specs=[SMEM] + [VMEM] * (5 + 2 * CHUNKS),
        out_specs=VMEM,
        scratch_shapes=[pltpu.VMEM((rows, width), jnp.float32)],
        compiler_params=limit(),
        cost_estimate=cost(10_000_000_000),
    )(info, row_places[None], col_places, below[1], below[2], *target_parts, ancestor)
    return (factor_diag, factor_below, ancestor_out)


def solution(mesh):
    placed = (P("tiles", "cols"), P("tiles", "cols"), P("tiles", "cols"), P(), P())
    return jax.shard_map(
        functools.partial(shards, mesh.shape["tiles"], mesh.shape["cols"]),
        mesh=mesh,
        in_specs=placed,
        out_specs=(P("tiles", "cols"), P("tiles", "cols"), P("tiles", "cols")),
        check_vma=False,
    )
```

time: 832 us -> 651 us (0.78)
  Pallas kernels: 97.9 us -> 267 us
  matrix products: 157 us -> 0 us
  waiting for transfers between devices: 283 us -> 181 us
  local copies, waits for them, and re-layouts: 68 us -> 6.6 us
  starting transfers between devices: 88.4 us -> 53.6 us
  other arithmetic: 77.7 us -> 104 us
  between operations: 19.1 us -> 3.02 us
    pallas_call x4 -> x12, Pallas kernels: 97.9 us -> 267 us  [the longest x8 173 us: tile_part(): pl.pallas_call(functools.partial(tile_kernel, index, first, last, order,...]
    dot_general x28 -> x0, matrix products: 157 us -> none  [the longest x17 97.8 us: dot_nt(): lax.dot_general(left, right, (((1,), (1,)), ((), ())), precision=lax.Prec...]
    ppermute x18 -> x30, waiting for transfers between devices: 129 us -> 44.8 us  [exchange(): lax.ppermute(block, 'tiles', [(i, i ^ bit) for i in range(tile_count)])]
    add x1 -> x36, other arithmetic: 0.6 us -> 66.1 us  [tie(): return value if self.token is None else value + self.token[0, 0]]
    select_n x9, other arithmetic: 27.8 us -> 4.99 us  [the longest x7 4.94 us: by_panel(): jnp.where(even, pair[0], pair[1])]
    dot_general x9 -> x0, local copies, waits for them, and re-layouts: 21.6 us -> none  [dot_nt(): lax.dot_general(left, right, (((1,), (1,)), ((), ())), precision=lax.Prec...]
    ppermute x30 -> x20, starting transfers between devices: 36.4 us -> 16 us  [the longest x10 13.2 us: climb(): other = lax.ppermute(held, 'cols', pairs)]
    ppermute x30 -> x20, waiting for transfers between devices: 154 us -> 137 us  [the longest x10 107 us: climb(): other = lax.ppermute(held, 'cols', pairs)]
  transfers between devices with their start and end apart: 48 -> 50, of which waited for: 16 -> 16; matrix products, arithmetic and copies ran while one was open for 15% -> 16% of each run, Pallas kernels for 12% -> 39%
where the time goes in v2:
time: 651 us; the launch traced here: 644 us
  Pallas kernels  267 us (41%)
  waiting for transfers between devices  181 us (28%)
  other arithmetic  104 us (16%)
  starting transfers between devices  53.6 us (8%)
  blocking collectives  28.4 us (4%)
  local copies, waits for them, and re-layouts  6.6 us (1%)
    pallas_call x8, Pallas kernels, tile_part(): pl.pallas_call(functools.partial(tile_kernel, index, first, last, order,...  173 us
    ppermute x10, waiting for transfers between devices, climb(): other = lax.ppermute(held, 'cols', pairs)  107 us
    add x36, other arithmetic, tie(): return value if self.token is None else value + self.token[0, 0]  66.1 us
    ppermute x30, waiting for transfers between devices, exchange(): lax.ppermute(block, 'tiles', [(i, i ^ bit) for i in range(tile_count)])  44.8 us
    ppermute x30, starting transfers between devices, exchange(): lax.ppermute(block, 'tiles', [(i, i ^ bit) for i in range(tile_count)])  37.6 us
    ppermute x10, waiting for transfers between devices, climb(): lax.ppermute(held, 'cols', [(at, at ^ 1) for at in range(col_count)])  29.4 us
    pallas_call x1, Pallas kernels, shards(): pl.pallas_call(functools.partial(change_kernel, orders, steps, sizes), ou...  29.3 us
    all_to_all x1, blocking collectives, shards(): lax.all_to_all(front_diag.reshape(tile_count, rows // tile_count, width),...  28.4 us
  transfers between devices with their start and end apart: 50, of which 16 were waited for; matrix products, arithmetic and copies ran while one was open for 16% of the time, Pallas kernels for 39%

profile of v2, /device:TPU:31, one launch (start us, length us, event | category | flops | bytes accessed | tf_op | source)
XLA Modules:
  0.0 643.7 jit_solution(14269434432689440607)
XLA Ops:
  0.6 28.4 %all_to_all.5 = f32[8,64,1024]{2,1,0:T(8,128)S(1)} all-to-all(f32[8,64,1024]{2,1,0:T(8,128)} %bitcast.63), channel_id=1, replica_groups=mesh['tiles'=8,'cols'=4] {'tiles'}, dimensions={0} | all-to-all | bytes 4194304 | tf_op jit(solution)/shard_map/all_to_all | solution.py:539
  30.4 9.6 %collective-permute-done.refs_2_ = f32[1,64,512]{2,1,0:T(8,128)S(1)} collective-permute-done((f32[1,64,512]{2,1,0:T(8,128)S(1)}, f32[1,64,512]{2,1,0:T(8,128)S(1)}, u32[]{:S(2)}, u32[]{:S(2)}) %collective-permute-start) | collective-permute-done | bytes 131104 | tf_op jit(solution)/shard_map/ppermute | solution.py:413
  40.1 4.5 collective-permute-done.1.refs_3_
  44.7 3.8 collective-permute-done.2.refs_5_
  51.3 2.6 collective-permute-done.3.refs_3_
  53.9 3.7 collective-permute-start.4
  57.6 9.0 %collective-permute-done.5.refs_4_ = f32[1,64,1024]{2,1,0:T(8,128)S(1)} collective-permute-done((f32[1,64,1024]{2,1,0:T(8,128)S(1)}, f32[1,64,1024]{2,1,0:T(8,128)S(1)}, u32[]{:S(2)}, u32[]{:S(2)}) %collective-permute-start.5) | collective-permute-done | bytes 262176 | tf_op jit(solution)/shard_map/ppermute | solution.py:413
  69.2 6.8 %collective-permute-done.6.refs_6_ = f32[1,64,1024]{2,1,0:T(8,128)} collective-permute-done((f32[1,64,1024]{2,1,0:T(8,128)S(1)}, f32[1,64,1024]{2,1,0:T(8,128)}, u32[]{:S(2)}, u32[]{:S(2)}) %collective-permute-start.6) | collective-permute-done | bytes 262176 | tf_op jit(solution)/shard_map/ppermute | solution.py:418
  79.2 17.5 %shard_map.85 = (f32[512,512]{1,0:T(8,128)}, f32[512,512]{1,0:T(8,128)}, f32[512,512]{1,0:T(8,128)}, bf16[512,512]{1,0:T(8,128)(2,1)}, bf16[512,512]{1,0:T(8,128)(2,1)}, /*index=5*/f32[1,1]{1,0:T(1,128)}) custom-call(s32[2]{0:T(128)} %pad_add_fusion.refs_0_.info_ref, f32[8,1,64,512]{3,2,1,0:T(8,128)} %pad_maximum_fusion.2.refs_1_, f32[1,64,512]{2,1,0:T(8,128)} %copy-done.29, ...), custom_call_target="tpu_custom_call" | custom-call | flops 16000000000 | bytes 1048576 | tf_op jit(solution)/shard_map/pallas_call | solution.py:220
  101.4 11.5 %collective-permute-done.8.refs_4_ = f32[1,64,1024]{2,1,0:T(8,128)S(1)} collective-permute-done((f32[1,64,1024]{2,1,0:T(8,128)S(1)}, f32[1,64,1024]{2,1,0:T(8,128)S(1)}, u32[]{:S(2)}, u32[]{:S(2)}) %collective-permute-start.8) | collective-permute-done | bytes 262176 | tf_op jit(solution)/shard_map/ppermute | solution.py:413
  114.3 6.0 collective-permute-done.10.refs_6_
  121.0 14.9 %shard_map.86 = (f32[512,512]{1,0:T(8,128)}, f32[512,512]{1,0:T(8,128)}, f32[512,512]{1,0:T(8,128)}, bf16[512,512]{1,0:T(8,128)(2,1)}, bf16[512,512]{1,0:T(8,128)(2,1)}, /*index=5*/f32[1,1]{1,0:T(1,128)}) custom-call(f32[512,512]{1,0:T(8,128)} %get-tuple-element.47.refs_0_, f32[512,512]{1,0:T(8,128)} %get-tuple-element.48.refs_1_, ...), custom_call_target="tpu_custom_call" | custom-call | flops 16000000000 | bytes 1048576 | tf_op jit(solution)/shard_map/pallas_call | solution.py:220
  135.9 2.1 slice_add_fusion
  144.7 21.1 %collective-permute-done.7.refs_7_ = f32[2,64,1024]{2,1,0:T(8,128)S(1)} collective-permute-done((f32[2,64,1024]{2,1,0:T(8,128)S(1)}, f32[2,64,1024]{2,1,0:T(8,128)S(1)}, u32[]{:S(2)}, u32[]{:S(2)}) %collective-permute-start.7) | collective-permute-done | bytes 524320 | tf_op jit(solution)/shard_map/ppermute | solution.py:413
  172.7 12.0 %collective-permute-done.12.refs_7_ = f32[2,64,1024]{2,1,0:T(8,128)S(1)} collective-permute-done((f32[2,64,1024]{2,1,0:T(8,128)S(1)}, f32[2,64,1024]{2,1,0:T(8,128)S(1)}, u32[]{:S(2)}, u32[]{:S(2)}) %collective-permute-start.12) | collective-permute-done | bytes 524320 | tf_op jit(solution)/shard_map/ppermute | solution.py:418
  187.0 21.2 %shard_map.87 = (f32[512,1024]{1,0:T(8,128)}, f32[512,512]{1,0:T(8,128)}, f32[512,512]{1,0:T(8,128)}, bf16[512,1024]{1,0:T(8,128)(2,1)}, bf16[512,1024]{1,0:T(8,128)(2,1)}, /*index=5*/f32[1,1]{1,0:T(1,128)}) custom-call(s32[2]{0:T(128)} %pad_add_fusion.refs_0_.info_ref, f32[8,1,64,1024]{3,2,1,0:T(8,128)} %maximum_bitcast_fusion.2.refs_1_, ...), custom_call_target="tpu_custom_call" | custom-call | flops 16000000000 | bytes 1048576 | tf_op jit(solution)/shard_map/pallas_call | solution.py:220
  208.9 2.9 collective-permute-start.17
  214.4 16.8 %shard_map.88 = (f32[512,1024]{1,0:T(8,128)}, f32[512,512]{1,0:T(8,128)}, f32[512,512]{1,0:T(8,128)}, bf16[512,1024]{1,0:T(8,128)(2,1)}, bf16[512,1024]{1,0:T(8,128)(2,1)}, /*index=5*/f32[1,1]{1,0:T(1,128)}) custom-call(f32[512,1024]{1,0:T(8,128)} %get-tuple-element.54.refs_0_, f32[512,512]{1,0:T(8,128)} %get-tuple-element.55.refs_1_, ...), custom_call_target="tpu_custom_call" | custom-call | flops 16000000000 | bytes 1048576 | tf_op jit(solution)/shard_map/pallas_call | solution.py:220
  231.2 2.1 maximum_add_fusion.5
  236.0 2.2 slice_add_fusion.4
  242.7 33.9 %collective-permute-done.23.refs_6_ = f32[512,256]{1,0:T(8,128)S(1)} collective-permute-done((f32[512,256]{1,0:T(8,128)S(1)}, f32[512,256]{1,0:T(8,128)S(1)}, u32[]{:S(2)}, u32[]{:S(2)}) %collective-permute-start.23) | collective-permute-done | bytes 524320 | tf_op jit(solution)/shard_map/ppermute | solution.py:413
  278.2 3.4 maximum_add_fusion.2
  284.7 24.9 %shard_map.89 = (f32[512,1536]{1,0:T(8,128)}, f32[512,512]{1,0:T(8,128)}, f32[512,512]{1,0:T(8,128)}, bf16[512,1536]{1,0:T(8,128)(2,1)}, bf16[512,1536]{1,0:T(8,128)(2,1)}, /*index=5*/f32[1,1]{1,0:T(1,128)}) custom-call(s32[2]{0:T(128)} %pad_add_fusion.refs_0_.info_ref, f32[8,1,64,1536]{3,2,1,0:T(8,128)} %maximum_bitcast_fusion.1.refs_1_, ...), custom_call_target="tpu_custom_call" | custom-call | flops 16000000000 | bytes 1048576 | tf_op jit(solution)/shard_map/pallas_call | solution.py:220
  312.8 2.4 collective-permute-start.31
  315.2 2.5 select_add_fusion.10.refs_2_
  319.5 7.7 %collective-permute-done.21.refs_9_ = f32[2,2,64,2048]{3,2,1,0:T(8,128)} collective-permute-done((f32[2,2,64,2048]{3,2,1,0:T(8,128)}, f32[2,2,64,2048]{3,2,1,0:T(8,128)}, u32[]{:S(2)}, u32[]{:S(2)}) %collective-permute-start.21) | collective-permute-done | bytes 2097184 | tf_op jit(solution)/shard_map/ppermute | solution.py:396
  327.2 20.8 %shard_map.90 = (f32[512,1536]{1,0:T(8,128)}, f32[512,512]{1,0:T(8,128)}, f32[512,512]{1,0:T(8,128)}, bf16[512,1536]{1,0:T(8,128)(2,1)}, bf16[512,1536]{1,0:T(8,128)(2,1)}, /*index=5*/f32[1,1]{1,0:T(1,128)}) custom-call(f32[512,1536]{1,0:T(8,128)} %get-tuple-element.60.refs_0_, f32[512,512]{1,0:T(8,128)} %get-tuple-element.61.refs_1_, ...), custom_call_target="tpu_custom_call" | custom-call | flops 16000000000 | bytes 1048576 | tf_op jit(solution)/shard_map/pallas_call | solution.py:220
  348.1 5.5 maximum_add_fusion
  353.6 5.1 collective-permute-start.28
  367.5 3.4 maximum_add_fusion.3
  372.4 14.4 %collective-permute-done.32.refs_8_ = f32[512,512]{1,0:T(8,128)} collective-permute-done((f32[512,512]{1,0:T(8,128)}, f32[512,512]{1,0:T(8,128)}, u32[]{:S(2)}, u32[]{:S(2)}) %collective-permute-start.32) | collective-permute-done | bytes 1048608 | tf_op jit(solution)/shard_map/ppermute | solution.py:396
  386.8 3.1 select_add_fusion.7
  397.1 4.0 maximum_bitcast_fusion.refs_1_
  401.0 20.2 %collective-permute-done.38.refs_12_ = f32[512,256]{1,0:T(8,128)S(1)} collective-permute-done((f32[512,256]{1,0:T(8,128)S(1)}, f32[512,256]{1,0:T(8,128)S(1)}, u32[]{:S(2)}, u32[]{:S(2)}) %collective-permute-start.38) | collective-permute-done | bytes 524320 | tf_op jit(solution)/shard_map/ppermute | solution.py:413
  422.0 30.8 %shard_map.91 = (f32[512,2048]{1,0:T(8,128)}, f32[512,512]{1,0:T(8,128)}, f32[512,512]{1,0:T(8,128)}, bf16[512,2048]{1,0:T(8,128)(2,1)}, bf16[512,2048]{1,0:T(8,128)(2,1)}, /*index=5*/f32[1,1]{1,0:T(1,128)}) custom-call(s32[2]{0:T(128)} %pad_add_fusion.refs_0_.info_ref, f32[8,1,64,2048]{3,2,1,0:T(8,128)} %maximum_bitcast_fusion.refs_1_, ...), custom_call_target="tpu_custom_call" | custom-call | flops 16000000000 | bytes 1048576 | tf_op jit(solution)/shard_map/pallas_call | solution.py:220
  455.0 25.8 %shard_map.92 = (f32[512,2048]{1,0:T(8,128)}, f32[512,512]{1,0:T(8,128)}, f32[512,512]{1,0:T(8,128)}, bf16[512,2048]{1,0:T(8,128)(2,1)}, bf16[512,2048]{1,0:T(8,128)(2,1)}, /*index=5*/f32[1,1]{1,0:T(1,128)}) custom-call(f32[512,2048]{1,0:T(8,128)} %get-tuple-element.67.refs_0_, f32[512,512]{1,0:T(8,128)} %get-tuple-element.68.refs_1_, ...), custom_call_target="tpu_custom_call" | custom-call | flops 16000000000 | bytes 1048576 | tf_op jit(solution)/shard_map/pallas_call | solution.py:220
  480.9 5.4 maximum_add_fusion.1
  487.4 3.1 select_add_fusion.6.refs_0_
  490.4 2.1 select_add_fusion.5
  496.1 24.3 %shard_map.93 = (f32[512,1024]{1,0:T(8,128)}, bf16[512,2048]{1,0:T(8,128)(2,1)}, bf16[512,2048]{1,0:T(8,128)(2,1)}, f32[1,1]{1,0:T(1,128)}) custom-call(s32[2]{0:T(128)} %pad_add_fusion.refs_0_.info_ref, f32[512,256]{1,0:T(8,128)} %select_add_fusion.11.refs_0_, f32[512,256]{1,0:T(8,128)} %collective-permute-done.26.refs_7_.refs_1_, ...), custom_call_target="tpu_custom_call" | custom-call | flops 20000000000 | bytes 1048576 | tf_op jit(solution)/shard_map/pallas_call | solution.py:595
  523.3 16.2 %collective-permute-done.44 = f32[512,512]{1,0:T(8,128)} collective-permute-done((f32[512,512]{1,0:T(8,128)S(1)}, f32[512,512]{1,0:T(8,128)}, u32[]{:S(2)}, u32[]{:S(2)}) %collective-permute-start.44) | collective-permute-done | bytes 1048608 | tf_op jit(solution)/shard_map/ppermute | solution.py:396
  542.7 7.9 %pad_maximum_fusion.refs_0_ = f32[8,2,64,2048]{3,2,1,0:T(8,128)} fusion(f32[4,2,64,2048]{3,2,1,0:T(8,128)} %collective-permute-done.28.refs_13_, f32[4,2,64,2048]{3,2,1,0:T(8,128)} %maximum_add_fusion), kind=kLoop, calls=%fused_computation | loop fusion | flops 2097152 | bytes 16777216 | tf_op jit(solution)/shard_map/concatenate | solution.py:436
  550.6 7.9 %pad_maximum_fusion.1.refs_1_ = f32[8,2,64,2048]{3,2,1,0:T(8,128)} fusion(f32[4,2,64,2048]{3,2,1,0:T(8,128)} %collective-permute-done.39, f32[4,2,64,2048]{3,2,1,0:T(8,128)} %maximum_add_fusion.1), kind=kLoop, calls=%fused_computation.1 | loop fusion | flops 2097152 | bytes 16777216 | tf_op jit(solution)/shard_map/concatenate | solution.py:436
  558.5 25.3 %shard_map.94 = (f32[512,1024]{1,0:T(8,128)}, bf16[512,2048]{1,0:T(8,128)(2,1)}, bf16[512,2048]{1,0:T(8,128)(2,1)}, f32[1,1]{1,0:T(1,128)}) custom-call(s32[2]{0:T(128)} %pad_add_fusion.refs_0_.info_ref, f32[8,2,64,2048]{3,2,1,0:T(8,128)} %pad_maximum_fusion.refs_0_, f32[8,2,64,2048]{3,2,1,0:T(8,128)} %pad_maximum_fusion.1.refs_1_, ...), custom_call_target="tpu_custom_call" | custom-call | flops 20000000000 | bytes 1048576 | tf_op jit(solution)/shard_map/pallas_call | solution.py:610
  583.8 2.1 select_add_fusion.2.refs_4_
  587.8 2.1 select_add_fusion.1
  591.3 29.3 %shard_map.95 = (f32[512,1024]{1,0:T(8,128)}, f32[512,1024]{1,0:T(8,128)}, f32[1,1]{1,0:T(1,128)}) custom-call(s32[2]{0:T(128)} %pad_add_fusion.refs_0_.info_ref, f32[8,2,64,2048]{3,2,1,0:T(8,128)} %pad_maximum_fusion.refs_0_, f32[8,2,64,2048]{3,2,1,0:T(8,128)} %pad_maximum_fusion.1.refs_1_, f32[512,512]{1,0:T(8,128)} %get-tuple-element.71.refs_2_, ...), custom_call_target="tpu_custom_call" | custom-call | flops 20000000000 | bytes 1048576 | tf_op jit(solution)/shard_map/pallas_call | solution.py:622
  627.9 15.6 %shard_map.96 = f32[512,1024]{1,0:T(8,128)} custom-call(s32[2]{0:T(128)} %pad_add_fusion.refs_0_.info_ref, s32[1,512]{1,0:T(1,128)} %bitcast.68, s32[2,512]{1,0:T(2,128)} %broadcast_subtract_fusion.col_ref, bf16[512,2048]{1,0:T(8,128)(2,1)} %get-tuple-element.79.refs_7_.high_ref, bf16[512,2048]{1,0:T(8,128)(2,1)} %get-tuple-element.80.refs_8_.low_ref, ...), custom_call_target="tpu_custom_call" | custom-call | flops 10000000000 | bytes 1048576 | tf_op jit(solution)/shard_map/pallas_call | solution.py:637
  (200 shorter events, 92.8 us)
Async XLA Ops:
  29.0 10.9 %collective-permute-start = (f32[1,64,512]{2,1,0:T(8,128)S(1)}, f32[1,64,512]{2,1,0:T(8,128)S(1)}, u32[]{:S(2)}, u32[]{:S(2)}) collective-permute-start(f32[1,64,512]{2,1,0:T(8,128)S(1)} %slice.45), channel_id=1, source_target_pairs={{0,2},{1,3},{4,6},{5,7},{8,10},{9,11},{12,14},{13,15},{16,18},{17,... | collective-permute-start | bytes 393224 | tf_op jit(solution)/shard_map/ppermute | solution.py:413
  40.0 4.6 collective-permute-start.1
  48.6 5.3 collective-permute-start.3
  50.0 16.6 %collective-permute-start.5 = (f32[1,64,1024]{2,1,0:T(8,128)S(1)}, f32[1,64,1024]{2,1,0:T(8,128)S(1)}, u32[]{:S(2)}, u32[]{:S(2)}) collective-permute-start(f32[1,64,1024]{2,1,0:T(8,128)S(1)} %slice.46), channel_id=1, source_target_pairs={{0,2},{1,3},{4,6},{5,7},{8,10},{9,11},{12,14},{13,15},{16,18},{17,... | collective-permute-start | bytes 786440 | tf_op jit(solution)/shard_map/ppermute | solution.py:413
  53.9 23.2 %collective-permute-start.4 = (f32[4,1,64,512]{3,2,1,0:T(8,128)S(1)}, f32[4,1,64,512]{3,2,1,0:T(8,128)}, u32[]{:S(2)}, u32[]{:S(2)}) collective-permute-start(f32[4,1,64,512]{3,2,1,0:T(8,128)S(1)} %pad_maximum_fusion.3), channel_id=1, source_target_pairs={{0,4},{4,0},{8,12},{12,8},{16,20},{20,16},{24,28},{28,24},{1,5},{5... | collective-permute-start | bytes 1572872 | tf_op jit(solution)/shard_map/ppermute | solution.py:396
  67.4 8.7 %collective-permute-start.6 = (f32[1,64,1024]{2,1,0:T(8,128)S(1)}, f32[1,64,1024]{2,1,0:T(8,128)}, u32[]{:S(2)}, u32[]{:S(2)}) collective-permute-start(f32[1,64,1024]{2,1,0:T(8,128)S(1)} %get-tuple-element.98), channel_id=1, source_target_pairs={{0,1},{1,0},{2,3},{3,2},{4,5},{5,4},{6,7},{7,6},{8,9},{9,8},{10,11... | collective-permute-start | bytes 786440 | tf_op jit(solution)/shard_map/ppermute | solution.py:418
  67.9 28.8 %collective-permute-start.11 = (f32[1,64,1024]{2,1,0:T(8,128)}, f32[1,64,1024]{2,1,0:T(8,128)}, u32[]{:S(2)}, u32[]{:S(2)}) collective-permute-start(f32[1,64,1024]{2,1,0:T(8,128)} %get-tuple-element.97), channel_id=1, source_target_pairs={{0,2},{1,3},{4,6},{5,7},{8,10},{9,11},{12,14},{13,15},{16,18},{17,... | collective-permute-start | bytes 786440 | tf_op jit(solution)/shard_map/ppermute | solution.py:413
  77.0 22.8 %collective-permute-start.9 = (f32[1,1,64,1024]{3,2,0,1:T(8,128)S(1)}, f32[1,1,64,1024]{3,2,0,1:T(8,128)S(1)}, u32[]{:S(2)}, u32[]{:S(2)}) collective-permute-start(f32[1,1,64,1024]{3,2,0,1:T(8,128)S(1)} %bitcast.59), channel_id=1, source_target_pairs={{0,8},{4,12},{8,0},{12,4},{16,24},{20,28},{24,16},{28,20},{1,9},{5... | collective-permute-start | bytes 786440 | tf_op jit(solution)/shard_map/ppermute | solution.py:396
  98.3 14.6 %collective-permute-start.8 = (f32[1,64,1024]{2,1,0:T(8,128)S(1)}, f32[1,64,1024]{2,1,0:T(8,128)S(1)}, u32[]{:S(2)}, u32[]{:S(2)}) collective-permute-start(f32[1,64,1024]{2,1,0:T(8,128)S(1)} %get-tuple-element.96), channel_id=1, source_target_pairs={{0,2},{1,3},{4,6},{5,7},{8,10},{9,11},{12,14},{13,15},{16,18},{17,... | collective-permute-start | bytes 786440 | tf_op jit(solution)/shard_map/ppermute | solution.py:413
  101.2 38.1 %collective-permute-start.13 = (f32[2,1,64,1024]{3,2,0,1:T(8,128)}, f32[2,1,64,1024]{3,2,0,1:T(8,128)}, u32[]{:S(2)}, u32[]{:S(2)}) collective-permute-start(f32[2,1,64,1024]{3,2,0,1:T(8,128)} %maximum_add_fusion.18), channel_id=1, source_target_pairs={{0,16},{4,20},{8,24},{12,28},{16,0},{20,4},{24,8},{28,12},{1,17},{... | collective-permute-start | bytes 1572872 | tf_op jit(solution)/shard_map/ppermute | solution.py:396
  101.4 12.8 %collective-permute-start.16 = (f32[1,64,1024]{2,1,0:T(8,128)S(1)}, f32[1,64,1024]{2,1,0:T(8,128)S(1)}, u32[]{:S(2)}, u32[]{:S(2)}) collective-permute-start(f32[1,64,1024]{2,1,0:T(8,128)S(1)} %get-tuple-element.95), channel_id=1, source_target_pairs={{0,1},{1,0},{2,3},{3,2},{4,5},{5,4},{6,7},{7,6},{8,9},{9,8},{10,11... | collective-permute-start | bytes 786440 | tf_op jit(solution)/shard_map/ppermute | solution.py:418
  112.9 7.4 %collective-permute-start.10 = (f32[1,64,1024]{2,1,0:T(8,128)S(1)}, f32[1,64,1024]{2,1,0:T(8,128)S(1)}, u32[]{:S(2)}, u32[]{:S(2)}) collective-permute-start(f32[1,64,1024]{2,1,0:T(8,128)S(1)} %broadcast_select_fusion.13), channel_id=1, source_target_pairs={{0,1},{1,0},{2,3},{3,2},{4,5},{5,4},{6,7},{7,6},{8,9},{9,8},{10,11... | collective-permute-start | bytes 786440 | tf_op jit(solution)/shard_map/ppermute | solution.py:418
  138.0 27.8 %collective-permute-start.7 = (f32[2,64,1024]{2,1,0:T(8,128)S(1)}, f32[2,64,1024]{2,1,0:T(8,128)S(1)}, u32[]{:S(2)}, u32[]{:S(2)}) collective-permute-start(f32[2,64,1024]{2,1,0:T(8,128)S(1)} %get-tuple-element.94), channel_id=1, source_target_pairs={{0,2},{1,3},{4,6},{5,7},{8,10},{9,11},{12,14},{13,15},{16,18},{17,... | collective-permute-start | bytes 1572872 | tf_op jit(solution)/shard_map/ppermute | solution.py:413
  141.1 44.4 %collective-permute-start.14 = (f32[4,1,64,1024]{3,2,0,1:T(8,128)S(1)}, f32[4,1,64,1024]{3,2,0,1:T(8,128)S(1)}, u32[]{:S(2)}, u32[]{:S(2)}) collective-permute-start(f32[4,1,64,1024]{3,2,0,1:T(8,128)S(1)} %maximum_add_fusion.7), channel_id=1, source_target_pairs={{0,4},{4,0},{8,12},{12,8},{16,20},{20,16},{24,28},{28,24},{1,5},{5... | collective-permute-start | bytes 3145736 | tf_op jit(solution)/shard_map/ppermute | solution.py:396
  143.2 26.9 %collective-permute-start.15 = (f32[1,1,64,1536]{3,2,0,1:T(8,128)S(1)}, f32[1,1,64,1536]{3,2,0,1:T(8,128)S(1)}, u32[]{:S(2)}, u32[]{:S(2)}) collective-permute-start(f32[1,1,64,1536]{3,2,0,1:T(8,128)S(1)} %bitcast.57), channel_id=1, source_target_pairs={{0,8},{4,12},{8,0},{12,4},{16,24},{20,28},{24,16},{28,20},{1,9},{5... | collective-permute-start | bytes 1179656 | tf_op jit(solution)/shard_map/ppermute | solution.py:396
  166.5 18.2 %collective-permute-start.12 = (f32[2,64,1024]{2,1,0:T(8,128)S(1)}, f32[2,64,1024]{2,1,0:T(8,128)S(1)}, u32[]{:S(2)}, u32[]{:S(2)}) collective-permute-start(f32[2,64,1024]{2,1,0:T(8,128)S(1)} %select_add_fusion.13), channel_id=1, source_target_pairs={{0,1},{1,0},{2,3},{3,2},{4,5},{5,4},{6,7},{7,6},{8,9},{9,8},{10,11... | collective-permute-start | bytes 1572872 | tf_op jit(solution)/shard_map/ppermute | solution.py:418
  167.3 46.3 %collective-permute-start.19 = (f32[1,1,64,2048]{3,2,0,1:T(8,128)S(1)}, f32[1,1,64,2048]{3,2,0,1:T(8,128)S(1)}, u32[]{:S(2)}, u32[]{:S(2)}) collective-permute-start(f32[1,1,64,2048]{3,2,0,1:T(8,128)S(1)} %bitcast.55), channel_id=1, source_target_pairs={{0,8},{4,12},{8,0},{12,4},{16,24},{20,28},{24,16},{28,20},{1,9},{5... | collective-permute-start | bytes 1572872 | tf_op jit(solution)/shard_map/ppermute | solution.py:396
  168.8 43.0 %collective-permute-start.20 = (f32[2,64,1024]{2,1,0:T(8,128)}, f32[2,64,1024]{2,1,0:T(8,128)}, u32[]{:S(2)}, u32[]{:S(2)}) collective-permute-start(f32[2,64,1024]{2,1,0:T(8,128)} %get-tuple-element.93), channel_id=1, source_target_pairs={{0,2},{1,3},{4,6},{5,7},{8,10},{9,11},{12,14},{13,15},{16,18},{17,... | collective-permute-start | bytes 1572872 | tf_op jit(solution)/shard_map/ppermute | solution.py:413
  171.7 41.9 %collective-permute-start.18 = (f32[2,1,64,1536]{3,2,0,1:T(8,128)}, f32[2,1,64,1536]{3,2,0,1:T(8,128)}, u32[]{:S(2)}, u32[]{:S(2)}) collective-permute-start(f32[2,1,64,1536]{3,2,0,1:T(8,128)} %maximum_add_fusion.15), channel_id=1, source_target_pairs={{0,16},{4,20},{8,24},{12,28},{16,0},{20,4},{24,8},{28,12},{1,17},{... | collective-permute-start | bytes 2359304 | tf_op jit(solution)/shard_map/ppermute | solution.py:396
  208.9 69.3 %collective-permute-start.17 = (f32[1,2,64,2048]{3,2,1,0:T(8,128)S(1)}, f32[1,2,64,2048]{3,2,1,0:T(8,128)}, u32[]{:S(2)}, u32[]{:S(2)}) collective-permute-start(f32[1,2,64,2048]{3,2,1,0:T(8,128)S(1)} %maximum_add_fusion.6), channel_id=1, source_target_pairs={{0,8},{4,12},{8,0},{12,4},{16,24},{20,28},{24,16},{28,20},{1,9},{5... | collective-permute-start | bytes 3145736 | tf_op jit(solution)/shard_map/ppermute | solution.py:396
  213.6 27.6 %collective-permute-start.25 = (f32[2,64,1024]{2,1,0:T(8,128)S(1)}, f32[2,64,1024]{2,1,0:T(8,128)S(1)}, u32[]{:S(2)}, u32[]{:S(2)}) collective-permute-start(f32[2,64,1024]{2,1,0:T(8,128)S(1)} %select_add_fusion.12), channel_id=1, source_target_pairs={{0,1},{1,0},{2,3},{3,2},{4,5},{5,4},{6,7},{7,6},{8,9},{9,8},{10,11... | collective-permute-start | bytes 1572872 | tf_op jit(solution)/shard_map/ppermute | solution.py:418
  233.3 49.5 %collective-permute-start.22 = (f32[4,1,64,1536]{3,2,0,1:T(8,128)S(1)}, f32[4,1,64,1536]{3,2,0,1:T(8,128)S(1)}, u32[]{:S(2)}, u32[]{:S(2)}) collective-permute-start(f32[4,1,64,1536]{3,2,0,1:T(8,128)S(1)} %maximum_add_fusion.5), channel_id=1, source_target_pairs={{0,4},{4,0},{8,12},{12,8},{16,20},{20,16},{24,28},{28,24},{1,5},{5... | collective-permute-start | bytes 4718600 | tf_op jit(solution)/shard_map/ppermute | solution.py:396
  235.7 49.0 %collective-permute-start.24 = (f32[2,1,64,2048]{3,2,0,1:T(8,128)S(1)}, f32[2,1,64,2048]{3,2,0,1:T(8,128)}, u32[]{:S(2)}, u32[]{:S(2)}) collective-permute-start(f32[2,1,64,2048]{3,2,0,1:T(8,128)S(1)} %maximum_add_fusion.8), channel_id=1, source_target_pairs={{0,16},{4,20},{8,24},{12,28},{16,0},{20,4},{24,8},{28,12},{1,17},{... | collective-permute-start | bytes 3145736 | tf_op jit(solution)/shard_map/ppermute | solution.py:396
  238.2 38.5 %collective-permute-start.23 = (f32[512,256]{1,0:T(8,128)S(1)}, f32[512,256]{1,0:T(8,128)S(1)}, u32[]{:S(2)}, u32[]{:S(2)}) collective-permute-start(f32[512,256]{1,0:T(8,128)S(1)} %get-tuple-element.92), channel_id=1, source_target_pairs={{0,2},{1,3},{4,6},{5,7},{8,10},{9,11},{12,14},{13,15},{16,18},{17,... | collective-permute-start | bytes 1572872 | tf_op jit(solution)/shard_map/ppermute | solution.py:413
  241.2 74.1 %collective-permute-start.27 = (f32[512,256]{1,0:T(8,128)}, f32[512,256]{1,0:T(8,128)}, u32[]{:S(2)}, u32[]{:S(2)}) collective-permute-start(f32[512,256]{1,0:T(8,128)} %get-tuple-element.91), channel_id=1, source_target_pairs={{0,2},{1,3},{4,6},{5,7},{8,10},{9,11},{12,14},{13,15},{16,18},{17,... | collective-permute-start | bytes 1572872 | tf_op jit(solution)/shard_map/ppermute | solution.py:413
  278.2 41.3 %collective-permute-start.26 = (f32[512,256]{1,0:T(8,128)}, f32[512,256]{1,0:T(8,128)}, u32[]{:S(2)}, u32[]{:S(2)}) collective-permute-start(f32[512,256]{1,0:T(8,128)} %select_add_fusion.11.refs_0_), channel_id=1, source_target_pairs={{0,1},{1,0},{2,3},{3,2},{4,5},{5,4},{6,7},{7,6},{8,9},{9,8},{10,11... | collective-permute-start | bytes 1572872 | tf_op jit(solution)/shard_map/ppermute | solution.py:418
  281.6 45.6 %collective-permute-start.21 = (f32[2,2,64,2048]{3,2,1,0:T(8,128)}, f32[2,2,64,2048]{3,2,1,0:T(8,128)}, u32[]{:S(2)}, u32[]{:S(2)}) collective-permute-start(f32[2,2,64,2048]{3,2,1,0:T(8,128)} %maximum_add_fusion.2), channel_id=1, source_target_pairs={{0,16},{4,20},{8,24},{12,28},{16,0},{20,4},{24,8},{28,12},{1,17},{... | collective-permute-start | bytes 6291464 | tf_op jit(solution)/shard_map/ppermute | solution.py:396
  310.4 57.1 %collective-permute-start.29 = (f32[1,2,64,2048]{3,2,1,0:T(8,128)S(1)}, f32[1,2,64,2048]{3,2,1,0:T(8,128)}, u32[]{:S(2)}, u32[]{:S(2)}) collective-permute-start(f32[1,2,64,2048]{3,2,1,0:T(8,128)S(1)} %maximum_add_fusion.9), channel_id=1, source_target_pairs={{0,16},{4,20},{8,24},{12,28},{16,0},{20,4},{24,8},{28,12},{1,17},{... | collective-permute-start | bytes 3145736 | tf_op jit(solution)/shard_map/ppermute | solution.py:396
  312.8 83.0 %collective-permute-start.31 = (f32[4,1,64,2048]{3,2,0,1:T(8,128)S(1)}, f32[4,1,64,2048]{3,2,0,1:T(8,128)}, u32[]{:S(2)}, u32[]{:S(2)}) collective-permute-start(f32[4,1,64,2048]{3,2,0,1:T(8,128)S(1)} %maximum_add_fusion.4), channel_id=1, source_target_pairs={{0,4},{4,0},{8,12},{12,8},{16,20},{20,16},{24,28},{28,24},{1,5},{5... | collective-permute-start | bytes 6291464 | tf_op jit(solution)/shard_map/ppermute | solution.py:396
  317.7 45.2 %collective-permute-start.33 = (f32[512,256]{1,0:T(8,128)}, f32[512,256]{1,0:T(8,128)}, u32[]{:S(2)}, u32[]{:S(2)}) collective-permute-start(f32[512,256]{1,0:T(8,128)} %select_add_fusion.10.refs_2_), channel_id=1, source_target_pairs={{0,1},{1,0},{2,3},{3,2},{4,5},{5,4},{6,7},{7,6},{8,9},{9,8},{10,11... | collective-permute-start | bytes 1572872 | tf_op jit(solution)/shard_map/ppermute | solution.py:418
  353.6 100.7 %collective-permute-start.28 = (f32[4,2,64,2048]{3,2,1,0:T(8,128)}, f32[4,2,64,2048]{3,2,1,0:T(8,128)}, u32[]{:S(2)}, u32[]{:S(2)}) collective-permute-start(f32[4,2,64,2048]{3,2,1,0:T(8,128)} %maximum_add_fusion), channel_id=1, source_target_pairs={{0,4},{4,0},{8,12},{12,8},{16,20},{20,16},{24,28},{28,24},{1,5},{5... | collective-permute-start | bytes 12582920 | tf_op jit(solution)/shard_map/ppermute | solution.py:396
  361.7 25.1 %collective-permute-start.32 = (f32[512,512]{1,0:T(8,128)}, f32[512,512]{1,0:T(8,128)}, u32[]{:S(2)}, u32[]{:S(2)}) collective-permute-start(f32[512,512]{1,0:T(8,128)} %maximum_add_fusion.11), channel_id=1, source_target_pairs={{0,8},{4,12},{8,0},{12,4},{16,24},{20,28},{24,16},{28,20},{1,9},{5... | collective-permute-start | bytes 3145736 | tf_op jit(solution)/shard_map/ppermute | solution.py:396
  366.2 27.5 %collective-permute-start.34 = (f32[512,256]{1,0:T(8,128)S(1)}, f32[512,256]{1,0:T(8,128)S(1)}, u32[]{:S(2)}, u32[]{:S(2)}) collective-permute-start(f32[512,256]{1,0:T(8,128)S(1)} %get-tuple-element.90), channel_id=1, source_target_pairs={{0,2},{1,3},{4,6},{5,7},{8,10},{9,11},{12,14},{13,15},{16,18},{17,... | collective-permute-start | bytes 1572872 | tf_op jit(solution)/shard_map/ppermute | solution.py:413
  370.9 83.3 %collective-permute-start.30 = (f32[2,2,64,2048]{3,2,1,0:T(8,128)}, f32[2,2,64,2048]{3,2,1,0:T(8,128)}, u32[]{:S(2)}, u32[]{:S(2)}) collective-permute-start(f32[2,2,64,2048]{3,2,1,0:T(8,128)} %maximum_add_fusion.3), channel_id=1, source_target_pairs={{0,8},{4,12},{8,0},{12,4},{16,24},{20,28},{24,16},{28,20},{1,9},{5... | collective-permute-start | bytes 6291464 | tf_op jit(solution)/shard_map/ppermute | solution.py:396
  389.9 63.6 %collective-permute-start.35 = (f32[512,512]{1,0:T(8,128)}, f32[512,512]{1,0:T(8,128)}, u32[]{:S(2)}, u32[]{:S(2)}) collective-permute-start(f32[512,512]{1,0:T(8,128)} %select_add_fusion.7), channel_id=1, source_target_pairs={{0,16},{4,20},{8,24},{12,28},{16,0},{20,4},{24,8},{28,12},{1,17},{... | collective-permute-start | bytes 3145736 | tf_op jit(solution)/shard_map/ppermute | solution.py:396
  393.7 27.5 %collective-permute-start.38 = (f32[512,256]{1,0:T(8,128)S(1)}, f32[512,256]{1,0:T(8,128)S(1)}, u32[]{:S(2)}, u32[]{:S(2)}) collective-permute-start(f32[512,256]{1,0:T(8,128)S(1)} %get-tuple-element.89), channel_id=1, source_target_pairs={{0,2},{1,3},{4,6},{5,7},{8,10},{9,11},{12,14},{13,15},{16,18},{17,... | collective-permute-start | bytes 1572872 | tf_op jit(solution)/shard_map/ppermute | solution.py:413
  395.8 58.4 %collective-permute-start.36 = (f32[512,512]{1,0:T(8,128)S(1)}, f32[512,512]{1,0:T(8,128)}, u32[]{:S(2)}, u32[]{:S(2)}) collective-permute-start(f32[512,512]{1,0:T(8,128)S(1)} %maximum_add_fusion.12), channel_id=1, source_target_pairs={{0,16},{4,20},{8,24},{12,28},{16,0},{20,4},{24,8},{28,12},{1,17},{... | collective-permute-start | bytes 3145736 | tf_op jit(solution)/shard_map/ppermute | solution.py:396
  421.2 33.0 %collective-permute-start.37 = (f32[512,256]{1,0:T(8,128)S(1)}, f32[512,256]{1,0:T(8,128)S(1)}, u32[]{:S(2)}, u32[]{:S(2)}) collective-permute-start(f32[512,256]{1,0:T(8,128)S(1)} %select_add_fusion.9.refs_4_), channel_id=1, source_target_pairs={{0,1},{1,0},{2,3},{3,2},{4,5},{5,4},{6,7},{7,6},{8,9},{9,8},{10,11... | collective-permute-start | bytes 1572872 | tf_op jit(solution)/shard_map/ppermute | solution.py:418
  453.5 41.5 %collective-permute-start.40 = (f32[512,256]{1,0:T(8,128)S(1)}, f32[512,256]{1,0:T(8,128)}, u32[]{:S(2)}, u32[]{:S(2)}) collective-permute-start(f32[512,256]{1,0:T(8,128)S(1)} %select_add_fusion.8.refs_6_), channel_id=1, source_target_pairs={{0,1},{1,0},{2,3},{3,2},{4,5},{5,4},{6,7},{7,6},{8,9},{9,8},{10,11... | collective-permute-start | bytes 1572872 | tf_op jit(solution)/shard_map/ppermute | solution.py:418
  486.3 64.4 %collective-permute-start.39 = (f32[4,2,64,2048]{3,2,1,0:T(8,128)}, f32[4,2,64,2048]{3,2,1,0:T(8,128)}, u32[]{:S(2)}, u32[]{:S(2)}) collective-permute-start(f32[4,2,64,2048]{3,2,1,0:T(8,128)} %maximum_add_fusion.1), channel_id=1, source_target_pairs={{0,4},{4,0},{8,12},{12,8},{16,20},{20,16},{24,28},{28,24},{1,5},{5... | collective-permute-start | bytes 12582920 | tf_op jit(solution)/shard_map/ppermute | solution.py:396
  490.4 136.4 %collective-permute-start.41 = (f32[512,512]{1,0:T(8,128)}, f32[512,512]{1,0:T(8,128)}, u32[]{:S(2)}, u32[]{:S(2)}) collective-permute-start(f32[512,512]{1,0:T(8,128)} %select_add_fusion.6.refs_0_), channel_id=1, source_target_pairs={{0,4},{4,0},{8,12},{12,8},{16,20},{20,16},{24,28},{28,24},{1,5},{5... | collective-permute-start | bytes 3145736 | tf_op jit(solution)/shard_map/ppermute | solution.py:396
  492.6 27.8 %collective-permute-start.42 = (f32[512,512]{1,0:T(8,128)S(1)}, f32[512,512]{1,0:T(8,128)}, u32[]{:S(2)}, u32[]{:S(2)}) collective-permute-start(f32[512,512]{1,0:T(8,128)S(1)} %select_add_fusion.5), channel_id=1, source_target_pairs={{0,8},{4,12},{8,0},{12,4},{16,24},{20,28},{24,16},{28,20},{1,9},{5... | collective-permute-start | bytes 3145736 | tf_op jit(solution)/shard_map/ppermute | solution.py:396
  493.6 45.9 %collective-permute-start.44 = (f32[512,512]{1,0:T(8,128)S(1)}, f32[512,512]{1,0:T(8,128)}, u32[]{:S(2)}, u32[]{:S(2)}) collective-permute-start(f32[512,512]{1,0:T(8,128)S(1)} %maximum_add_fusion.13), channel_id=1, source_target_pairs={{0,8},{4,12},{8,0},{12,4},{16,24},{20,28},{24,16},{28,20},{1,9},{5... | collective-permute-start | bytes 3145736 | tf_op jit(solution)/shard_map/ppermute | solution.py:396
  522.3 104.6 %collective-permute-start.43 = (f32[512,512]{1,0:T(8,128)}, f32[512,512]{1,0:T(8,128)}, u32[]{:S(2)}, u32[]{:S(2)}) collective-permute-start(f32[512,512]{1,0:T(8,128)} %select_add_fusion.4.refs_2_), channel_id=1, source_target_pairs={{0,4},{4,0},{8,12},{12,8},{16,20},{20,16},{24,28},{28,24},{1,5},{5... | collective-permute-start | bytes 3145736 | tf_op jit(solution)/shard_map/ppermute | solution.py:396
  540.3 43.5 %collective-permute-start.45 = (f32[512,512]{1,0:T(8,128)S(1)}, f32[512,512]{1,0:T(8,128)}, u32[]{:S(2)}, u32[]{:S(2)}) collective-permute-start(f32[512,512]{1,0:T(8,128)S(1)} %select_add_fusion.3), channel_id=1, source_target_pairs={{0,16},{4,20},{8,24},{12,28},{16,0},{20,4},{24,8},{28,12},{1,17},{... | collective-permute-start | bytes 3145736 | tf_op jit(solution)/shard_map/ppermute | solution.py:396
  541.2 46.6 %collective-permute-start.47 = (f32[512,512]{1,0:T(8,128)S(1)}, f32[512,512]{1,0:T(8,128)}, u32[]{:S(2)}, u32[]{:S(2)}) collective-permute-start(f32[512,512]{1,0:T(8,128)S(1)} %maximum_add_fusion.14), channel_id=1, source_target_pairs={{0,16},{4,20},{8,24},{12,28},{16,0},{20,4},{24,8},{28,12},{1,17},{... | collective-permute-start | bytes 3145736 | tf_op jit(solution)/shard_map/ppermute | solution.py:396
  585.9 41.0 %collective-permute-start.46 = (f32[512,512]{1,0:T(8,128)S(1)}, f32[512,512]{1,0:T(8,128)}, u32[]{:S(2)}, u32[]{:S(2)}) collective-permute-start(f32[512,512]{1,0:T(8,128)S(1)} %select_add_fusion.2.refs_4_), channel_id=1, source_target_pairs={{0,4},{4,0},{8,12},{12,8},{16,20},{20,16},{24,28},{28,24},{1,5},{5... | collective-permute-start | bytes 3145736 | tf_op jit(solution)/shard_map/ppermute | solution.py:396
  589.9 30.7 %collective-permute-start.48 = (f32[512,512]{1,0:T(8,128)S(1)}, f32[512,512]{1,0:T(8,128)S(1)}, u32[]{:S(2)}, u32[]{:S(2)}) collective-permute-start(f32[512,512]{1,0:T(8,128)S(1)} %select_add_fusion.1), channel_id=1, source_target_pairs={{0,8},{4,12},{8,0},{12,4},{16,24},{20,28},{24,16},{28,20},{1,9},{5... | collective-permute-start | bytes 3145736 | tf_op jit(solution)/shard_map/ppermute | solution.py:396
  (35 other events, 471.3 us)

commit v3 on v2

--- a/solution.py
+++ b/solution.py
@@ -92,28 +92,42 @@
     return pair[0][:, start:stop], pair[1][:, start:stop]
 
 
-def collect(held_ref, chosen, out_ref, tile_pos, order, sems):
-    count, rows = held_ref.shape[0], held_ref.shape[2]
-    copies = []
-    for i in range(count):
-        place = 0
-        if count > 1:
-            apart = i ^ tile_pos
-            for p, bit in enumerate(order):
-                place = place + ((apart // bit) % 2) * 2**p
-        copies.append(
+def collect(held_refs, chosen, out_ref, tile_pos, order, sems):
+    def run(sources):
+        copies = [
             pltpu.make_async_copy(
-                held_ref.at[place, chosen], out_ref.at[pl.ds(i * rows, rows), :], sems.at[i]
+                ref.at[place, chosen], out_ref.at[pl.ds(i * rows, rows), :], sems.at[i]
             )
-        )
-    return copies
-
-
-def tile_kernel(index, first, last, order, waits, *refs):
+            for i, (ref, place) in enumerate(sources)
+        ]
+        for copy in copies:
+            copy.start()
+        for copy in copies:
+            copy.wait()
+
+    count, rows = held_refs[0].shape[0], held_refs[0].shape[2]
+    if len(held_refs) == 1:
+        run([(held_refs[0], i) for i in range(count)])
+        return
+    for parity in range(2):
+
+        @pl.when(tile_pos % 2 == parity)
+        def _(parity=parity):
+            sources = []
+            for i in range(2 * count):
+                place = 0
+                for p, bit in enumerate(order[:-1]):
+                    place = place + (((i ^ tile_pos) // bit) % 2) * 2**p
+                sources.append((held_refs[(i ^ parity) % 2], place))
+            run(sources)
+
+
+def tile_kernel(index, first, last, order, sources, waits, *refs):
     refs = list(refs)
     begin = first == 0
     if begin:
-        info_ref, held_ref = refs.pop(0), refs.pop(0)
+        info_ref = refs.pop(0)
+        held_refs = [refs.pop(0) for _ in range(sources)]
     else:
         state = [refs.pop(0) for _ in range(3)]
     done_refs = [(refs.pop(0), refs.pop(0)) for _ in range(index)]
@@ -127,13 +141,9 @@
     col = lax.broadcasted_iota(jnp.int32, (BLOCK, BLOCK), 1)
     if begin:
         t_ref, sems = refs[6:]
-        copies = collect(held_ref, 0, t_ref, info_ref[0], order, sems)
-        for copy in copies:
-            copy.start()
+        collect(held_refs, 0, t_ref, info_ref[0], order, sems)
         l_ref[:, lead:] = jnp.zeros((rows, rows), jnp.float32)
         w_ref[...] = jnp.zeros_like(w_ref)
-        for copy in copies:
-            copy.wait()
         diag = t_ref[:, lead:]
         if index:
             given = split(t_ref[:, :lead])
@@ -215,16 +225,16 @@
     wide = jax.ShapeDtypeStruct((rows, (index + 1) * rows), jnp.float32)
     half = jax.ShapeDtypeStruct((rows, (index + 1) * rows), jnp.bfloat16)
     begin = first == 0
-    given = [info, held] if begin else list(state)
+    given = [info, *held] if begin else list(state)
     pairs = [part for pair in done for part in pair]
     return pl.pallas_call(
-        functools.partial(tile_kernel, index, first, last, order, len(waits)),
+        functools.partial(tile_kernel, index, first, last, order, len(held), len(waits)),
         out_shape=[wide, flat, flat, half, half, TOKEN],
-        in_specs=([SMEM, ANY] if begin else [VMEM] * 3) + [VMEM] * len(pairs) + [ANY] * len(waits),
+        in_specs=([SMEM] + [ANY] * len(held) if begin else [VMEM] * 3) + [VMEM] * len(pairs) + [ANY] * len(waits),
         out_specs=[VMEM] * 5 + [SMEM],
         scratch_shapes=[
             pltpu.VMEM((rows, (index + 1) * rows), jnp.float32),
-            pltpu.SemaphoreType.DMA((held.shape[0],)),
+            pltpu.SemaphoreType.DMA((held[0].shape[0] * len(held),)),
         ] if begin else [],
         compiler_params=limit(),
         cost_estimate=cost((last - first) * 8_000_000_000),
@@ -271,32 +281,20 @@
     )
 
 
-def side_kernel(orders, steps, sizes, info_ref, *refs):
+def side_kernel(steps, info_ref, held_ref, *refs):
     refs = list(refs)
-    held = [refs.pop(0) for _ in sizes]
     inverse = [(refs.pop(0), refs.pop(0)) for _ in range(steps)]
     solved_ref, high_ref, low_ref, token_ref, scratch_ref, sems = refs
     token_ref[0, 0] = 0.0
-    tile_pos = info_ref[0]
-    own = jnp.maximum(tile_pos - steps, 0)
-    start = 0
-    for ref, size, order in zip(held, sizes, orders):
-        @pl.when((own >= start) & (own < start + size))
-        def _(ref=ref, start=start, order=order):
-            copies = collect(ref, own - start, scratch_ref, tile_pos, order, sems)
-            for copy in copies:
-                copy.start()
-            for copy in copies:
-                copy.wait()
-        start += size
+    own = jnp.maximum(info_ref[0] - steps, 0)
+    collect([held_ref], own, scratch_ref, info_ref[0], None, sems)
     both_solves(
         split(scratch_ref[...]), solved_ref.shape[1], info_ref[1], inverse, solved_ref, scratch_ref, high_ref, low_ref
     )
 
 
-def change_kernel(orders, steps, sizes, info_ref, *refs):
+def change_kernel(steps, info_ref, held_ref, *refs):
     refs = list(refs)
-    held = [refs.pop(0) for _ in sizes]
     factor = [refs.pop(0) for _ in range(steps)]
     below, side = refs[:3], refs[3:6]
     front_below_ref, front_diag_ref, below_ref, diag_ref, token_ref, match_ref, sems = refs[6:]
@@ -310,18 +308,9 @@
 
     @pl.when(col_pos >= PANELS)
     def _():
-        start = 0
-        for ref, size, order in zip(held, sizes, orders):
-            for n in range(size):
-                @pl.when((start + n + steps) // 2 == col_pos)
-                def _(ref=ref, n=n, at=start + n, order=order):
-                    half = match_ref.at[pl.ds((at % 2) * rows, rows), :]
-                    copies = collect(ref, n, half, tile_pos, order, sems)
-                    for copy in copies:
-                        copy.start()
-                    for copy in copies:
-                        copy.wait()
-            start += size
+        for half in range(2):
+            part = match_ref.at[pl.ds(half * rows, rows), :]
+            collect([held_ref], 2 * col_pos + half - steps, part, tile_pos, None, sems)
         for part in range(width // rows):
             here = slice(part * rows, (part + 1) * rows)
             match = split(match_ref[here, :])
@@ -433,20 +422,21 @@
         held = tie(held)
         other = exchange(held, bit, tile_count)
         yield [other]
+        if bit == 1 and piece.shape[1] % 8 == 0:
+            return held, other
         held = jnp.concatenate((held, other), 0)
-    if piece.shape[1] % 8 == 0:
-        return held
     place = {}
     for m in range(tile_count):
         place[sum(bit for p, bit in enumerate(order) if m >> p & 1)] = m
     table = jnp.array([place[w] for w in range(tile_count)], jnp.int32)
-    return jnp.concatenate(
+    ordered = jnp.concatenate(
         [
             lax.dynamic_index_in_dim(held, table[i ^ tile_pos], 0, keepdims=False)
             for i in range(tile_count)
         ],
         1,
-    )[None]
+    )
+    return (ordered[None],)
 
 
 def fetch_target(block, order, tile_pos, tile_count, target, tie):
@@ -505,11 +495,11 @@
         return self.results[name]
 
 
-CHUNKS = 4
+CHUNKS = 2
 PARTS = 2
 LEAD_WINDOWS = ([1, 2, 3, 4, 5], [2, 3, 5, 6, 7], [4, 5, 6, 7, 9], [5, 6, 7, 8, 10])
-SIDE_WINDOWS = ([6, 7, 8, 9, 11], [7, 8, 10, 11, 13])
-BELOW_WINDOWS = ([8, 9, 10, 11, 12], [9, 10, 11, 12, 14], [10, 11, 12, 13, 15], [11, 12, 14, 15, 16])
+SIDE_WINDOWS = [6, 7, 8]
+BELOW_WINDOWS = ([7, 8, 9, 10, 11], [8, 9, 11, 12, 13])
 
 
 def shards(tile_count, col_count, front_diag, front_below, ancestor, owner_cols, rel):
@@ -548,16 +538,18 @@
         piece = panels[0] if size <= width else jnp.concatenate(panels, 2)[:, :, :size]
         return (yield from gather_rows(piece, bits, tile_pos, tile_count, plan.tie))
 
-    def side_stream(start, stop, order):
-        pair = yield from climb(pieces[start:stop], col_pos, col_count, plan.tie)
-        piece = jnp.concatenate(by_panel(pair, col_pos), 2)
-        return (yield from gather_rows(piece, order, tile_pos, tile_count, plan.tie))
+    def side_stream():
+        pair = yield from climb(pieces[steps:], col_pos, col_count, plan.tie)
+        piece = plan.tie(jnp.concatenate(by_panel(pair, col_pos), 2))
+        held = lax.all_gather(piece, "tiles")
+        yield []
+        if piece.shape[1] % 8:
+            held = jnp.swapaxes(held, 0, 1).reshape(1, tile_count - steps, rows, lead)
+        return held
 
     for i, windows in enumerate(LEAD_WINDOWS):
         plan.add(("lead", i), lead_stream(i), windows)
-    middle = steps + (tile_count - steps) // 2
-    plan.add(("side", 0), side_stream(steps, middle, bits), SIDE_WINDOWS[0])
-    plan.add(("side", 1), side_stream(middle, tile_count, turned), SIDE_WINDOWS[1])
+    plan.add("side", side_stream(), SIDE_WINDOWS)
     flying = []
     for window in range(1, 4):
         flying += plan.run(window)
@@ -603,31 +595,29 @@
     )(info, *[part for k in range(CHUNKS) for part in own_parts[k]], *pairs)
     plan.token = below[3]
     plan.run(window + 1)
-    sides = [plan.finish(("side", n)) for n in range(2)]
-    sems = pltpu.SemaphoreType.DMA((sides[0].shape[0],))
-    sizes = (middle - steps, tile_count - middle)
-    orders = (bits, turned)
+    gathered = plan.finish("side")
+    sems = pltpu.SemaphoreType.DMA((gathered.shape[0],))
     side = pl.pallas_call(
-        functools.partial(side_kernel, orders, steps, sizes),
+        functools.partial(side_kernel, steps),
         out_shape=solves,
-        in_specs=[SMEM, ANY, ANY] + [VMEM] * len(pairs),
+        in_specs=[SMEM, ANY] + [VMEM] * len(pairs),
         out_specs=[VMEM] * 3 + [SMEM],
         scratch_shapes=[wide, sems],
         compiler_params=limit(),
         cost_estimate=cost(20_000_000_000),
-    )(info, *sides, *pairs)
+    )(info, gathered, *pairs)
     plan.token = side[3]
     plan.run(window + 2)
     flat = jax.ShapeDtypeStruct((rows, width), jnp.float32)
     factor_below, factor_diag, token = pl.pallas_call(
-        functools.partial(change_kernel, orders, steps, sizes),
+        functools.partial(change_kernel, steps),
         out_shape=[flat, flat, TOKEN],
-        in_specs=[SMEM, ANY, ANY] + [VMEM] * (steps + 8),
+        in_specs=[SMEM, ANY] + [VMEM] * (steps + 8),
         out_specs=[VMEM] * 2 + [SMEM],
         scratch_shapes=[pltpu.VMEM((width, lead), jnp.float32), sems],
         compiler_params=limit(),
         cost_estimate=cost(20_000_000_000),
-    )(info, *sides, *factor_rows, *below[:3], *side[:3], front_below, front_diag)
+    )(info, gathered, *factor_rows, *below[:3], *side[:3], front_below, front_diag)
     plan.token = token
     plan.run(window + 3)
     target_parts = [part for k in range(CHUNKS) for part in plan.finish(("below", k))]

time: 651 us -> 631 us (0.969)
  other arithmetic: 104 us -> 54.8 us
  waiting for transfers between devices: 181 us -> 217 us
  starting transfers between devices: 53.6 us -> 32.2 us
  between operations: 3.02 us -> 16.2 us
    add x36 -> x21, other arithmetic: 66.1 us -> 41.1 us  [tie(): return value if self.token is None else value + self.token[0, 0]]
    concatenate x11 -> x5, other arithmetic: 28.3 us -> 3.78 us  [gather_rows(): held = jnp.concatenate((held, other), 0)]
    ppermute x10 -> x7, waiting for transfers between devices: 29.4 us -> 50.8 us  [climb(): lax.ppermute(held, 'cols', [(at, at ^ 1) for at in range(col_count)])]
    ppermute x30 -> x18, starting transfers between devices: 37.6 us -> 20.4 us  [exchange(): lax.ppermute(block, 'tiles', [(i, i ^ bit) for i in range(tile_count)])]
    ppermute x10 -> x7, waiting for transfers between devices: 107 us -> 118 us  [climb(): other = lax.ppermute(held, 'cols', pairs)]
    ppermute x10 -> x7, starting transfers between devices: 13.2 us -> 9.67 us  [climb(): other = lax.ppermute(held, 'cols', pairs)]
    ppermute x30 -> x18, waiting for transfers between devices: 44.8 us -> 48.3 us  [exchange(): lax.ppermute(block, 'tiles', [(i, i ^ bit) for i in range(tile_count)])]
  transfers between devices with their start and end apart: 50 -> 33, of which waited for: 16 -> 17; matrix products, arithmetic and copies ran while one was open for 16% -> 9% of each run, Pallas kernels for 39% -> 34%
where the time goes in v3:
time: 631 us; the launch traced here: 623 us
  Pallas kernels  267 us (42%)
  waiting for transfers between devices  217 us (34%)
  other arithmetic  54.8 us (9%)
  starting transfers between devices  32.2 us (5%)
  blocking collectives  28.4 us (5%)
  between operations  16.2 us (3%)
  local copies, waits for them, and re-layouts  6.87 us (1%)
    pallas_call x8, Pallas kernels, tile_part(): pl.pallas_call(functools.partial(tile_kernel, index, first, last, order,...  173 us
    ppermute x7, waiting for transfers between devices, climb(): other = lax.ppermute(held, 'cols', pairs)  118 us
    ppermute x7, waiting for transfers between devices, climb(): lax.ppermute(held, 'cols', [(at, at ^ 1) for at in range(col_count)])  50.8 us
    ppermute x18, waiting for transfers between devices, exchange(): lax.ppermute(block, 'tiles', [(i, i ^ bit) for i in range(tile_count)])  48.3 us
    add x21, other arithmetic, tie(): return value if self.token is None else value + self.token[0, 0]  41.1 us
    pallas_call x1, Pallas kernels, shards(): pl.pallas_call(functools.partial(change_kernel, steps), out_shape=[flat,...  29 us
    all_to_all x1, blocking collectives, shards(): lax.all_to_all(front_diag.reshape(tile_count, rows // tile_count, width),...  28.4 us
    pallas_call x1, Pallas kernels, shards(): pl.pallas_call(functools.partial(side_kernel, steps), out_shape=solves, i...  25.2 us
  transfers between devices with their start and end apart: 33, of which 17 were waited for; matrix products, arithmetic and copies ran while one was open for 9% of the time, Pallas kernels for 34%

profile of v3, /device:TPU:31, one launch (start us, length us, event | category | flops | bytes accessed | tf_op | source)
XLA Modules:
  0.0 622.7 jit_solution(15122217480509118205)
XLA Ops:
  7.2 28.4 %all_to_all.5 = f32[8,64,1024]{2,1,0:T(8,128)S(1)} all-to-all(f32[8,64,1024]{2,1,0:T(8,128)} %bitcast.50), channel_id=1, replica_groups=mesh['tiles'=8,'cols'=4] {'tiles'}, dimensions={0} | all-to-all | bytes 4194304 | tf_op jit(solution)/shard_map/all_to_all | solution.py:529
  36.9 9.6 %collective-permute-done.refs_3_ = f32[1,64,512]{2,1,0:T(8,128)S(1)} collective-permute-done((f32[1,64,512]{2,1,0:T(8,128)S(1)}, f32[1,64,512]{2,1,0:T(8,128)S(1)}, u32[]{:S(2)}, u32[]{:S(2)}) %collective-permute-start) | collective-permute-done | bytes 131104 | tf_op jit(solution)/shard_map/ppermute | solution.py:402
  46.6 4.5 collective-permute-done.1.refs_4_
  51.8 3.3 collective-permute-done.2.refs_6_
  57.8 2.6 collective-permute-done.3.refs_3_
  60.5 3.7 collective-permute-start.4
  64.2 8.9 %collective-permute-done.5.refs_5_ = f32[1,64,1024]{2,1,0:T(8,128)S(1)} collective-permute-done((f32[1,64,1024]{2,1,0:T(8,128)S(1)}, f32[1,64,1024]{2,1,0:T(8,128)S(1)}, u32[]{:S(2)}, u32[]{:S(2)}) %collective-permute-start.5) | collective-permute-done | bytes 262176 | tf_op jit(solution)/shard_map/ppermute | solution.py:402
  75.2 6.8 %collective-permute-done.6.refs_7_ = f32[1,64,1024]{2,1,0:T(8,128)} collective-permute-done((f32[1,64,1024]{2,1,0:T(8,128)S(1)}, f32[1,64,1024]{2,1,0:T(8,128)}, u32[]{:S(2)}, u32[]{:S(2)}) %collective-permute-start.6) | collective-permute-done | bytes 262176 | tf_op jit(solution)/shard_map/ppermute | solution.py:407
  83.1 17.6 %shard_map.85 = (f32[512,512]{1,0:T(8,128)}, f32[512,512]{1,0:T(8,128)}, f32[512,512]{1,0:T(8,128)}, bf16[512,512]{1,0:T(8,128)(2,1)}, bf16[512,512]{1,0:T(8,128)(2,1)}, /*index=5*/f32[1,1]{1,0:T(1,128)}) custom-call(s32[2]{0:T(128)} %pad_add_fusion.refs_0_.info_ref, f32[4,1,64,512]{3,2,1,0:T(8,128)} %copy-done.14, ...), custom_call_target="tpu_custom_call" | custom-call | flops 16000000000 | bytes 1048576 | tf_op jit(solution)/shard_map/pallas_call | solution.py:230
  100.7 2.3 select_add_fusion.7
  105.8 11.7 %collective-permute-done.8.refs_4_ = f32[1,64,1024]{2,1,0:T(8,128)S(1)} collective-permute-done((f32[1,64,1024]{2,1,0:T(8,128)S(1)}, f32[1,64,1024]{2,1,0:T(8,128)S(1)}, u32[]{:S(2)}, u32[]{:S(2)}) %collective-permute-start.8) | collective-permute-done | bytes 262176 | tf_op jit(solution)/shard_map/ppermute | solution.py:402
  121.3 3.7 collective-permute-done.10.refs_6_
  125.7 14.8 %shard_map.86 = (f32[512,512]{1,0:T(8,128)}, f32[512,512]{1,0:T(8,128)}, f32[512,512]{1,0:T(8,128)}, bf16[512,512]{1,0:T(8,128)(2,1)}, bf16[512,512]{1,0:T(8,128)(2,1)}, /*index=5*/f32[1,1]{1,0:T(1,128)}) custom-call(f32[512,512]{1,0:T(8,128)} %get-tuple-element.44.refs_0_, f32[512,512]{1,0:T(8,128)} %get-tuple-element.45.refs_1_, ...), custom_call_target="tpu_custom_call" | custom-call | flops 16000000000 | bytes 1048576 | tf_op jit(solution)/shard_map/pallas_call | solution.py:230
  141.3 2.6 collective-permute-start.14
  146.1 23.0 %collective-permute-done.7.refs_8_ = f32[4,64,1024]{2,1,0:T(8,128)} collective-permute-done((f32[4,64,1024]{2,1,0:T(8,128)}, f32[4,64,1024]{2,1,0:T(8,128)}, u32[]{:S(2)}, u32[]{:S(2)}) %collective-permute-start.7) | collective-permute-done | bytes 1048608 | tf_op jit(solution)/shard_map/ppermute | solution.py:402
  169.1 2.5 select_add_fusion.6
  171.7 3.1 collective-permute-done.16.refs_7_
  176.6 21.1 %shard_map.87 = (f32[512,1024]{1,0:T(8,128)}, f32[512,512]{1,0:T(8,128)}, f32[512,512]{1,0:T(8,128)}, bf16[512,1024]{1,0:T(8,128)(2,1)}, bf16[512,1024]{1,0:T(8,128)(2,1)}, /*index=5*/f32[1,1]{1,0:T(1,128)}) custom-call(s32[2]{0:T(128)} %pad_add_fusion.refs_0_.info_ref, f32[4,1,64,1024]{3,2,1,0:T(8,128)} %bitcast.53, f32[4,1,64,1024]{3,2,1,0:T(8,128)} %bitcast.59, ...), custom_call_target="tpu_custom_call" | custom-call | flops 16000000000 | bytes 1048576 | tf_op jit(solution)/shard_map/pallas_call | solution.py:230
  198.7 2.0 maximum_add_fusion
  200.7 2.9 slice_add_fusion.1
  211.3 64.2 %collective-permute-done.17.refs_5_ = f32[512,512]{1,0:T(8,128)S(1)} collective-permute-done((f32[512,512]{1,0:T(8,128)S(1)}, f32[512,512]{1,0:T(8,128)S(1)}, u32[]{:S(2)}, u32[]{:S(2)}) %collective-permute-start.17) | collective-permute-done | bytes 1048608 | tf_op jit(solution)/shard_map/ppermute | solution.py:402
  277.5 16.9 %shard_map.88 = (f32[512,1024]{1,0:T(8,128)}, f32[512,512]{1,0:T(8,128)}, f32[512,512]{1,0:T(8,128)}, bf16[512,1024]{1,0:T(8,128)(2,1)}, bf16[512,1024]{1,0:T(8,128)(2,1)}, /*index=5*/f32[1,1]{1,0:T(1,128)}) custom-call(f32[512,1024]{1,0:T(8,128)} %get-tuple-element.52.refs_0_, f32[512,512]{1,0:T(8,128)} %get-tuple-element.53.refs_1_, ...), custom_call_target="tpu_custom_call" | custom-call | flops 16000000000 | bytes 1048576 | tf_op jit(solution)/shard_map/pallas_call | solution.py:230
  294.4 3.0 maximum_add_fusion.4
  298.2 3.1 select_add_fusion.4.refs_2_
  301.2 1.8 collective-permute-start.25
  304.6 16.0 %collective-permute-done.21.refs_7_.refs_1_ = f32[512,512]{1,0:T(8,128)} collective-permute-done((f32[512,512]{1,0:T(8,128)S(1)}, f32[512,512]{1,0:T(8,128)}, u32[]{:S(2)}, u32[]{:S(2)}) %collective-permute-start.21) | collective-permute-done | bytes 1048608 | tf_op jit(solution)/shard_map/ppermute | solution.py:407
  326.4 16.7 %collective-permute-done.25.refs_8_.refs_3_ = f32[512,512]{1,0:T(8,128)} collective-permute-done((f32[512,512]{1,0:T(8,128)}, f32[512,512]{1,0:T(8,128)}, u32[]{:S(2)}, u32[]{:S(2)}) %collective-permute-start.25) | collective-permute-done | bytes 1048608 | tf_op jit(solution)/shard_map/ppermute | solution.py:407
  343.1 2.9 broadcast_select_fusion.1
  346.0 25.2 %shard_map.89 = (f32[512,1536]{1,0:T(8,128)}, f32[512,512]{1,0:T(8,128)}, f32[512,512]{1,0:T(8,128)}, bf16[512,1536]{1,0:T(8,128)(2,1)}, bf16[512,1536]{1,0:T(8,128)(2,1)}, /*index=5*/f32[1,1]{1,0:T(1,128)}) custom-call(s32[2]{0:T(128)} %pad_add_fusion.refs_0_.info_ref, f32[4,1,64,1536]{3,2,1,0:T(8,128)} %bitcast.23.refs_1_, ...), custom_call_target="tpu_custom_call" | custom-call | flops 16000000000 | bytes 1048576 | tf_op jit(solution)/shard_map/pallas_call | solution.py:230
  371.2 2.4 select_add_fusion.3
  373.7 3.3 maximum_add_fusion.2.refs_1_
  377.8 21.0 %shard_map.90 = (f32[512,1536]{1,0:T(8,128)}, f32[512,512]{1,0:T(8,128)}, f32[512,512]{1,0:T(8,128)}, bf16[512,1536]{1,0:T(8,128)(2,1)}, bf16[512,1536]{1,0:T(8,128)(2,1)}, /*index=5*/f32[1,1]{1,0:T(1,128)}) custom-call(f32[512,1536]{1,0:T(8,128)} %get-tuple-element.59.refs_0_, f32[512,512]{1,0:T(8,128)} %get-tuple-element.60.refs_1_, ...), custom_call_target="tpu_custom_call" | custom-call | flops 16000000000 | bytes 1048576 | tf_op jit(solution)/shard_map/pallas_call | solution.py:230
  398.7 2.0 maximum_add_fusion.3
  402.2 18.4 %collective-permute-done.27.refs_9_ = f32[512,1024]{1,0:T(8,128)} collective-permute-done((f32[512,1024]{1,0:T(8,128)}, f32[512,1024]{1,0:T(8,128)}, u32[]{:S(2)}, u32[]{:S(2)}) %collective-permute-start.27) | collective-permute-done | bytes 2097184 | tf_op jit(solution)/shard_map/ppermute | solution.py:385
  420.6 4.1 select_add_fusion.2.refs_0_
  424.7 2.3 collective-permute-start.28
  427.0 30.8 %shard_map.91 = (f32[512,2048]{1,0:T(8,128)}, f32[512,512]{1,0:T(8,128)}, f32[512,512]{1,0:T(8,128)}, bf16[512,2048]{1,0:T(8,128)(2,1)}, bf16[512,2048]{1,0:T(8,128)(2,1)}, /*index=5*/f32[1,1]{1,0:T(1,128)}) custom-call(s32[2]{0:T(128)} %pad_add_fusion.refs_0_.info_ref, f32[4,1,64,2048]{3,2,1,0:T(8,128)} %maximum_add_fusion.2.refs_1_, ...), custom_call_target="tpu_custom_call" | custom-call | flops 16000000000 | bytes 1048576 | tf_op jit(solution)/shard_map/pallas_call | solution.py:230
  457.7 7.8 %collective-permute-done.29.refs_10_ = f32[512,1024]{1,0:T(8,128)} collective-permute-done((f32[512,1024]{1,0:T(8,128)S(1)}, f32[512,1024]{1,0:T(8,128)}, u32[]{:S(2)}, u32[]{:S(2)}) %collective-permute-start.29) | collective-permute-done | bytes 2097184 | tf_op jit(solution)/shard_map/ppermute | solution.py:385
  465.6 2.6 select_add_fusion.1
  468.2 2.2 collective-permute-start.30
  473.0 25.9 %shard_map.92 = (f32[512,2048]{1,0:T(8,128)}, f32[512,512]{1,0:T(8,128)}, f32[512,512]{1,0:T(8,128)}, bf16[512,2048]{1,0:T(8,128)(2,1)}, bf16[512,2048]{1,0:T(8,128)(2,1)}, /*index=5*/f32[1,1]{1,0:T(1,128)}) custom-call(f32[512,2048]{1,0:T(8,128)} %get-tuple-element.66.refs_0_, f32[512,512]{1,0:T(8,128)} %get-tuple-element.67.refs_1_, ...), custom_call_target="tpu_custom_call" | custom-call | flops 16000000000 | bytes 1048576 | tf_op jit(solution)/shard_map/pallas_call | solution.py:230
  499.0 16.2 %collective-permute-done.30 = f32[512,1024]{1,0:T(8,128)} collective-permute-done((f32[512,1024]{1,0:T(8,128)S(1)}, f32[512,1024]{1,0:T(8,128)}, u32[]{:S(2)}, u32[]{:S(2)}) %collective-permute-start.30) | collective-permute-done | bytes 2097184 | tf_op jit(solution)/shard_map/ppermute | solution.py:385
  515.1 2.3 select_add_fusion.refs_2_
  517.4 2.0 collective-permute-start.31
  520.1 24.2 %shard_map.93 = (f32[512,1024]{1,0:T(8,128)}, bf16[512,2048]{1,0:T(8,128)(2,1)}, bf16[512,2048]{1,0:T(8,128)(2,1)}, f32[1,1]{1,0:T(1,128)}) custom-call(s32[2]{0:T(128)} %pad_add_fusion.refs_0_.info_ref, f32[512,512]{1,0:T(8,128)} %copy-done.2, f32[512,512]{1,0:T(8,128)} %collective-permute-done.21.refs_7_.refs_1_, f32[512,512]{1,0:T(8,128)} %select_add_fusion.4.refs_2_, ...), custom_call_target="tpu_custom_call" | custom-call | flops 20000000000 | bytes 1048576 | tf_op jit(solution)/shard_map/pallas_call | solution.py:587
  545.7 15.7 %shard_map.96 = f32[512,1024]{1,0:T(8,128)} custom-call(s32[2]{0:T(128)} %pad_add_fusion.refs_0_.info_ref, s32[1,512]{1,0:T(1,128)} %bitcast.58, s32[2,512]{1,0:T(2,128)} %broadcast_subtract_fusion.col_ref, bf16[512,2048]{1,0:T(8,128)(2,1)} %get-tuple-element.74.refs_5_.high_ref, bf16[512,2048]{1,0:T(8,128)(2,1)} %get-tuple-element.75.refs_6_.low_ref, ...), custom_call_target="tpu_custom_call" | custom-call | flops 10000000000 | bytes 1048576 | tf_op jit(solution)/shard_map/pallas_call | solution.py:627
  561.4 25.2 %shard_map.94 = (f32[512,1024]{1,0:T(8,128)}, bf16[512,2048]{1,0:T(8,128)(2,1)}, bf16[512,2048]{1,0:T(8,128)(2,1)}, f32[1,1]{1,0:T(1,128)}) custom-call(s32[2]{0:T(128)} %pad_add_fusion.refs_0_.info_ref, f32[8,4,64,2048]{3,2,1,0:T(8,128)} %all-gather.2.cloned.1.call-done.held_ref, bf16[512,512]{1,0:T(8,128)(2,1)} %get-tuple-element.48.refs_3_.refs_4_.refs_0_, ...), custom_call_target="tpu_custom_call" | custom-call | flops 20000000000 | bytes 1048576 | tf_op jit(solution)/shard_map/pallas_call | solution.py:600
  586.6 29.0 %shard_map.95 = (f32[512,1024]{1,0:T(8,128)}, f32[512,1024]{1,0:T(8,128)}, f32[1,1]{1,0:T(1,128)}) custom-call(s32[2]{0:T(128)} %pad_add_fusion.refs_0_.info_ref, f32[8,4,64,2048]{3,2,1,0:T(8,128)} %all-gather.2.cloned.1.call-done.held_ref, f32[512,512]{1,0:T(8,128)} %get-tuple-element.51.refs_0_, f32[512,1024]{1,0:T(8,128)} %get-tuple-element.55.refs_1_, ...), custom_call_target="tpu_custom_call" | custom-call | flops 20000000000 | bytes 1048576 | tf_op jit(solution)/shard_map/pallas_call | solution.py:612
  (133 shorter events, 44.2 us)
Async XLA Ops:
  7.2 554.2 %all-gather.2.cloned.1.call-start = ((), (), s32[]{:S(2)}) async-start(), calls=%async_computation.1 | async-start | bytes 18874368 | tf_op jit(solution)/shard_map/all_gather | solution.py:544
  35.6 10.9 %collective-permute-start = (f32[1,64,512]{2,1,0:T(8,128)S(1)}, f32[1,64,512]{2,1,0:T(8,128)S(1)}, u32[]{:S(2)}, u32[]{:S(2)}) collective-permute-start(f32[1,64,512]{2,1,0:T(8,128)S(1)} %slice.33), channel_id=1, source_target_pairs={{0,2},{1,3},{4,6},{5,7},{8,10},{9,11},{12,14},{13,15},{16,18},{17,... | collective-permute-start | bytes 393224 | tf_op jit(solution)/shard_map/ppermute | solution.py:402
  46.5 8.6 %copy-start.23 = (f32[1,64,512]{2,1,0:T(8,128)}, f32[1,64,512]{2,1,0:T(8,128)S(1)}, u32[]{:S(2)}) copy-start(f32[1,64,512]{2,1,0:T(8,128)S(1)} %collective-permute-done.refs_3_) | copy-start | bytes 393220
  46.6 4.6 collective-permute-start.1
  51.2 3.9 collective-permute-start.2
  55.1 27.8 %copy-start.15 = (f32[1,1,64,512]{3,2,1,0:T(8,128)}, f32[1,1,64,512]{3,2,1,0:T(8,128)S(1)}, u32[]{:S(2)}) copy-start(f32[1,1,64,512]{3,2,1,0:T(8,128)S(1)} %collective-permute-done.2.refs_6_) | copy-start | bytes 393220
  55.1 5.3 collective-permute-start.3
  56.5 16.6 %collective-permute-start.5 = (f32[1,64,1024]{2,1,0:T(8,128)S(1)}, f32[1,64,1024]{2,1,0:T(8,128)S(1)}, u32[]{:S(2)}, u32[]{:S(2)}) collective-permute-start(f32[1,64,1024]{2,1,0:T(8,128)S(1)} %slice.34), channel_id=1, source_target_pairs={{0,2},{1,3},{4,6},{5,7},{8,10},{9,11},{12,14},{13,15},{16,18},{17,... | collective-permute-start | bytes 786440 | tf_op jit(solution)/shard_map/ppermute | solution.py:402
  60.4 12.8 %copy-start.17 = (f32[2,1,64,512]{3,2,1,0:T(8,128)}, f32[2,1,64,512]{3,2,1,0:T(8,128)S(1)}, u32[]{:S(2)}) copy-start(f32[2,1,64,512]{3,2,1,0:T(8,128)S(1)} %collective-permute-done.3.refs_3_) | copy-start | bytes 786436
  60.5 22.6 %copy-start.14 = (f32[4,1,64,512]{3,2,1,0:T(8,128)}, f32[4,1,64,512]{3,2,1,0:T(8,128)S(1)}, u32[]{:S(2)}) copy-start(f32[4,1,64,512]{3,2,1,0:T(8,128)S(1)} %pad_maximum_fusion.refs_1_) | copy-start | bytes 1572868
  60.5 22.6 %collective-permute-start.4 = (f32[4,1,64,512]{3,2,1,0:T(8,128)S(1)}, f32[4,1,64,512]{3,2,1,0:T(8,128)}, u32[]{:S(2)}, u32[]{:S(2)}) collective-permute-start(f32[4,1,64,512]{3,2,1,0:T(8,128)S(1)} %pad_maximum_fusion.refs_1_), channel_id=1, source_target_pairs={{0,4},{4,0},{8,12},{12,8},{16,20},{20,16},{24,28},{28,24},{1,5},{5... | collective-permute-start | bytes 1572872 | tf_op jit(solution)/shard_map/ppermute | solution.py:385
  73.1 9.9 %copy-start.16 = (f32[1,64,1024]{2,1,0:T(8,128)}, f32[1,64,1024]{2,1,0:T(8,128)S(1)}, u32[]{:S(2)}) copy-start(f32[1,64,1024]{2,1,0:T(8,128)S(1)} %collective-permute-done.5.refs_5_) | copy-start | bytes 786436
  73.2 8.8 %collective-permute-start.6 = (f32[1,64,1024]{2,1,0:T(8,128)S(1)}, f32[1,64,1024]{2,1,0:T(8,128)}, u32[]{:S(2)}, u32[]{:S(2)}) collective-permute-start(f32[1,64,1024]{2,1,0:T(8,128)S(1)} %get-tuple-element.94), channel_id=1, source_target_pairs={{0,1},{1,0},{2,3},{3,2},{4,5},{5,4},{6,7},{7,6},{8,9},{9,8},{10,11... | collective-permute-start | bytes 786440 | tf_op jit(solution)/shard_map/ppermute | solution.py:407
  73.9 26.8 %collective-permute-start.11 = (f32[1,64,1024]{2,1,0:T(8,128)S(1)}, f32[1,64,1024]{2,1,0:T(8,128)}, u32[]{:S(2)}, u32[]{:S(2)}) collective-permute-start(f32[1,64,1024]{2,1,0:T(8,128)S(1)} %get-tuple-element.93), channel_id=1, source_target_pairs={{0,2},{1,3},{4,6},{5,7},{8,10},{9,11},{12,14},{13,15},{16,18},{17,... | collective-permute-start | bytes 786440 | tf_op jit(solution)/shard_map/ppermute | solution.py:402
  83.0 21.3 %collective-permute-start.9 = (f32[1,1,64,1024]{3,2,0,1:T(8,128)S(1)}, f32[1,1,64,1024]{3,2,0,1:T(8,128)S(1)}, u32[]{:S(2)}, u32[]{:S(2)}) collective-permute-start(f32[1,1,64,1024]{3,2,0,1:T(8,128)S(1)} %bitcast.47), channel_id=1, source_target_pairs={{0,8},{4,12},{8,0},{12,4},{16,24},{20,28},{24,16},{28,20},{1,9},{5... | collective-permute-start | bytes 786440 | tf_op jit(solution)/shard_map/ppermute | solution.py:385
  103.0 14.5 %collective-permute-start.8 = (f32[1,64,1024]{2,1,0:T(8,128)S(1)}, f32[1,64,1024]{2,1,0:T(8,128)S(1)}, u32[]{:S(2)}, u32[]{:S(2)}) collective-permute-start(f32[1,64,1024]{2,1,0:T(8,128)S(1)} %get-tuple-element.90), channel_id=1, source_target_pairs={{0,2},{1,3},{4,6},{5,7},{8,10},{9,11},{12,14},{13,15},{16,18},{17,... | collective-permute-start | bytes 786440 | tf_op jit(solution)/shard_map/ppermute | solution.py:402
  104.3 17.1 %copy-start.11 = (f32[1,1,64,1024]{3,2,0,1:T(8,128)}, f32[1,1,64,1024]{3,2,0,1:T(8,128)S(1)}, u32[]{:S(2)}) copy-start(f32[1,1,64,1024]{3,2,0,1:T(8,128)S(1)} %collective-permute-done.9) | copy-start | bytes 786436
  105.7 34.9 %collective-permute-start.13 = (f32[2,1,64,1024]{3,2,0,1:T(8,128)}, f32[2,1,64,1024]{3,2,0,1:T(8,128)S(1)}, u32[]{:S(2)}, u32[]{:S(2)}) collective-permute-start(f32[2,1,64,1024]{3,2,0,1:T(8,128)} %maximum_add_fusion.11), channel_id=1, source_target_pairs={{0,16},{4,20},{8,24},{12,28},{16,0},{20,4},{24,8},{28,12},{1,17},{... | collective-permute-start | bytes 1572872 | tf_op jit(solution)/shard_map/ppermute | solution.py:385
  117.5 7.5 %collective-permute-start.10 = (f32[1,64,1024]{2,1,0:T(8,128)S(1)}, f32[1,64,1024]{2,1,0:T(8,128)S(1)}, u32[]{:S(2)}, u32[]{:S(2)}) collective-permute-start(f32[1,64,1024]{2,1,0:T(8,128)S(1)} %broadcast_select_fusion.9), channel_id=1, source_target_pairs={{0,1},{1,0},{2,3},{3,2},{4,5},{5,4},{6,7},{7,6},{8,9},{9,8},{10,11... | collective-permute-start | bytes 786440 | tf_op jit(solution)/shard_map/ppermute | solution.py:407
  119.2 49.9 %collective-permute-start.7 = (f32[4,64,1024]{2,1,0:T(8,128)}, f32[4,64,1024]{2,1,0:T(8,128)}, u32[]{:S(2)}, u32[]{:S(2)}) collective-permute-start(f32[4,64,1024]{2,1,0:T(8,128)} %slice_add_fusion), channel_id=1, source_target_pairs={{0,2},{1,3},{4,6},{5,7},{8,10},{9,11},{12,14},{13,15},{16,18},{17,... | collective-permute-start | bytes 3145736 | tf_op jit(solution)/shard_map/ppermute | solution.py:402
  140.6 3.4 copy-start.22
  140.6 5.5 copy-start.13
  141.3 30.3 %copy-start.9 = (f32[4,1,64,1024]{3,2,0,1:T(8,128)}, f32[4,1,64,1024]{3,2,0,1:T(8,128)S(1)}, u32[]{:S(2)}) copy-start(f32[4,1,64,1024]{3,2,0,1:T(8,128)S(1)} %maximum_add_fusion.5) | copy-start | bytes 3145732
  141.3 33.5 %collective-permute-start.14 = (f32[4,1,64,1024]{3,2,0,1:T(8,128)S(1)}, f32[4,1,64,1024]{3,2,0,1:T(8,128)S(1)}, u32[]{:S(2)}, u32[]{:S(2)}) collective-permute-start(f32[4,1,64,1024]{3,2,0,1:T(8,128)S(1)} %maximum_add_fusion.5), channel_id=1, source_target_pairs={{0,4},{4,0},{8,12},{12,8},{16,20},{20,16},{24,28},{28,24},{1,5},{5... | collective-permute-start | bytes 3145736 | tf_op jit(solution)/shard_map/ppermute | solution.py:385
  144.6 30.3 %collective-permute-start.15 = (f32[1,1,64,1536]{3,2,0,1:T(8,128)S(1)}, f32[1,1,64,1536]{3,2,0,1:T(8,128)S(1)}, u32[]{:S(2)}, u32[]{:S(2)}) collective-permute-start(f32[1,1,64,1536]{3,2,0,1:T(8,128)S(1)} %bitcast.45), channel_id=1, source_target_pairs={{0,8},{4,12},{8,0},{12,4},{16,24},{20,28},{24,16},{28,20},{1,9},{5... | collective-permute-start | bytes 1179656 | tf_op jit(solution)/shard_map/ppermute | solution.py:385
  146.1 28.7 %collective-permute-start.16 = (f32[1,64,1024]{2,1,0:T(8,128)}, f32[1,64,1024]{2,1,0:T(8,128)S(1)}, u32[]{:S(2)}, u32[]{:S(2)}) collective-permute-start(f32[1,64,1024]{2,1,0:T(8,128)} %get-tuple-element.89), channel_id=1, source_target_pairs={{0,1},{1,0},{2,3},{3,2},{4,5},{5,4},{6,7},{7,6},{8,9},{9,8},{10,11... | collective-permute-start | bytes 786440 | tf_op jit(solution)/shard_map/ppermute | solution.py:407
  171.6 26.0 %collective-permute-start.12 = (f32[4,64,1024]{2,1,0:T(8,128)S(1)}, f32[4,64,1024]{2,1,0:T(8,128)S(1)}, u32[]{:S(2)}, u32[]{:S(2)}) collective-permute-start(f32[4,64,1024]{2,1,0:T(8,128)S(1)} %select_add_fusion.6), channel_id=1, source_target_pairs={{0,1},{1,0},{2,3},{3,2},{4,5},{5,4},{6,7},{7,6},{8,9},{9,8},{10,11... | collective-permute-start | bytes 3145736 | tf_op jit(solution)/shard_map/ppermute | solution.py:407
  200.7 4.2 copy-start.19
  200.7 5.3 copy-start.7
  203.7 71.9 %collective-permute-start.17 = (f32[512,512]{1,0:T(8,128)S(1)}, f32[512,512]{1,0:T(8,128)S(1)}, u32[]{:S(2)}, u32[]{:S(2)}) collective-permute-start(f32[512,512]{1,0:T(8,128)S(1)} %get-tuple-element.88), channel_id=1, source_target_pairs={{0,2},{1,3},{4,6},{5,7},{8,10},{9,11},{12,14},{13,15},{16,18},{17,... | collective-permute-start | bytes 3145736 | tf_op jit(solution)/shard_map/ppermute | solution.py:402
  206.6 69.9 %collective-permute-start.18 = (f32[2,1,64,1536]{3,2,0,1:T(8,128)S(1)}, f32[2,1,64,1536]{3,2,0,1:T(8,128)S(1)}, u32[]{:S(2)}, u32[]{:S(2)}) collective-permute-start(f32[2,1,64,1536]{3,2,0,1:T(8,128)S(1)} %maximum_add_fusion.8), channel_id=1, source_target_pairs={{0,16},{4,20},{8,24},{12,28},{16,0},{20,4},{24,8},{28,12},{1,17},{... | collective-permute-start | bytes 2359304 | tf_op jit(solution)/shard_map/ppermute | solution.py:385
  207.4 69.0 %collective-permute-start.19 = (f32[1,1,64,2048]{3,2,1,0:T(8,128)S(1)}, f32[1,1,64,2048]{3,2,1,0:T(8,128)S(1)}, u32[]{:S(2)}, u32[]{:S(2)}) collective-permute-start(f32[1,1,64,2048]{3,2,1,0:T(8,128)S(1)} %bitcast.43), channel_id=1, source_target_pairs={{0,8},{4,12},{8,0},{12,4},{16,24},{20,28},{24,16},{28,20},{1,9},{5... | collective-permute-start | bytes 1572872 | tf_op jit(solution)/shard_map/ppermute | solution.py:385
  209.6 88.6 %collective-permute-start.22 = (f32[512,512]{1,0:T(8,128)S(1)}, f32[512,512]{1,0:T(8,128)}, u32[]{:S(2)}, u32[]{:S(2)}) collective-permute-start(f32[512,512]{1,0:T(8,128)S(1)} %get-tuple-element.87), channel_id=1, source_target_pairs={{0,2},{1,3},{4,6},{5,7},{8,10},{9,11},{12,14},{13,15},{16,18},{17,... | collective-permute-start | bytes 3145736 | tf_op jit(solution)/shard_map/ppermute | solution.py:402
  276.3 44.3 %copy-start.2 = (f32[512,512]{1,0:T(8,128)}, f32[512,512]{1,0:T(8,128)S(1)}, u32[]{:S(2)}) copy-start(f32[512,512]{1,0:T(8,128)S(1)} %select_add_fusion.5.refs_0_) | copy-start | bytes 3145732
  276.4 44.3 %collective-permute-start.21 = (f32[512,512]{1,0:T(8,128)S(1)}, f32[512,512]{1,0:T(8,128)}, u32[]{:S(2)}, u32[]{:S(2)}) collective-permute-start(f32[512,512]{1,0:T(8,128)S(1)} %select_add_fusion.5.refs_0_), channel_id=1, source_target_pairs={{0,1},{1,0},{2,3},{3,2},{4,5},{5,4},{6,7},{7,6},{8,9},{9,8},{10,11... | collective-permute-start | bytes 3145736 | tf_op jit(solution)/shard_map/ppermute | solution.py:407
  277.5 16.9 %copy-start.3 = (f32[2,1,64,1536]{3,2,0,1:T(8,128)S(1)}, f32[2,1,64,1536]{3,2,0,1:T(8,128)}, u32[]{:S(2)}) copy-start(f32[2,1,64,1536]{3,2,0,1:T(8,128)} %fusion.1) | copy-start | bytes 2359300
  297.4 5.6 copy-start.5
  297.4 48.6 %collective-permute-start.20 = (f32[4,1,64,1536]{3,2,0,1:T(8,128)}, f32[4,1,64,1536]{3,2,0,1:T(8,128)}, u32[]{:S(2)}, u32[]{:S(2)}) collective-permute-start(f32[4,1,64,1536]{3,2,0,1:T(8,128)} %maximum_add_fusion.4), channel_id=1, source_target_pairs={{0,4},{4,0},{8,12},{12,8},{16,20},{20,16},{24,28},{28,24},{1,5},{5... | collective-permute-start | bytes 4718600 | tf_op jit(solution)/shard_map/ppermute | solution.py:385
  301.2 41.8 %collective-permute-start.25 = (f32[512,512]{1,0:T(8,128)}, f32[512,512]{1,0:T(8,128)}, u32[]{:S(2)}, u32[]{:S(2)}) collective-permute-start(f32[512,512]{1,0:T(8,128)} %select_add_fusion.4.refs_2_), channel_id=1, source_target_pairs={{0,1},{1,0},{2,3},{3,2},{4,5},{5,4},{6,7},{7,6},{8,9},{9,8},{10,11... | collective-permute-start | bytes 3145736 | tf_op jit(solution)/shard_map/ppermute | solution.py:407
  304.6 41.3 %collective-permute-start.23 = (f32[2,1,64,2048]{3,2,1,0:T(8,128)}, f32[2,1,64,2048]{3,2,1,0:T(8,128)}, u32[]{:S(2)}, u32[]{:S(2)}) collective-permute-start(f32[2,1,64,2048]{3,2,1,0:T(8,128)} %maximum_add_fusion.6), channel_id=1, source_target_pairs={{0,16},{4,20},{8,24},{12,28},{16,0},{20,4},{24,8},{28,12},{1,17},{... | collective-permute-start | bytes 3145736 | tf_op jit(solution)/shard_map/ppermute | solution.py:385
  322.9 48.3 %collective-permute-start.24 = (f32[512,1024]{1,0:T(8,128)S(1)}, f32[512,1024]{1,0:T(8,128)}, u32[]{:S(2)}, u32[]{:S(2)}) collective-permute-start(f32[512,1024]{1,0:T(8,128)S(1)} %maximum_add_fusion.1), channel_id=1, source_target_pairs={{0,8},{4,12},{8,0},{12,4},{16,24},{20,28},{24,16},{28,20},{1,9},{5... | collective-permute-start | bytes 6291464 | tf_op jit(solution)/shard_map/ppermute | solution.py:385
  373.6 47.0 %collective-permute-start.27 = (f32[512,1024]{1,0:T(8,128)}, f32[512,1024]{1,0:T(8,128)}, u32[]{:S(2)}, u32[]{:S(2)}) collective-permute-start(f32[512,1024]{1,0:T(8,128)} %select_add_fusion.3), channel_id=1, source_target_pairs={{0,16},{4,20},{8,24},{12,28},{16,0},{20,4},{24,8},{28,12},{1,17},{... | collective-permute-start | bytes 6291464 | tf_op jit(solution)/shard_map/ppermute | solution.py:385
  377.0 50.0 %collective-permute-start.26 = (f32[4,1,64,2048]{3,2,1,0:T(8,128)}, f32[4,1,64,2048]{3,2,1,0:T(8,128)}, u32[]{:S(2)}, u32[]{:S(2)}) collective-permute-start(f32[4,1,64,2048]{3,2,1,0:T(8,128)} %maximum_add_fusion.2.refs_1_), channel_id=1, source_target_pairs={{0,4},{4,0},{8,12},{12,8},{16,20},{20,16},{24,28},{28,24},{1,5},{5... | collective-permute-start | bytes 6291464 | tf_op jit(solution)/shard_map/ppermute | solution.py:385
  400.8 23.9 %copy-start = (f32[512,1024]{1,0:T(8,128)}, f32[512,1024]{1,0:T(8,128)S(1)}, u32[]{:S(2)}) copy-start(f32[512,1024]{1,0:T(8,128)S(1)} %maximum_add_fusion.3) | copy-start | bytes 6291460
  400.8 64.8 %collective-permute-start.29 = (f32[512,1024]{1,0:T(8,128)S(1)}, f32[512,1024]{1,0:T(8,128)}, u32[]{:S(2)}, u32[]{:S(2)}) collective-permute-start(f32[512,1024]{1,0:T(8,128)S(1)} %maximum_add_fusion.3), channel_id=1, source_target_pairs={{0,16},{4,20},{8,24},{12,28},{16,0},{20,4},{24,8},{28,12},{1,17},{... | collective-permute-start | bytes 6291464 | tf_op jit(solution)/shard_map/ppermute | solution.py:385
  424.7 48.3 %collective-permute-start.28 = (f32[512,1024]{1,0:T(8,128)}, f32[512,1024]{1,0:T(8,128)}, u32[]{:S(2)}, u32[]{:S(2)}) collective-permute-start(f32[512,1024]{1,0:T(8,128)} %select_add_fusion.2.refs_0_), channel_id=1, source_target_pairs={{0,4},{4,0},{8,12},{12,8},{16,20},{20,16},{24,28},{28,24},{1,5},{5... | collective-permute-start | bytes 6291464 | tf_op jit(solution)/shard_map/ppermute | solution.py:385
  468.2 47.0 %collective-permute-start.30 = (f32[512,1024]{1,0:T(8,128)S(1)}, f32[512,1024]{1,0:T(8,128)}, u32[]{:S(2)}, u32[]{:S(2)}) collective-permute-start(f32[512,1024]{1,0:T(8,128)S(1)} %select_add_fusion.1), channel_id=1, source_target_pairs={{0,8},{4,12},{8,0},{12,4},{16,24},{20,28},{24,16},{28,20},{1,9},{5... | collective-permute-start | bytes 6291464 | tf_op jit(solution)/shard_map/ppermute | solution.py:385
  517.4 26.8 %collective-permute-start.31 = (f32[512,1024]{1,0:T(8,128)}, f32[512,1024]{1,0:T(8,128)S(1)}, u32[]{:S(2)}, u32[]{:S(2)}) collective-permute-start(f32[512,1024]{1,0:T(8,128)} %select_add_fusion.refs_2_), channel_id=1, source_target_pairs={{0,4},{4,0},{8,12},{12,8},{16,20},{20,16},{24,28},{28,24},{1,5},{5... | collective-permute-start | bytes 6291464 | tf_op jit(solution)/shard_map/ppermute | solution.py:385
  (13 other events, 17.4 us)
Sparse Core Ops, SparseCore 0:
  200.8 104.0 all-gather.1

commit v4 on v3

--- a/solution.py
+++ b/solution.py
@@ -497,9 +497,10 @@
 
 CHUNKS = 2
 PARTS = 2
-LEAD_WINDOWS = ([1, 2, 3, 4, 5], [2, 3, 5, 6, 7], [4, 5, 6, 7, 9], [5, 6, 7, 8, 10])
-SIDE_WINDOWS = [6, 7, 8]
-BELOW_WINDOWS = ([7, 8, 9, 10, 11], [8, 9, 11, 12, 13])
+LEAD_WINDOWS = ([1, 2, 3, 4, 5], [1, 2, 4, 5, 6], [6, 7, 8], [8, 9, 10])
+PAIR_WINDOWS = [3, 5]
+SIDE_WINDOWS = [7, 8, 10]
+BELOW_WINDOWS = ([9, 10, 11, 13, 15], [10, 11, 12, 14, 15])
 
 
 def shards(tile_count, col_count, front_diag, front_below, ancestor, owner_cols, rel):
@@ -530,8 +531,17 @@
         front_diag.reshape(tile_count, rows // tile_count, width), "tiles", 0, 0, tiled=True
     )
 
+    lead_pair = {0: []}
+
+    def pair_stream():
+        yield from climb(pieces[2:steps], col_pos, col_count, plan.tie, lead_pair[0])
+
     def lead_stream(i):
         size = (i + 1) * rows
+        if i >= 2:
+            plan.advance("pair", lead_pair, 0)
+            piece = jnp.concatenate(by_panel(lead_pair[0], col_pos), 2)[i - 2 : i - 1, :, :size]
+            return (yield from gather_rows(piece, bits, tile_pos, tile_count, plan.tie))
         take = pieces[i : i + 1, :, : min(size, width)]
         pair = yield from climb(take, col_pos, col_count, plan.tie)
         panels = by_panel(pair, col_pos)
@@ -547,13 +557,14 @@
             held = jnp.swapaxes(held, 0, 1).reshape(1, tile_count - steps, rows, lead)
         return held
 
+    plan.add("pair", pair_stream(), PAIR_WINDOWS)
     for i, windows in enumerate(LEAD_WINDOWS):
         plan.add(("lead", i), lead_stream(i), windows)
     plan.add("side", side_stream(), SIDE_WINDOWS)
     flying = []
     for window in range(1, 4):
         flying += plan.run(window)
-    started = plan.run(4)
+    plan.run(4)
 
     factor_rows, inverse_rows = [], []
     window = 5
@@ -563,11 +574,11 @@
         held = plan.finish(("lead", i))
         state = None
         for first, last in zip(cuts[:-1], cuts[1:]):
-            begun = plan.run(window)
+            plan.run(window)
             state = tile_part(
                 i, first, last, rows, bits, info, held, state and state[:3], inverse_rows, flying
             )
-            flying, started = started + begun, []
+            flying = []
             plan.token = state[5]
             window += 1
         window = 5 + PARTS * (i + 1)
@@ -575,7 +586,7 @@
         inverse_rows.append(tuple(state[3:5]))
     for k in range(CHUNKS):
         plan.advance(("below", k), own_parts, k)
-    begun = plan.run(window)
+    plan.run(window)
     pairs = [part for pair in inverse_rows for part in pair]
     solves = [
         jax.ShapeDtypeStruct((rows, width), jnp.float32),

time: 631 us -> 620 us (0.983)
  waiting for transfers between devices: 217 us -> 208 us
    ppermute x7 -> x6, waiting for transfers between devices: 118 us -> 89.3 us  [climb(): other = lax.ppermute(held, 'cols', pairs)]
    ppermute x18, waiting for transfers between devices: 48.3 us -> 70 us  [exchange(): lax.ppermute(block, 'tiles', [(i, i ^ bit) for i in range(tile_count)])]
    add x21 -> x19, other arithmetic: 41.1 us -> 43.8 us  [tie(): return value if self.token is None else value + self.token[0, 0]]
    ppermute x7 -> x6, waiting for transfers between devices: 50.8 us -> 48.2 us  [climb(): lax.ppermute(held, 'cols', [(at, at ^ 1) for at in range(col_count)])]
  transfers between devices with their start and end apart: 33 -> 31, of which waited for: 17 -> 16; matrix products, arithmetic and copies ran while one was open for 9% -> 10% of each run, Pallas kernels for 34% -> 37%
where the time goes in v4:
time: 620 us; the launch traced here: 609 us
  Pallas kernels  268 us (43%)
  waiting for transfers between devices  208 us (34%)
  other arithmetic  59.5 us (10%)
  blocking collectives  28.4 us (5%)
  starting transfers between devices  26.3 us (4%)
  between operations  16.1 us (3%)
    pallas_call x8, Pallas kernels, tile_part(): pl.pallas_call(functools.partial(tile_kernel, index, first, last, order,...  173 us
    ppermute x6, waiting for transfers between devices, climb(): other = lax.ppermute(held, 'cols', pairs)  89.3 us
    ppermute x18, waiting for transfers between devices, exchange(): lax.ppermute(block, 'tiles', [(i, i ^ bit) for i in range(tile_count)])  70 us
    ppermute x6, waiting for transfers between devices, climb(): lax.ppermute(held, 'cols', [(at, at ^ 1) for at in range(col_count)])  48.2 us
    add x19, other arithmetic, tie(): return value if self.token is None else value + self.token[0, 0]  43.8 us
    pallas_call x1, Pallas kernels, shards(): pl.pallas_call(functools.partial(change_kernel, steps), out_shape=[flat,...  29.3 us
    all_to_all x1, blocking collectives, shards(): lax.all_to_all(front_diag.reshape(tile_count, rows // tile_count, width),...  28.4 us
    pallas_call x1, Pallas kernels, shards(): pl.pallas_call(functools.partial(side_kernel, steps), out_shape=solves, i...  25.3 us
  transfers between devices with their start and end apart: 31, of which 16 were waited for; matrix products, arithmetic and copies ran while one was open for 10% of the time, Pallas kernels for 37%

profile of v4, /device:TPU:31, one launch (start us, length us, event | category | flops | bytes accessed | tf_op | source)
XLA Modules:
  0.0 609.0 jit_solution(5110991970250270993)
XLA Ops:
  7.2 28.4 %all_to_all.5 = f32[8,64,1024]{2,1,0:T(8,128)S(1)} all-to-all(f32[8,64,1024]{2,1,0:T(8,128)} %bitcast.42), channel_id=1, replica_groups=mesh['tiles'=8,'cols'=4] {'tiles'}, dimensions={0} | all-to-all | bytes 4194304 | tf_op jit(solution)/shard_map/all_to_all | solution.py:530
  36.9 9.6 %collective-permute-done.refs_3_ = f32[1,64,512]{2,1,0:T(8,128)S(1)} collective-permute-done((f32[1,64,512]{2,1,0:T(8,128)S(1)}, f32[1,64,512]{2,1,0:T(8,128)S(1)}, u32[]{:S(2)}, u32[]{:S(2)}) %collective-permute-start) | collective-permute-done | bytes 131104 | tf_op jit(solution)/shard_map/ppermute | solution.py:402
  49.3 1.9 collective-permute-done.1.refs_5_
  52.0 21.7 %collective-permute-done.5.refs_4_ = f32[1,64,1024]{2,1,0:T(8,128)S(1)} collective-permute-done((f32[1,64,1024]{2,1,0:T(8,128)S(1)}, f32[1,64,1024]{2,1,0:T(8,128)S(1)}, u32[]{:S(2)}, u32[]{:S(2)}) %collective-permute-start.5) | collective-permute-done | bytes 262176 | tf_op jit(solution)/shard_map/ppermute | solution.py:402
  75.2 9.7 %collective-permute-done.7.refs_7_ = f32[2,64,1024]{2,1,0:T(8,128)S(1)} collective-permute-done((f32[2,64,1024]{2,1,0:T(8,128)S(1)}, f32[2,64,1024]{2,1,0:T(8,128)S(1)}, u32[]{:S(2)}, u32[]{:S(2)}) %collective-permute-start.7) | collective-permute-done | bytes 524320 | tf_op jit(solution)/shard_map/ppermute | solution.py:402
  85.2 6.2 %collective-permute-done.6.refs_6_ = f32[1,64,1024]{2,1,0:T(8,128)S(1)} collective-permute-done((f32[1,64,1024]{2,1,0:T(8,128)S(1)}, f32[1,64,1024]{2,1,0:T(8,128)S(1)}, u32[]{:S(2)}, u32[]{:S(2)}) %collective-permute-start.6) | collective-permute-done | bytes 262176 | tf_op jit(solution)/shard_map/ppermute | solution.py:407
  94.1 4.8 collective-permute-done.9
  101.1 1.6 collective-permute-done.13
  104.0 17.6 %shard_map.85 = (f32[512,512]{1,0:T(8,128)}, f32[512,512]{1,0:T(8,128)}, f32[512,512]{1,0:T(8,128)}, bf16[512,512]{1,0:T(8,128)(2,1)}, bf16[512,512]{1,0:T(8,128)(2,1)}, /*index=5*/f32[1,1]{1,0:T(1,128)}) custom-call(s32[2]{0:T(128)} %pad_add_fusion.refs_0_.info_ref, f32[4,1,64,512]{3,2,1,0:T(8,128)} %pad_maximum_fusion.1.refs_1_, ...), custom_call_target="tpu_custom_call" | custom-call | flops 16000000000 | bytes 1048576 | tf_op jit(solution)/shard_map/pallas_call | solution.py:230
  122.5 2.8 maximum_add_fusion.5.refs_1_
  126.1 14.9 %shard_map.86 = (f32[512,512]{1,0:T(8,128)}, f32[512,512]{1,0:T(8,128)}, f32[512,512]{1,0:T(8,128)}, bf16[512,512]{1,0:T(8,128)(2,1)}, bf16[512,512]{1,0:T(8,128)(2,1)}, /*index=5*/f32[1,1]{1,0:T(1,128)}) custom-call(f32[512,512]{1,0:T(8,128)} %get-tuple-element.45.refs_0_, f32[512,512]{1,0:T(8,128)} %get-tuple-element.46.refs_1_, ...), custom_call_target="tpu_custom_call" | custom-call | flops 16000000000 | bytes 1048576 | tf_op jit(solution)/shard_map/pallas_call | solution.py:230
  141.0 1.7 slice_add_fusion
  143.9 2.6 maximum_add_fusion.9
  147.6 2.6 fusion.1
  150.3 21.1 %shard_map.87 = (f32[512,1024]{1,0:T(8,128)}, f32[512,512]{1,0:T(8,128)}, f32[512,512]{1,0:T(8,128)}, bf16[512,1024]{1,0:T(8,128)(2,1)}, bf16[512,1024]{1,0:T(8,128)(2,1)}, /*index=5*/f32[1,1]{1,0:T(1,128)}) custom-call(s32[2]{0:T(128)} %pad_add_fusion.refs_0_.info_ref, f32[4,1,64,1024]{3,2,1,0:T(8,128)} %maximum_add_fusion.5.refs_1_, ...), custom_call_target="tpu_custom_call" | custom-call | flops 16000000000 | bytes 1048576 | tf_op jit(solution)/shard_map/pallas_call | solution.py:230
  171.4 20.8 %collective-permute-done.8 = f32[4,64,1024]{2,1,0:T(8,128)} collective-permute-done((f32[4,64,1024]{2,1,0:T(8,128)}, f32[4,64,1024]{2,1,0:T(8,128)}, u32[]{:S(2)}, u32[]{:S(2)}) %collective-permute-start.8) | collective-permute-done | bytes 1048608 | tf_op jit(solution)/shard_map/ppermute | solution.py:402
  192.2 3.6 select_add_fusion.6
  195.8 3.0 maximum_add_fusion.4
  199.2 16.8 %shard_map.88 = (f32[512,1024]{1,0:T(8,128)}, f32[512,512]{1,0:T(8,128)}, f32[512,512]{1,0:T(8,128)}, bf16[512,1024]{1,0:T(8,128)(2,1)}, bf16[512,1024]{1,0:T(8,128)(2,1)}, /*index=5*/f32[1,1]{1,0:T(1,128)}) custom-call(f32[512,1024]{1,0:T(8,128)} %get-tuple-element.53.refs_0_, f32[512,512]{1,0:T(8,128)} %get-tuple-element.54.refs_1_, ...), custom_call_target="tpu_custom_call" | custom-call | flops 16000000000 | bytes 1048576 | tf_op jit(solution)/shard_map/pallas_call | solution.py:230
  216.0 4.3 collective-permute-done.12
  220.4 1.8 select_bitcast_fusion.1
  222.2 25.2 %shard_map.89 = (f32[512,1536]{1,0:T(8,128)}, f32[512,512]{1,0:T(8,128)}, f32[512,512]{1,0:T(8,128)}, bf16[512,1536]{1,0:T(8,128)(2,1)}, bf16[512,1536]{1,0:T(8,128)(2,1)}, /*index=5*/f32[1,1]{1,0:T(1,128)}) custom-call(s32[2]{0:T(128)} %pad_add_fusion.refs_0_.info_ref, f32[4,1,64,1536]{3,2,1,0:T(8,128)} %bitcast.13.refs_1_, ...), custom_call_target="tpu_custom_call" | custom-call | flops 16000000000 | bytes 1048576 | tf_op jit(solution)/shard_map/pallas_call | solution.py:230
  247.5 2.2 maximum_add_fusion
  251.8 10.9 %collective-permute-done.17 = f32[1,1,64,2048]{3,2,1,0:T(8,128)S(1)} collective-permute-done((f32[1,1,64,2048]{3,2,1,0:T(8,128)S(1)}, f32[1,1,64,2048]{3,2,1,0:T(8,128)S(1)}, u32[]{:S(2)}, u32[]{:S(2)}) %collective-permute-start.17) | collective-permute-done | bytes 524320 | tf_op jit(solution)/shard_map/ppermute | solution.py:385
  263.5 2.1 collective-permute-start.18
  269.2 36.9 %collective-permute-done.18 = f32[2,1,64,2048]{3,2,1,0:T(8,128)S(1)} collective-permute-done((f32[2,1,64,2048]{3,2,1,0:T(8,128)S(1)}, f32[2,1,64,2048]{3,2,1,0:T(8,128)S(1)}, u32[]{:S(2)}, u32[]{:S(2)}) %collective-permute-start.18) | collective-permute-done | bytes 1048608 | tf_op jit(solution)/shard_map/ppermute | solution.py:385
  306.1 2.1 maximum_add_fusion.1.refs_1_
  308.2 2.4 collective-permute-start.19
  310.6 1.7 collective-permute-start.22
  312.2 26.9 %collective-permute-done.20 = f32[512,512]{1,0:T(8,128)S(1)} collective-permute-done((f32[512,512]{1,0:T(8,128)S(1)}, f32[512,512]{1,0:T(8,128)S(1)}, u32[]{:S(2)}, u32[]{:S(2)}) %collective-permute-start.20) | collective-permute-done | bytes 1048608 | tf_op jit(solution)/shard_map/ppermute | solution.py:402
  340.1 21.1 %shard_map.90 = (f32[512,1536]{1,0:T(8,128)}, f32[512,512]{1,0:T(8,128)}, f32[512,512]{1,0:T(8,128)}, bf16[512,1536]{1,0:T(8,128)(2,1)}, bf16[512,1536]{1,0:T(8,128)(2,1)}, /*index=5*/f32[1,1]{1,0:T(1,128)}) custom-call(f32[512,1536]{1,0:T(8,128)} %get-tuple-element.61.refs_0_, f32[512,512]{1,0:T(8,128)} %get-tuple-element.62.refs_1_, ...), custom_call_target="tpu_custom_call" | custom-call | flops 16000000000 | bytes 1048576 | tf_op jit(solution)/shard_map/pallas_call | solution.py:230
  362.6 2.0 select_add_fusion.4.refs_2_
  369.3 15.8 %collective-permute-done.21.refs_1_ = f32[512,512]{1,0:T(8,128)} collective-permute-done((f32[512,512]{1,0:T(8,128)S(1)}, f32[512,512]{1,0:T(8,128)}, u32[]{:S(2)}, u32[]{:S(2)}) %collective-permute-start.21) | collective-permute-done | bytes 1048608 | tf_op jit(solution)/shard_map/ppermute | solution.py:407
  387.3 1.8 collective-permute-start.24
  389.1 18.4 %collective-permute-done.23.refs_3_ = f32[512,512]{1,0:T(8,128)} collective-permute-done((f32[512,512]{1,0:T(8,128)S(1)}, f32[512,512]{1,0:T(8,128)}, u32[]{:S(2)}, u32[]{:S(2)}) %collective-permute-start.23) | collective-permute-done | bytes 1048608 | tf_op jit(solution)/shard_map/ppermute | solution.py:407
  407.5 2.5 broadcast_select_fusion.1
  410.0 30.5 %shard_map.91 = (f32[512,2048]{1,0:T(8,128)}, f32[512,512]{1,0:T(8,128)}, f32[512,512]{1,0:T(8,128)}, bf16[512,2048]{1,0:T(8,128)(2,1)}, bf16[512,2048]{1,0:T(8,128)(2,1)}, /*index=5*/f32[1,1]{1,0:T(1,128)}) custom-call(s32[2]{0:T(128)} %pad_add_fusion.refs_0_.info_ref, f32[4,1,64,2048]{3,2,1,0:T(8,128)} %maximum_add_fusion.1.refs_1_, ...), custom_call_target="tpu_custom_call" | custom-call | flops 16000000000 | bytes 1048576 | tf_op jit(solution)/shard_map/pallas_call | solution.py:230
  440.5 3.4 maximum_add_fusion.3
  443.9 25.9 %shard_map.92 = (f32[512,2048]{1,0:T(8,128)}, f32[512,512]{1,0:T(8,128)}, f32[512,512]{1,0:T(8,128)}, bf16[512,2048]{1,0:T(8,128)(2,1)}, bf16[512,2048]{1,0:T(8,128)(2,1)}, /*index=5*/f32[1,1]{1,0:T(1,128)}) custom-call(f32[512,2048]{1,0:T(8,128)} %get-tuple-element.68.refs_0_, f32[512,512]{1,0:T(8,128)} %get-tuple-element.69.refs_1_, ...), custom_call_target="tpu_custom_call" | custom-call | flops 16000000000 | bytes 1048576 | tf_op jit(solution)/shard_map/pallas_call | solution.py:230
  469.8 24.2 %shard_map.93 = (f32[512,1024]{1,0:T(8,128)}, bf16[512,2048]{1,0:T(8,128)(2,1)}, bf16[512,2048]{1,0:T(8,128)(2,1)}, f32[1,1]{1,0:T(1,128)}) custom-call(s32[2]{0:T(128)} %pad_add_fusion.refs_0_.info_ref, f32[512,512]{1,0:T(8,128)} %copy-done, f32[512,512]{1,0:T(8,128)} %collective-permute-done.21.refs_1_, f32[512,512]{1,0:T(8,128)} %copy-done.1, ...), custom_call_target="tpu_custom_call" | custom-call | flops 20000000000 | bytes 1048576 | tf_op jit(solution)/shard_map/pallas_call | solution.py:598
  494.1 4.2 select_add_fusion.3
  499.8 2.7 select_add_fusion.1
  502.7 25.3 %shard_map.94 = (f32[512,1024]{1,0:T(8,128)}, bf16[512,2048]{1,0:T(8,128)(2,1)}, bf16[512,2048]{1,0:T(8,128)(2,1)}, f32[1,1]{1,0:T(1,128)}) custom-call(s32[2]{0:T(128)} %pad_add_fusion.refs_0_.info_ref, f32[8,4,64,2048]{3,2,1,0:T(8,128)} %all-gather.2.cloned.1.call-done.held_ref, bf16[512,512]{1,0:T(8,128)(2,1)} %get-tuple-element.50.refs_3_.refs_4_.refs_0_, ...), custom_call_target="tpu_custom_call" | custom-call | flops 20000000000 | bytes 1048576 | tf_op jit(solution)/shard_map/pallas_call | solution.py:611
  527.9 17.4 %collective-permute-done.25 = f32[512,1024]{1,0:T(8,128)} collective-permute-done((f32[512,1024]{1,0:T(8,128)}, f32[512,1024]{1,0:T(8,128)}, u32[]{:S(2)}, u32[]{:S(2)}) %collective-permute-start.25) | collective-permute-done | bytes 2097184 | tf_op jit(solution)/shard_map/ppermute | solution.py:385
  545.3 4.2 select_add_fusion.2.refs_0_
  550.9 4.0 select_add_fusion.refs_2_
  555.6 29.3 %shard_map.95 = (f32[512,1024]{1,0:T(8,128)}, f32[512,1024]{1,0:T(8,128)}, f32[1,1]{1,0:T(1,128)}) custom-call(s32[2]{0:T(128)} %pad_add_fusion.refs_0_.info_ref, f32[8,4,64,2048]{3,2,1,0:T(8,128)} %all-gather.2.cloned.1.call-done.held_ref, f32[512,512]{1,0:T(8,128)} %get-tuple-element.59.refs_0_, f32[512,1024]{1,0:T(8,128)} %get-tuple-element.60.refs_1_, ...), custom_call_target="tpu_custom_call" | custom-call | flops 20000000000 | bytes 1048576 | tf_op jit(solution)/shard_map/pallas_call | solution.py:623
  586.3 15.7 %shard_map.96 = f32[512,1024]{1,0:T(8,128)} custom-call(s32[2]{0:T(128)} %pad_add_fusion.refs_0_.info_ref, s32[1,512]{1,0:T(1,128)} %bitcast.43, s32[2,512]{1,0:T(2,128)} %broadcast_subtract_fusion.col_ref, bf16[512,2048]{1,0:T(8,128)(2,1)} %get-tuple-element.76.refs_5_.high_ref, bf16[512,2048]{1,0:T(8,128)(2,1)} %get-tuple-element.77.refs_6_.low_ref, ...), custom_call_target="tpu_custom_call" | custom-call | flops 10000000000 | bytes 1048576 | tf_op jit(solution)/shard_map/pallas_call | solution.py:638
  (105 shorter events, 36.5 us)
Async XLA Ops:
  7.2 495.5 %all-gather.2.cloned.1.call-start = ((), (), s32[]{:S(2)}) async-start(), calls=%async_computation.1 | async-start | bytes 18874368 | tf_op jit(solution)/shard_map/all_gather | solution.py:554
  35.6 10.9 %collective-permute-start = (f32[1,64,512]{2,1,0:T(8,128)S(1)}, f32[1,64,512]{2,1,0:T(8,128)S(1)}, u32[]{:S(2)}, u32[]{:S(2)}) collective-permute-start(f32[1,64,512]{2,1,0:T(8,128)S(1)} %slice.33), channel_id=1, source_target_pairs={{0,2},{1,3},{4,6},{5,7},{8,10},{9,11},{12,14},{13,15},{16,18},{17,... | collective-permute-start | bytes 393224 | tf_op jit(solution)/shard_map/ppermute | solution.py:402
  46.5 1.4 copy-start.13
  46.6 4.6 collective-permute-start.1
  46.7 27.0 %collective-permute-start.5 = (f32[1,64,1024]{2,1,0:T(8,128)S(1)}, f32[1,64,1024]{2,1,0:T(8,128)S(1)}, u32[]{:S(2)}, u32[]{:S(2)}) collective-permute-start(f32[1,64,1024]{2,1,0:T(8,128)S(1)} %slice.34), channel_id=1, source_target_pairs={{0,2},{1,3},{4,6},{5,7},{8,10},{9,11},{12,14},{13,15},{16,18},{17,... | collective-permute-start | bytes 786440 | tf_op jit(solution)/shard_map/ppermute | solution.py:402
  48.0 36.9 %collective-permute-start.7 = (f32[2,64,1024]{2,1,0:T(8,128)S(1)}, f32[2,64,1024]{2,1,0:T(8,128)S(1)}, u32[]{:S(2)}, u32[]{:S(2)}) collective-permute-start(f32[2,64,1024]{2,1,0:T(8,128)S(1)} %slice.35), channel_id=1, source_target_pairs={{0,2},{1,3},{4,6},{5,7},{8,10},{9,11},{12,14},{13,15},{16,18},{17,... | collective-permute-start | bytes 1572872 | tf_op jit(solution)/shard_map/ppermute | solution.py:402
  51.2 0.7 copy-start.14
  51.9 21.9 %collective-permute-start.2 = (f32[1,1,64,512]{3,2,1,0:T(8,128)S(1)}, f32[1,1,64,512]{3,2,1,0:T(8,128)S(1)}, u32[]{:S(2)}, u32[]{:S(2)}) collective-permute-start(f32[1,1,64,512]{3,2,1,0:T(8,128)S(1)} %select_bitcast_fusion.3), channel_id=1, source_target_pairs={{0,8},{4,12},{8,0},{12,4},{16,24},{20,28},{24,16},{28,20},{1,9},{5... | collective-permute-start | bytes 393224 | tf_op jit(solution)/shard_map/ppermute | solution.py:385
  73.7 11.5 %copy-start.11 = (f32[1,64,1024]{2,1,0:T(8,128)}, f32[1,64,1024]{2,1,0:T(8,128)S(1)}, u32[]{:S(2)}) copy-start(f32[1,64,1024]{2,1,0:T(8,128)S(1)} %collective-permute-done.5.refs_4_) | copy-start | bytes 786436
  73.7 17.7 %collective-permute-start.6 = (f32[1,64,1024]{2,1,0:T(8,128)S(1)}, f32[1,64,1024]{2,1,0:T(8,128)S(1)}, u32[]{:S(2)}, u32[]{:S(2)}) collective-permute-start(f32[1,64,1024]{2,1,0:T(8,128)S(1)} %broadcast_select_fusion.7), channel_id=1, source_target_pairs={{0,1},{1,0},{2,3},{3,2},{4,5},{5,4},{6,7},{7,6},{8,9},{9,8},{10,11... | collective-permute-start | bytes 786440 | tf_op jit(solution)/shard_map/ppermute | solution.py:407
  73.8 25.9 %copy-start.10 = (f32[1,1,64,512]{3,2,1,0:T(8,128)}, f32[1,1,64,512]{3,2,1,0:T(8,128)S(1)}, u32[]{:S(2)}) copy-start(f32[1,1,64,512]{3,2,1,0:T(8,128)S(1)} %collective-permute-done.2.refs_8_) | copy-start | bytes 393220
  73.9 17.9 %collective-permute-start.3 = (f32[2,1,64,512]{3,2,1,0:T(8,128)S(1)}, f32[2,1,64,512]{3,2,1,0:T(8,128)S(1)}, u32[]{:S(2)}, u32[]{:S(2)}) collective-permute-start(f32[2,1,64,512]{3,2,1,0:T(8,128)S(1)} %pad_maximum_fusion.3), channel_id=1, source_target_pairs={{0,16},{4,20},{8,24},{12,28},{16,0},{20,4},{24,8},{28,12},{1,17},{... | collective-permute-start | bytes 786440 | tf_op jit(solution)/shard_map/ppermute | solution.py:385
  85.0 7.6 %copy-start.9 = (f32[2,64,1024]{2,1,0:T(8,128)}, f32[2,64,1024]{2,1,0:T(8,128)S(1)}, u32[]{:S(2)}) copy-start(f32[2,64,1024]{2,1,0:T(8,128)S(1)} %collective-permute-done.7.refs_7_) | copy-start | bytes 1572868
  85.1 16.0 %copy-start.6 = (f32[2,64,1024]{2,1,0:T(8,128)}, f32[2,64,1024]{2,1,0:T(8,128)S(1)}, u32[]{:S(2)}) copy-start(f32[2,64,1024]{2,1,0:T(8,128)S(1)} %broadcast_select_fusion.4) | copy-start | bytes 1572868
  85.1 17.7 %collective-permute-start.13 = (f32[2,64,1024]{2,1,0:T(8,128)S(1)}, f32[2,64,1024]{2,1,0:T(8,128)}, u32[]{:S(2)}, u32[]{:S(2)}) collective-permute-start(f32[2,64,1024]{2,1,0:T(8,128)S(1)} %broadcast_select_fusion.4), channel_id=1, source_target_pairs={{0,1},{1,0},{2,3},{3,2},{4,5},{5,4},{6,7},{7,6},{8,9},{9,8},{10,11... | collective-permute-start | bytes 1572872 | tf_op jit(solution)/shard_map/ppermute | solution.py:407
  91.4 1.2 copy-start.12
  91.4 7.4 %collective-permute-start.9 = (f32[1,1,64,1024]{3,2,1,0:T(8,128)S(1)}, f32[1,1,64,1024]{3,2,1,0:T(8,128)S(1)}, u32[]{:S(2)}, u32[]{:S(2)}) collective-permute-start(f32[1,1,64,1024]{3,2,1,0:T(8,128)S(1)} %select_bitcast_fusion.2), channel_id=1, source_target_pairs={{0,8},{4,12},{8,0},{12,4},{16,24},{20,28},{24,16},{28,20},{1,9},{5... | collective-permute-start | bytes 786440 | tf_op jit(solution)/shard_map/ppermute | solution.py:385
  92.6 11.4 %collective-permute-start.4 = (f32[4,1,64,512]{3,2,1,0:T(8,128)}, f32[4,1,64,512]{3,2,1,0:T(8,128)}, u32[]{:S(2)}, u32[]{:S(2)}) collective-permute-start(f32[4,1,64,512]{3,2,1,0:T(8,128)} %pad_maximum_fusion.1.refs_1_), channel_id=1, source_target_pairs={{0,4},{4,0},{8,12},{12,8},{16,20},{20,16},{24,28},{28,24},{1,5},{5... | collective-permute-start | bytes 1572872 | tf_op jit(solution)/shard_map/ppermute | solution.py:385
  98.9 2.2 copy-start.8
  99.8 22.7 %collective-permute-start.10 = (f32[2,1,64,1024]{3,2,1,0:T(8,128)}, f32[2,1,64,1024]{3,2,1,0:T(8,128)}, u32[]{:S(2)}, u32[]{:S(2)}) collective-permute-start(f32[2,1,64,1024]{3,2,1,0:T(8,128)} %pad_maximum_fusion.2), channel_id=1, source_target_pairs={{0,16},{4,20},{8,24},{12,28},{16,0},{20,4},{24,8},{28,12},{1,17},{... | collective-permute-start | bytes 1572872 | tf_op jit(solution)/shard_map/ppermute | solution.py:385
  122.2 21.7 %collective-permute-start.14 = (f32[1,1,64,1536]{3,2,0,1:T(8,128)S(1)}, f32[1,1,64,1536]{3,2,0,1:T(8,128)}, u32[]{:S(2)}, u32[]{:S(2)}) collective-permute-start(f32[1,1,64,1536]{3,2,0,1:T(8,128)S(1)} %bitcast.39), channel_id=1, source_target_pairs={{0,8},{4,12},{8,0},{12,4},{16,24},{20,28},{24,16},{28,20},{1,9},{5... | collective-permute-start | bytes 1179656 | tf_op jit(solution)/shard_map/ppermute | solution.py:385
  125.3 25.0 %collective-permute-start.11 = (f32[4,1,64,1024]{3,2,1,0:T(8,128)}, f32[4,1,64,1024]{3,2,1,0:T(8,128)}, u32[]{:S(2)}, u32[]{:S(2)}) collective-permute-start(f32[4,1,64,1024]{3,2,1,0:T(8,128)} %maximum_add_fusion.5.refs_1_), channel_id=1, source_target_pairs={{0,4},{4,0},{8,12},{12,8},{16,20},{20,16},{24,28},{28,24},{1,5},{5... | collective-permute-start | bytes 3145736 | tf_op jit(solution)/shard_map/ppermute | solution.py:385
  142.6 49.5 %collective-permute-start.8 = (f32[4,64,1024]{2,1,0:T(8,128)}, f32[4,64,1024]{2,1,0:T(8,128)}, u32[]{:S(2)}, u32[]{:S(2)}) collective-permute-start(f32[4,64,1024]{2,1,0:T(8,128)} %slice_add_fusion), channel_id=1, source_target_pairs={{0,2},{1,3},{4,6},{5,7},{8,10},{9,11},{12,14},{13,15},{16,18},{17,... | collective-permute-start | bytes 3145736 | tf_op jit(solution)/shard_map/ppermute | solution.py:402
  146.5 49.3 %collective-permute-start.15 = (f32[2,1,64,1536]{3,2,0,1:T(8,128)}, f32[2,1,64,1536]{3,2,0,1:T(8,128)}, u32[]{:S(2)}, u32[]{:S(2)}) collective-permute-start(f32[2,1,64,1536]{3,2,0,1:T(8,128)} %maximum_add_fusion.9), channel_id=1, source_target_pairs={{0,16},{4,20},{8,24},{12,28},{16,0},{20,4},{24,8},{28,12},{1,17},{... | collective-permute-start | bytes 2359304 | tf_op jit(solution)/shard_map/ppermute | solution.py:385
  171.4 24.4 %copy-start.4 = (f32[2,1,64,1536]{3,2,0,1:T(8,128)S(1)}, f32[2,1,64,1536]{3,2,0,1:T(8,128)}, u32[]{:S(2)}) copy-start(f32[2,1,64,1536]{3,2,0,1:T(8,128)} %fusion.1) | copy-start | bytes 2359300
  195.8 24.6 %collective-permute-start.12 = (f32[4,64,1024]{2,1,0:T(8,128)}, f32[4,64,1024]{2,1,0:T(8,128)}, u32[]{:S(2)}, u32[]{:S(2)}) collective-permute-start(f32[4,64,1024]{2,1,0:T(8,128)} %select_add_fusion.6), channel_id=1, source_target_pairs={{0,1},{1,0},{2,3},{3,2},{4,5},{5,4},{6,7},{7,6},{8,9},{9,8},{10,11... | collective-permute-start | bytes 3145736 | tf_op jit(solution)/shard_map/ppermute | solution.py:407
  198.8 23.4 %collective-permute-start.16 = (f32[4,1,64,1536]{3,2,0,1:T(8,128)}, f32[4,1,64,1536]{3,2,0,1:T(8,128)}, u32[]{:S(2)}, u32[]{:S(2)}) collective-permute-start(f32[4,1,64,1536]{3,2,0,1:T(8,128)} %maximum_add_fusion.4), channel_id=1, source_target_pairs={{0,4},{4,0},{8,12},{12,8},{16,20},{20,16},{24,28},{28,24},{1,5},{5... | collective-permute-start | bytes 4718600 | tf_op jit(solution)/shard_map/ppermute | solution.py:385
  249.7 15.9 %copy-start.5 = (f32[512,1024]{1,0:T(8,128)S(1)}, f32[512,1024]{1,0:T(8,128)}, u32[]{:S(2)}) copy-start(f32[512,1024]{1,0:T(8,128)} %refs_10_.1) | copy-start | bytes 6291460
  250.5 12.2 %collective-permute-start.17 = (f32[1,1,64,2048]{3,2,1,0:T(8,128)S(1)}, f32[1,1,64,2048]{3,2,1,0:T(8,128)S(1)}, u32[]{:S(2)}, u32[]{:S(2)}) collective-permute-start(f32[1,1,64,2048]{3,2,1,0:T(8,128)S(1)} %bitcast.37), channel_id=1, source_target_pairs={{0,8},{4,12},{8,0},{12,4},{16,24},{20,28},{24,16},{28,20},{1,9},{5... | collective-permute-start | bytes 1572872 | tf_op jit(solution)/shard_map/ppermute | solution.py:385
  263.5 42.6 %collective-permute-start.18 = (f32[2,1,64,2048]{3,2,1,0:T(8,128)S(1)}, f32[2,1,64,2048]{3,2,1,0:T(8,128)S(1)}, u32[]{:S(2)}, u32[]{:S(2)}) collective-permute-start(f32[2,1,64,2048]{3,2,1,0:T(8,128)S(1)} %maximum_add_fusion.7), channel_id=1, source_target_pairs={{0,16},{4,20},{8,24},{12,28},{16,0},{20,4},{24,8},{28,12},{1,17},{... | collective-permute-start | bytes 3145736 | tf_op jit(solution)/shard_map/ppermute | solution.py:385
  267.1 94.1 %copy-start.3 = (f32[512,512]{1,0:T(8,128)}, f32[512,512]{1,0:T(8,128)S(1)}, u32[]{:S(2)}) copy-start(f32[512,512]{1,0:T(8,128)S(1)} %get-tuple-element.91) | copy-start | bytes 3145732
  267.1 72.0 %collective-permute-start.20 = (f32[512,512]{1,0:T(8,128)S(1)}, f32[512,512]{1,0:T(8,128)S(1)}, u32[]{:S(2)}, u32[]{:S(2)}) collective-permute-start(f32[512,512]{1,0:T(8,128)S(1)} %get-tuple-element.92), channel_id=1, source_target_pairs={{0,2},{1,3},{4,6},{5,7},{8,10},{9,11},{12,14},{13,15},{16,18},{17,... | collective-permute-start | bytes 3145736 | tf_op jit(solution)/shard_map/ppermute | solution.py:402
  308.2 101.8 %collective-permute-start.19 = (f32[4,1,64,2048]{3,2,1,0:T(8,128)}, f32[4,1,64,2048]{3,2,1,0:T(8,128)}, u32[]{:S(2)}, u32[]{:S(2)}) collective-permute-start(f32[4,1,64,2048]{3,2,1,0:T(8,128)} %maximum_add_fusion.1.refs_1_), channel_id=1, source_target_pairs={{0,4},{4,0},{8,12},{12,8},{16,20},{20,16},{24,28},{28,24},{1,5},{5... | collective-permute-start | bytes 6291464 | tf_op jit(solution)/shard_map/ppermute | solution.py:385
  310.6 51.1 %collective-permute-start.22 = (f32[512,512]{1,0:T(8,128)S(1)}, f32[512,512]{1,0:T(8,128)S(1)}, u32[]{:S(2)}, u32[]{:S(2)}) collective-permute-start(f32[512,512]{1,0:T(8,128)S(1)} %get-tuple-element.91), channel_id=1, source_target_pairs={{0,2},{1,3},{4,6},{5,7},{8,10},{9,11},{12,14},{13,15},{16,18},{17,... | collective-permute-start | bytes 3145736 | tf_op jit(solution)/shard_map/ppermute | solution.py:402
  340.0 45.0 %copy-start = (f32[512,512]{1,0:T(8,128)}, f32[512,512]{1,0:T(8,128)S(1)}, u32[]{:S(2)}) copy-start(f32[512,512]{1,0:T(8,128)S(1)} %select_add_fusion.5.refs_0_) | copy-start | bytes 3145732
  340.0 45.0 %collective-permute-start.21 = (f32[512,512]{1,0:T(8,128)S(1)}, f32[512,512]{1,0:T(8,128)}, u32[]{:S(2)}, u32[]{:S(2)}) collective-permute-start(f32[512,512]{1,0:T(8,128)S(1)} %select_add_fusion.5.refs_0_), channel_id=1, source_target_pairs={{0,1},{1,0},{2,3},{3,2},{4,5},{5,4},{6,7},{7,6},{8,9},{9,8},{10,11... | collective-permute-start | bytes 3145736 | tf_op jit(solution)/shard_map/ppermute | solution.py:407
  361.2 4.1 copy-start.16
  361.7 1.0 copy-start.7
  364.7 21.8 %copy-start.1 = (f32[512,512]{1,0:T(8,128)}, f32[512,512]{1,0:T(8,128)S(1)}, u32[]{:S(2)}) copy-start(f32[512,512]{1,0:T(8,128)S(1)} %select_add_fusion.4.refs_2_) | copy-start | bytes 3145732
  364.7 42.8 %collective-permute-start.23 = (f32[512,512]{1,0:T(8,128)S(1)}, f32[512,512]{1,0:T(8,128)}, u32[]{:S(2)}, u32[]{:S(2)}) collective-permute-start(f32[512,512]{1,0:T(8,128)S(1)} %select_add_fusion.4.refs_2_), channel_id=1, source_target_pairs={{0,1},{1,0},{2,3},{3,2},{4,5},{5,4},{6,7},{7,6},{8,9},{9,8},{10,11... | collective-permute-start | bytes 3145736 | tf_op jit(solution)/shard_map/ppermute | solution.py:407
  386.5 21.0 %copy-start.2 = (f32[512,512]{1,0:T(8,128)S(1)}, f32[512,512]{1,0:T(8,128)}, u32[]{:S(2)}) copy-start(f32[512,512]{1,0:T(8,128)} %copy-done.1) | copy-start | bytes 3145732
  387.3 106.8 %collective-permute-start.24 = (f32[512,1024]{1,0:T(8,128)S(1)}, f32[512,1024]{1,0:T(8,128)}, u32[]{:S(2)}, u32[]{:S(2)}) collective-permute-start(f32[512,1024]{1,0:T(8,128)S(1)} %maximum_add_fusion.2), channel_id=1, source_target_pairs={{0,8},{4,12},{8,0},{12,4},{16,24},{20,28},{24,16},{28,20},{1,9},{5... | collective-permute-start | bytes 6291464 | tf_op jit(solution)/shard_map/ppermute | solution.py:385
  443.9 55.9 %collective-permute-start.27 = (f32[512,1024]{1,0:T(8,128)}, f32[512,1024]{1,0:T(8,128)}, u32[]{:S(2)}, u32[]{:S(2)}) collective-permute-start(f32[512,1024]{1,0:T(8,128)} %maximum_add_fusion.3), channel_id=1, source_target_pairs={{0,16},{4,20},{8,24},{12,28},{16,0},{20,4},{24,8},{28,12},{1,17},{... | collective-permute-start | bytes 6291464 | tf_op jit(solution)/shard_map/ppermute | solution.py:385
  498.3 47.0 %collective-permute-start.25 = (f32[512,1024]{1,0:T(8,128)}, f32[512,1024]{1,0:T(8,128)}, u32[]{:S(2)}, u32[]{:S(2)}) collective-permute-start(f32[512,1024]{1,0:T(8,128)} %select_add_fusion.3), channel_id=1, source_target_pairs={{0,16},{4,20},{8,24},{12,28},{16,0},{20,4},{24,8},{28,12},{1,17},{... | collective-permute-start | bytes 6291464 | tf_op jit(solution)/shard_map/ppermute | solution.py:385
  502.5 48.5 %collective-permute-start.28 = (f32[512,1024]{1,0:T(8,128)S(1)}, f32[512,1024]{1,0:T(8,128)}, u32[]{:S(2)}, u32[]{:S(2)}) collective-permute-start(f32[512,1024]{1,0:T(8,128)S(1)} %select_add_fusion.1), channel_id=1, source_target_pairs={{0,8},{4,12},{8,0},{12,4},{16,24},{20,28},{24,16},{28,20},{1,9},{5... | collective-permute-start | bytes 6291464 | tf_op jit(solution)/shard_map/ppermute | solution.py:385
  549.6 35.3 %collective-permute-start.26 = (f32[512,1024]{1,0:T(8,128)}, f32[512,1024]{1,0:T(8,128)}, u32[]{:S(2)}, u32[]{:S(2)}) collective-permute-start(f32[512,1024]{1,0:T(8,128)} %select_add_fusion.2.refs_0_), channel_id=1, source_target_pairs={{0,4},{4,0},{8,12},{12,8},{16,20},{20,16},{24,28},{28,24},{1,5},{5... | collective-permute-start | bytes 6291464 | tf_op jit(solution)/shard_map/ppermute | solution.py:385
  555.0 29.9 %collective-permute-start.29 = (f32[512,1024]{1,0:T(8,128)}, f32[512,1024]{1,0:T(8,128)S(1)}, u32[]{:S(2)}, u32[]{:S(2)}) collective-permute-start(f32[512,1024]{1,0:T(8,128)} %select_add_fusion.refs_2_), channel_id=1, source_target_pairs={{0,4},{4,0},{8,12},{12,8},{16,20},{20,16},{24,28},{28,24},{1,5},{5... | collective-permute-start | bytes 6291464 | tf_op jit(solution)/shard_map/ppermute | solution.py:385
  584.9 1.3 copy-start.15
Sparse Core Ops, SparseCore 0:
  249.8 110.1 all-gather.1
